TPU v7x, 32 devices: a whole 2x2x4 slice. The times are simulated.
32 devices in a mesh: dp: 8 (over z, x), heads: 2 (over y), feat: 2 (over core).
Axes of the slice: x: 2, y: 2, z: 4, core: 2. Of those that a mesh axis runs over, the one named last changes fastest.
Arguments:
- tokens: bfloat16 [4096, 1024], P(('dp', 'feat')), may hold values from -6 to 6
- qkv_weight: bfloat16 [1024, 3, 1024], P(('dp', 'feat'), None, 'heads'), may hold values from -0.1875 to 0.1875
- qkv_bias: bfloat16 [3, 16, 64], P(None, 'heads', ('dp', 'feat')), may hold values from -1.5 to 1.5
- out_weight: bfloat16 [1024, 1024], P('heads', ('dp', 'feat')), may hold values from -2 to 2
- norm_gains: bfloat16 [2, 1024], P(None, ('dp', 'feat')), may hold values from 0.099609375 to 1.8984375
- row_biases: bfloat16 [4, 1024], P(None, ('dp', 'feat')), may hold values from -2.5 to 2.5
- up_weight: bfloat16 [1024, 4096], P(('dp', 'feat'), 'heads'), may hold values from -0.1875 to 0.1875
- up_bias: bfloat16 [64, 64], P('heads', ('dp', 'feat')), may hold values from -2.5 to 2.5
- down_weight: bfloat16 [4096, 1024], P('heads', ('dp', 'feat')), may hold values from -0.09375 to 0.09375
- rpe_bias: bfloat16 [16, 1024], P('heads', ('dp', 'feat')), may hold values from -3 to 3
- omega: bfloat16 [16, 64, 64], P('heads', None, 'feat'), may hold values from -2.5 to 2.5
- bucket: int32 [8], P('dp'), may hold values from 0 to 2, as said below
- cotangent: bfloat16 [4096, 1024], P(('dp', 'feat')), may hold values from -6 to 6
Outputs:
- mixed: bfloat16 [4096, 1024], P(('dp', 'feat'))
- grad_tokens: float32 [4096, 1024], P(('dp', 'feat'))
- grad_qkv_weight: float32 [1024, 3, 1024], P(('dp', 'feat'), None, 'heads')
- grad_qkv_bias: float32 [3, 16, 64], P(None, 'heads', ('dp', 'feat'))
- grad_out_weight: float32 [1024, 1024], P('heads', ('dp', 'feat'))
- grad_norm_gains: float32 [2, 1024], P(None, ('dp', 'feat'))
- grad_row_biases: float32 [4, 1024], P(None, ('dp', 'feat'))
- grad_up_weight: float32 [1024, 4096], P(('dp', 'feat'), 'heads')
- grad_up_bias: float32 [64, 64], P('heads', ('dp', 'feat'))
- grad_down_weight: float32 [4096, 1024], P('heads', ('dp', 'feat'))
- grad_rpe_bias: float32 [16, 1024], P('heads', ('dp', 'feat'))
Inputs may be any that keep to these rules, and one draw needn't show every extreme that they name: Every one of 0, 1, 2 occurs; group g holds sequences of 128 * 2**bucket[g] tokens each, end to end.
All inputs are finite; a program needn't handle non-finite values.
Results may differ from a plain program's by a relative error of at most 0.03.
Values may be sent and summed in bfloat16 or wider, within the bound.
A program may use at most 128 MiB of HBM per device.

v0:
```python
import jax
import jax.numpy as jnp
from jax import lax
from jax.sharding import PartitionSpec as P

HEAD = 64
M = 64


EPSILON = 1e-12
UNIT_EPS = 1e-06


def toeplitz_block(window, extent):
    leading = window.shape[0]
    tiled_rows = jnp.broadcast_to(window[:, None, :], (leading, extent, 2 * extent - 1)).reshape(
        leading, -1
    )
    padded = jnp.pad(tiled_rows, ((0, 0), (0, extent)))
    sheared = padded.reshape(leading, extent, 2 * extent)[:, :, :extent]
    return sheared[:, :, ::-1]


def diagonal_sums(values_grid, extent):
    leading = values_grid.shape[0]
    flipped = values_grid[:, :, ::-1]
    padded = jnp.pad(flipped, ((0, 0), (0, 0), (0, extent))).reshape(leading, -1)
    sheared = padded[:, : extent * (2 * extent - 1)].reshape(leading, extent, 2 * extent - 1)
    return jnp.sum(sheared, axis=1)


def norm_forward(values, gain, shift):
    centred = values - jnp.mean(values, axis=-1, keepdims=True)
    inverse = lax.rsqrt(jnp.mean(centred * centred, axis=-1, keepdims=True) + EPSILON)
    normed = centred * inverse
    return (normed * gain + shift, normed, inverse)


def norm_backward(upstream, normed, inverse, gain):
    scaled_grad = upstream * gain
    return inverse * (
        scaled_grad
        - jnp.mean(scaled_grad, axis=-1, keepdims=True)
        - normed * jnp.mean(scaled_grad * normed, axis=-1, keepdims=True)
    )


def feature_logits(entries, omega_local):
    factor = HEAD ** (-0.25)
    wide = entries.astype(jnp.float32)
    inverse = lax.rsqrt(jnp.mean(wide * wide, axis=-1, keepdims=True) + UNIT_EPS)
    unit = wide * inverse
    projected = jnp.einsum(
        "rhe,hem->hmr",
        unit,
        omega_local.astype(jnp.float32),
        precision=lax.Precision.HIGHEST,
        preferred_element_type=jnp.float32,
    )
    squares = jnp.sum(unit * unit, axis=-1)
    return (factor * projected - 0.5 * factor * factor * squares.T[:, None, :], unit, inverse)


def feature_back(grad_phi, logits, unit, inverse, omega_local):
    factor = HEAD ** (-0.25)
    grad_logits = (grad_phi * (jnp.exp(logits) * M ** (-0.5))).astype(jnp.bfloat16)
    projected = jnp.einsum(
        "hmr,hem->rhe", grad_logits, omega_local, preferred_element_type=jnp.float32
    )
    totals = jnp.sum(grad_logits.astype(jnp.float32), axis=1)
    grad_unit = factor * projected - factor * factor * totals.T[:, :, None] * unit
    return inverse * (grad_unit - unit * jnp.mean(grad_unit * unit, axis=-1, keepdims=True))


def window_begin(row_start, col_start, extent, rows_total):
    return row_start - col_start + rows_total - extent + 1


def block_coeff(rpe_exp, window_start, extent):
    window = lax.dynamic_slice_in_dim(rpe_exp, window_start, 2 * extent - 1, 1)
    return toeplitz_block(window, extent)


def local(
    tokens,
    qkv_weight,
    qkv_bias,
    out_weight,
    norm_gains,
    row_biases,
    up_weight,
    up_bias,
    down_weight,
    rpe_bias,
    omega,
    bucket,
    cotangent,
):
    qkv_full, out_full, up_full, down_full, gains_all, biases_all, bias_qkv, bias_up, rpe_all = (
        lax.all_gather(qkv_weight, ("dp", "feat"), axis=0, tiled=True),
        lax.all_gather(out_weight, ("dp", "feat"), axis=1, tiled=True),
        lax.all_gather(up_weight, ("dp", "feat"), axis=0, tiled=True),
        lax.all_gather(down_weight, ("dp", "feat"), axis=1, tiled=True),
        lax.all_gather(norm_gains, ("dp", "feat"), axis=1, tiled=True),
        lax.all_gather(row_biases, ("dp", "feat"), axis=1, tiled=True),
        lax.all_gather(qkv_bias, ("dp", "feat"), axis=2, tiled=True),
        lax.all_gather(up_bias, ("dp", "feat"), axis=1, tiled=True),
        lax.all_gather(rpe_bias, ("dp", "feat"), axis=1, tiled=True),
    )
    model_width = qkv_full.shape[0]
    head_cols = qkv_full.shape[2]
    local_heads = omega.shape[0]
    local_feats = omega.shape[2]
    rows_own = tokens.shape[0]
    rows_total = rows_own * lax.axis_size("feat")
    block_rows = min(512, rows_total // 4)
    blocks = rows_total // block_rows
    seq_length = rows_total // 4 * jnp.where(bucket[0] == 0, 1, jnp.where(bucket[0] == 1, 2, 4))
    block_count = seq_length // block_rows
    gain_rows = gains_all.astype(jnp.float32)
    bias_rows = biases_all.astype(jnp.float32)
    rpe_exp = jnp.exp(rpe_all.astype(jnp.float32))
    projected = jnp.dot(
        tokens, qkv_full.reshape(model_width, 3 * head_cols), preferred_element_type=jnp.float32
    )
    projected = projected + bias_qkv.reshape(-1).astype(jnp.float32)
    qkv_own = projected.astype(jnp.bfloat16)
    qkv_all = lax.all_gather(qkv_own, "feat", axis=0, tiled=True).reshape(
        rows_total, 3, local_heads, HEAD
    )
    queries = qkv_all[:, 0]
    keys_rows = qkv_all[:, 1]
    values_rows = qkv_all[:, 2]
    logits_query, unit_query, inverse_query = feature_logits(queries, omega)
    logits_key, unit_key, inverse_key = feature_logits(keys_rows, omega)
    feat_query = (jnp.exp(logits_query) * M ** (-0.5)).astype(jnp.bfloat16)
    feat_key = (jnp.exp(logits_key) * M ** (-0.5)).astype(jnp.bfloat16)
    numer_parts = []
    denom_parts = []
    for row_block in range(blocks):
        row_start = row_block * block_rows
        first_block = row_start // seq_length * block_count
        phi_rows = feat_query[:, :, row_start : row_start + block_rows]

        def visit(column_block, carried, phi_rows=phi_rows, row_start=row_start):
            numer_acc, denom_acc = carried
            col_start = column_block * block_rows
            phi_cols = lax.dynamic_slice_in_dim(feat_key, col_start, block_rows, 2)
            value_cols = lax.dynamic_slice_in_dim(values_rows, col_start, block_rows, 0)
            coefficient = block_coeff(
                rpe_exp, window_begin(row_start, col_start, block_rows, rows_total), block_rows
            )
            scores = jnp.einsum(
                "hmi,hmj->hij", phi_rows, phi_cols, preferred_element_type=jnp.float32
            )
            weights = (coefficient * scores).astype(jnp.bfloat16)
            numer_acc = numer_acc + jnp.einsum(
                "hij,jhe->ihe", weights, value_cols, preferred_element_type=jnp.float32
            )
            denom_acc = denom_acc + jnp.sum(weights.astype(jnp.float32), axis=-1)
            return (numer_acc, denom_acc)

        start_pair = (
            jnp.zeros((block_rows, local_heads, HEAD), jnp.float32),
            jnp.zeros((local_heads, block_rows), jnp.float32),
        )
        numer_block, denom_block = lax.fori_loop(
            first_block, first_block + block_count, visit, start_pair
        )
        numer_parts.append(numer_block)
        denom_parts.append(denom_block)
    numer_all = jnp.concatenate(numer_parts, axis=0).reshape(rows_total, head_cols)
    denom_all = jnp.concatenate(denom_parts, axis=1)
    numer_own, denom_own = (
        lax.psum_scatter(
            numer_all.astype(jnp.bfloat16), "feat", scatter_dimension=0, tiled=True
        ).astype(jnp.float32),
        lax.psum_scatter(
            denom_all.astype(jnp.bfloat16), "feat", scatter_dimension=1, tiled=True
        ).astype(jnp.float32),
    )
    denom_rows = denom_own.T
    quotient = numer_own.reshape(rows_own, local_heads, HEAD) / denom_rows[:, :, None]
    attn_low = quotient.reshape(rows_own, head_cols).astype(jnp.bfloat16)
    z_part = jnp.dot(attn_low, out_full, preferred_element_type=jnp.float32)
    mixed_z = lax.psum(z_part.astype(jnp.bfloat16), "heads").astype(jnp.float32) + bias_rows[0]
    first_out, normed_one, inverse_one = norm_forward(
        tokens.astype(jnp.float32) + mixed_z, gain_rows[0], bias_rows[1]
    )
    first_low = first_out.astype(jnp.bfloat16)
    pre_act = jnp.dot(first_low, up_full, preferred_element_type=jnp.float32) + bias_up.reshape(
        -1
    ).astype(jnp.float32)
    act_value, act_pull = jax.vjp(lambda inner: jax.nn.gelu(inner, approximate=False), pre_act)
    act_low = act_value.astype(jnp.bfloat16)
    ffn_part = jnp.dot(act_low, down_full, preferred_element_type=jnp.float32)
    ffn_out = lax.psum(ffn_part.astype(jnp.bfloat16), "heads").astype(jnp.float32) + bias_rows[2]
    final_rows, normed_two, inverse_two = norm_forward(
        first_out + ffn_out, gain_rows[1], bias_rows[3]
    )
    mixed = final_rows.astype(jnp.bfloat16)
    qkv_full, out_full, up_full, down_full, gains_all, rpe_all = (
        lax.all_gather(qkv_weight, ("dp", "feat"), axis=0, tiled=True),
        lax.all_gather(out_weight, ("dp", "feat"), axis=1, tiled=True),
        lax.all_gather(up_weight, ("dp", "feat"), axis=0, tiled=True),
        lax.all_gather(down_weight, ("dp", "feat"), axis=1, tiled=True),
        lax.all_gather(norm_gains, ("dp", "feat"), axis=1, tiled=True),
        lax.all_gather(rpe_bias, ("dp", "feat"), axis=1, tiled=True),
    )
    gain_rows = gains_all.astype(jnp.float32)
    rpe_exp = jnp.exp(rpe_all.astype(jnp.float32))
    upstream = cotangent.astype(jnp.float32)
    grad_gain_two = jnp.sum(upstream * normed_two, axis=0)
    grad_shift_two = jnp.sum(upstream, axis=0)
    resid_two = norm_backward(upstream, normed_two, inverse_two, gain_rows[1])
    resid_low = resid_two.astype(jnp.bfloat16)
    grad_bias_down = jnp.sum(resid_low.astype(jnp.float32), axis=0)
    grad_down = jnp.einsum("rf,rd->fd", act_low, resid_low, preferred_element_type=jnp.float32)
    grad_act = jnp.einsum("rd,fd->rf", resid_low, down_full, preferred_element_type=jnp.float32)
    grad_pre = act_pull(grad_act)[0].astype(jnp.bfloat16)
    grad_up = jnp.einsum("rd,rf->df", first_low, grad_pre, preferred_element_type=jnp.float32)
    grad_bias_up = jnp.sum(grad_pre.astype(jnp.float32), axis=0).reshape(bias_up.shape)
    first_back = lax.psum(
        jnp.einsum("rf,df->rd", grad_pre, up_full, preferred_element_type=jnp.float32).astype(
            jnp.bfloat16
        ),
        "heads",
    ).astype(jnp.float32)
    grad_first = resid_two + first_back
    grad_gain_one = jnp.sum(grad_first * normed_one, axis=0)
    grad_shift_one = jnp.sum(grad_first, axis=0)
    resid_one = norm_backward(grad_first, normed_one, inverse_one, gain_rows[0])
    resid_one_low = resid_one.astype(jnp.bfloat16)
    grad_bias_out = jnp.sum(resid_one_low.astype(jnp.float32), axis=0)
    grad_out = jnp.einsum("rc,rd->cd", attn_low, resid_one_low, preferred_element_type=jnp.float32)
    grad_attn = jnp.einsum(
        "rd,cd->rc", resid_one_low, out_full, preferred_element_type=jnp.float32
    ).reshape(rows_own, local_heads, HEAD)
    grad_numer = (grad_attn / denom_rows[:, :, None]).astype(jnp.bfloat16)
    grad_denom = (-jnp.sum(grad_attn * quotient, axis=-1) / denom_rows).astype(jnp.bfloat16)
    numer_grad_all, denom_grad_all = (
        lax.all_gather(grad_numer.reshape(rows_own, head_cols), "feat", axis=0, tiled=True),
        lax.all_gather(grad_denom.T, "feat", axis=1, tiled=True),
    )
    numer_grad_all = numer_grad_all.reshape(rows_total, local_heads, HEAD)
    dphi_key = jnp.zeros((local_heads, local_feats, rows_total), jnp.float32)
    dvalues = jnp.zeros((rows_total, local_heads, HEAD), jnp.float32)
    grad_rpe = jnp.zeros(rpe_exp.shape, jnp.float32)
    dquery_parts = []
    for row_block in range(blocks):
        row_start = row_block * block_rows
        first_block = row_start // seq_length * block_count
        phi_rows = feat_query[:, :, row_start : row_start + block_rows]
        numer_rows = numer_grad_all[row_start : row_start + block_rows]
        denom_cols = denom_grad_all[:, row_start : row_start + block_rows].astype(jnp.float32)

        def visit_back(
            column_block,
            carried,
            phi_rows=phi_rows,
            row_start=row_start,
            numer_rows=numer_rows,
            denom_cols=denom_cols,
        ):
            dquery_acc, dkey_all, dvalue_all, drpe_all = carried
            col_start = column_block * block_rows
            phi_cols = lax.dynamic_slice_in_dim(feat_key, col_start, block_rows, 2)
            value_cols = lax.dynamic_slice_in_dim(values_rows, col_start, block_rows, 0)
            window_start = window_begin(row_start, col_start, block_rows, rows_total)
            coefficient = block_coeff(rpe_exp, window_start, block_rows)
            scores = jnp.einsum(
                "hmi,hmj->hij", phi_rows, phi_cols, preferred_element_type=jnp.float32
            )
            weights = (coefficient * scores).astype(jnp.bfloat16)
            grad_weights = (
                jnp.einsum(
                    "ihe,jhe->hij", numer_rows, value_cols, preferred_element_type=jnp.float32
                )
                + denom_cols[:, :, None]
            )
            dvalue_block = jnp.einsum(
                "hij,ihe->jhe", weights, numer_rows, preferred_element_type=jnp.float32
            )
            dvalue_all = lax.dynamic_update_slice_in_dim(
                dvalue_all,
                lax.dynamic_slice_in_dim(dvalue_all, col_start, block_rows, 0) + dvalue_block,
                col_start,
                0,
            )
            grad_scores = (grad_weights * coefficient).astype(jnp.bfloat16)
            diagonal = diagonal_sums(grad_weights * scores * coefficient, block_rows)
            drpe_all = lax.dynamic_update_slice_in_dim(
                drpe_all,
                lax.dynamic_slice_in_dim(drpe_all, window_start, 2 * block_rows - 1, 1) + diagonal,
                window_start,
                1,
            )
            dquery_acc = dquery_acc + jnp.einsum(
                "hij,hmj->hmi", grad_scores, phi_cols, preferred_element_type=jnp.float32
            )
            dkey_block = jnp.einsum(
                "hij,hmi->hmj", grad_scores, phi_rows, preferred_element_type=jnp.float32
            )
            dkey_all = lax.dynamic_update_slice_in_dim(
                dkey_all,
                lax.dynamic_slice_in_dim(dkey_all, col_start, block_rows, 2) + dkey_block,
                col_start,
                2,
            )
            return (dquery_acc, dkey_all, dvalue_all, drpe_all)

        start_state = (
            jnp.zeros((local_heads, local_feats, block_rows), jnp.float32),
            dphi_key,
            dvalues,
            grad_rpe,
        )
        dquery_block, dphi_key, dvalues, grad_rpe = lax.fori_loop(
            first_block, first_block + block_count, visit_back, start_state
        )
        dquery_parts.append(dquery_block)
    dphi_query = jnp.concatenate(dquery_parts, axis=2)
    grad_query = feature_back(dphi_query, logits_query, unit_query, inverse_query, omega)
    grad_key = feature_back(dphi_key, logits_key, unit_key, inverse_key, omega)
    grad_qkv_all = jnp.stack((grad_query, grad_key, dvalues), axis=1).reshape(
        rows_total, 3 * head_cols
    )
    grad_qkv_own = lax.psum_scatter(
        grad_qkv_all.astype(jnp.bfloat16), "feat", scatter_dimension=0, tiled=True
    )
    grad_bias_qkv = jnp.sum(grad_qkv_own.astype(jnp.float32), axis=0).reshape(bias_qkv.shape)
    grad_qkv_weight = jnp.einsum(
        "rd,rc->dc", tokens, grad_qkv_own, preferred_element_type=jnp.float32
    ).reshape(qkv_full.shape)
    input_terms = jnp.einsum(
        "rc,dc->rd",
        grad_qkv_own,
        qkv_full.reshape(model_width, 3 * head_cols),
        preferred_element_type=jnp.float32,
    )
    grad_tokens = resid_one + lax.psum(input_terms.astype(jnp.bfloat16), "heads").astype(
        jnp.float32
    )
    grad_gains = jnp.stack((grad_gain_one, grad_gain_two), axis=0)
    grad_shifts = jnp.stack((grad_bias_out, grad_shift_one, grad_bias_down, grad_shift_two), axis=0)
    (
        sent_qkv,
        sent_out,
        sent_up,
        sent_down,
        sent_gains,
        sent_shifts,
        sent_bias_qkv,
        sent_bias_up,
        sent_rpe,
    ) = (
        lax.psum_scatter(
            grad_qkv_weight.astype(jnp.bfloat16), ("dp", "feat"), scatter_dimension=0, tiled=True
        ).astype(jnp.float32),
        lax.psum_scatter(
            grad_out.astype(jnp.bfloat16), ("dp", "feat"), scatter_dimension=1, tiled=True
        ).astype(jnp.float32),
        lax.psum_scatter(
            grad_up.astype(jnp.bfloat16), ("dp", "feat"), scatter_dimension=0, tiled=True
        ).astype(jnp.float32),
        lax.psum_scatter(
            grad_down.astype(jnp.bfloat16), ("dp", "feat"), scatter_dimension=1, tiled=True
        ).astype(jnp.float32),
        lax.psum_scatter(
            grad_gains.astype(jnp.bfloat16), ("dp", "feat"), scatter_dimension=1, tiled=True
        ).astype(jnp.float32),
        lax.psum_scatter(
            grad_shifts.astype(jnp.bfloat16), ("dp", "feat"), scatter_dimension=1, tiled=True
        ).astype(jnp.float32),
        lax.psum_scatter(
            grad_bias_qkv.astype(jnp.bfloat16), ("dp", "feat"), scatter_dimension=2, tiled=True
        ).astype(jnp.float32),
        lax.psum_scatter(
            grad_bias_up.astype(jnp.bfloat16), ("dp", "feat"), scatter_dimension=1, tiled=True
        ).astype(jnp.float32),
        lax.psum_scatter(
            grad_rpe.astype(jnp.bfloat16), ("dp", "feat"), scatter_dimension=1, tiled=True
        ).astype(jnp.float32),
    )
    return (
        mixed,
        grad_tokens,
        sent_qkv,
        sent_bias_qkv,
        sent_out,
        sent_gains,
        sent_shifts,
        sent_up,
        sent_bias_up,
        sent_down,
        sent_rpe,
    )


def solution(mesh):
    return jax.shard_map(
        local,
        mesh=mesh,
        in_specs=(
            P(("dp", "feat"), None),
            P(("dp", "feat"), None, "heads"),
            P(None, "heads", ("dp", "feat")),
            P("heads", ("dp", "feat")),
            P(None, ("dp", "feat")),
            P(None, ("dp", "feat")),
            P(("dp", "feat"), "heads"),
            P("heads", ("dp", "feat")),
            P("heads", ("dp", "feat")),
            P("heads", ("dp", "feat")),
            P("heads", None, "feat"),
            P("dp"),
            P(("dp", "feat"), None),
        ),
        out_specs=(
            P(("dp", "feat"), None),
            P(("dp", "feat"), None),
            P(("dp", "feat"), None, "heads"),
            P(None, "heads", ("dp", "feat")),
            P("heads", ("dp", "feat")),
            P(None, ("dp", "feat")),
            P(None, ("dp", "feat")),
            P(("dp", "feat"), "heads"),
            P("heads", ("dp", "feat")),
            P("heads", ("dp", "feat")),
            P("heads", ("dp", "feat")),
        ),
        check_vma=False,
    )
```

profile of v0, /device:TPU:0, one launch (start us, length us, event | category | flops | bytes accessed | tf_op | source)
XLA Modules:
  0.0 1194.6 jit_solution(3078951095035628986)
XLA Ops:
  8.7 23.2 %all_gather.43 = bf16[3,8,64]{1,0,2:T(4,128)(2,1)S(1)} all-gather(bf16[3,8,4]{1,0,2:T(4,128)(2,1)S(1)} %copy.215), channel_id=1, replica_groups=mesh['dp'=8,'heads'=2,'feat'=2] {'dp','feat'}, dimensions={2}, use_global_device_ids=true | all-gather | bytes 3264 | tf_op jit(solution)/shard_map/all_gather | solution.py:106
  32.1 26.2 %all-gather.10.cloned.1.call-done = bf16[1024,3,512]{2,0,1:T(8,128)(2,1)} async-done(((bf16[64,3,512]{2,0,1:T(8,128)(2,1)}), bf16[1024,3,512]{2,0,1:T(8,128)(2,1)}) %all-gather.10.cloned.1.call-update) | async-done | bytes 3145744 | tf_op jit(solution)/shard_map/all_gather | solution.py:100
  58.2 4.7 copy.214
  67.5 19.3 %all-gather = bf16[16,64,8]{1,2,0:T(8,128)(2,1)S(1)} all-gather(bf16[1,64,8]{1,2,0:T(8,128)(2,1)S(1)} %bitcast.541), channel_id=1, replica_groups=mesh['dp'=8,'heads'=2,'feat'=2] {'dp','feat'}, dimensions={0}, use_global_device_ids=true | all-gather | bytes 17408 | tf_op jit(solution)/shard_map/all_gather | solution.py:108
  93.9 15.4 %while.144 = (s32[]{:T(128)}, f32[128,8,64]{0,2,1:T(8,128)S(1)}, f32[8,128]{1,0:T(8,128)S(1)}, s32[]{:T(128)}, bf16[512,8,64]{0,2,1:T(8,128)(2,1)}, /*index=5*/f...) while((s32[]{:T(128)}, f32[128,8,64]{0,2,1:T(8,128)S(1)}, ...), condition=%wide.region_6.7_spmd, body=%wide.region_4.6_spmd.sunk | while | flops 25755656 | bytes 12345497 | solution.py:167
  110.0 15.4 %while.145 = (s32[]{:T(128)}, f32[128,8,64]{0,2,1:T(8,128)S(1)}, f32[8,128]{1,0:T(8,128)S(1)}, s32[]{:T(128)}, bf16[512,8,64]{0,2,1:T(8,128)(2,1)}, /*index=5*/f...) while((s32[]{:T(128)}, f32[128,8,64]{0,2,1:T(8,128)S(1)}, ...), condition=%wide.region_9.10_spmd, body=%wide.region_7.9_spmd.sunk | while | flops 25755656 | bytes 12345497 | solution.py:167
  126.1 15.4 %while.146 = (s32[]{:T(128)}, f32[128,8,64]{0,2,1:T(8,128)S(1)}, f32[8,128]{1,0:T(8,128)S(1)}, s32[]{:T(128)}, bf16[512,8,64]{0,2,1:T(8,128)(2,1)}, /*index=5*/f...) while((s32[]{:T(128)}, f32[128,8,64]{0,2,1:T(8,128)S(1)}, ...), condition=%wide.region_12.13_spmd, body=%wide.region_10.12_spmd.sunk | while | flops 25755656 | bytes 12345497 | solution.py:167
  142.3 15.4 %while.147 = (s32[]{:T(128)}, f32[128,8,64]{0,2,1:T(8,128)S(1)}, f32[8,128]{1,0:T(8,128)S(1)}, s32[]{:T(128)}, bf16[512,8,64]{0,2,1:T(8,128)(2,1)}, /*index=5*/f...) while((s32[]{:T(128)}, f32[128,8,64]{0,2,1:T(8,128)S(1)}, ...), condition=%wide.region_15.16_spmd, body=%wide.region_13.15_spmd.sunk | while | flops 25755656 | bytes 12345497 | solution.py:167
  163.8 11.2 reduce-scatter.18.cloned.1.call-done
  176.0 40.4 %all-gather.14.cloned.1.call-done = bf16[512,1024]{0,1:T(8,128)(2,1)} async-done(((bf16[512,64]{0,1:T(8,128)(2,1)}), bf16[512,1024]{0,1:T(8,128)(2,1)}) %all-gather.14.cloned.1.call-update) | async-done | bytes 1048592 | tf_op jit(solution)/shard_map/all_gather | solution.py:101
  220.4 19.3 %all-gather.1 = bf16[16,64,4]{1,2,0:T(4,128)(2,1)S(1)} all-gather(bf16[1,64,4]{1,2,0:T(4,128)(2,1)S(1)} %bitcast.542), channel_id=1, replica_groups=mesh['dp'=8,'heads'=2,'feat'=2] {'dp','feat'}, dimensions={0}, use_global_device_ids=true | all-gather | bytes 8704 | tf_op jit(solution)/shard_map/all_gather | solution.py:105
  239.9 17.3 %all-gather.2 = bf16[16,64,2]{1,2,0:T(2,128)(2,1)S(1)} all-gather(bf16[1,64,2]{1,2,0:T(2,128)(2,1)S(1)} %bitcast.544), channel_id=1, replica_groups=mesh['dp'=8,'heads'=2,'feat'=2] {'dp','feat'}, dimensions={0}, use_global_device_ids=true | all-gather | bytes 4352 | tf_op jit(solution)/shard_map/all_gather | solution.py:104
  257.3 18.8 %all-gather.3 = bf16[16,4,32]{2,1,0:T(4,128)(2,1)S(1)} all-gather(bf16[1,4,32]{2,1,0:T(4,128)(2,1)S(1)} %bitcast.543), channel_id=1, replica_groups=mesh['dp'=8,'heads'=2,'feat'=2] {'dp','feat'}, dimensions={0}, use_global_device_ids=true | all-gather | bytes 4352 | tf_op jit(solution)/shard_map/all_gather | solution.py:107
  279.1 20.5 %all-gather.16.cloned.1.call-done = bf16[1024,2048]{1,0:T(8,128)(2,1)} async-done(((bf16[64,2048]{1,0:T(8,128)(2,1)}), bf16[1024,2048]{1,0:T(8,128)(2,1)}) %all-gather.16.cloned.1.call-update) | async-done | bytes 4194320 | tf_op jit(solution)/shard_map/all_gather | solution.py:102
  299.6 9.0 multiply_convert_fusion.12
  308.6 42.2 %all-gather.18.cloned.1.call-done = bf16[2048,1024]{0,1:T(8,128)(2,1)} async-done(((bf16[2048,64]{0,1:T(8,128)(2,1)}), bf16[2048,1024]{0,1:T(8,128)(2,1)}) %all-gather.18.cloned.1.call-update) | async-done | bytes 4194320 | tf_op jit(solution)/shard_map/all_gather | solution.py:103
  355.2 27.2 %all-reduce.22.cloned.1.call-done = bf16[256,1024]{1,0:T(8,128)(2,1)} async-done(((bf16[256,1024]{1,0:T(8,128)(2,1)}), bf16[256,1024]{1,0:T(8,128)(2,1)}) %all-reduce.22.cloned.1.call-update) | async-done | bytes 524304 | tf_op jit(solution)/shard_map/psum | solution.py:197
  399.4 25.6 %all-reduce.24.cloned.1.call-done = bf16[256,1024]{1,0:T(8,128)(2,1)} async-done(((bf16[256,1024]{1,0:T(8,128)(2,1)}), bf16[256,1024]{1,0:T(8,128)(2,1)}) %all-reduce.24.cloned.1.call-update) | async-done | bytes 524304 | tf_op jit(solution)/shard_map/psum | solution.py:223
  438.8 58.2 %while.148 = (s32[]{:T(128)}, f32[8,32,128]{2,1,0:T(8,128)}, f32[8,32,512]{2,1,0:T(8,128)}, f32[512,8,64]{0,2,1:T(8,128)}, f32[8,1024]{1,0:T(8,128)}, /*index=5*...) while((s32[]{:T(128)}, f32[8,32,128]{2,1,0:T(8,128)}, ...), condition=%wide.region_32.33_spmd, body=%wide.region_30.32_spmd.sunk | while | flops 60029960 | bytes 30843092 | solution.py:318
  498.7 61.4 %while.149 = (s32[]{:T(128)}, f32[8,32,128]{2,1,0:T(8,128)}, f32[8,32,512]{2,1,0:T(8,128)}, f32[512,8,64]{0,2,1:T(8,128)}, f32[8,1024]{1,0:T(8,128)}, /*index=5*...) while((s32[]{:T(128)}, f32[8,32,128]{2,1,0:T(8,128)}, ...), condition=%wide.region_35.36_spmd, body=%wide.region_33.35_spmd.sunk | while | flops 60029960 | bytes 30318748 | solution.py:318
  561.8 61.7 %while.150 = (s32[]{:T(128)}, f32[8,32,128]{2,1,0:T(8,128)}, f32[8,32,512]{2,1,0:T(8,128)}, f32[512,8,64]{0,2,1:T(8,128)}, f32[8,1024]{1,0:T(8,128)}, /*index=5*...) while((s32[]{:T(128)}, f32[8,32,128]{2,1,0:T(8,128)}, ...), condition=%wide.region_38.39_spmd, body=%wide.region_36.38_spmd.sunk | while | flops 60029960 | bytes 30318748 | solution.py:318
  625.2 57.7 %while.151 = (s32[]{:T(128)}, f32[8,32,128]{2,1,0:T(8,128)}, f32[8,32,512]{2,1,0:T(8,128)}, f32[512,8,64]{0,2,1:T(8,128)}, f32[8,1024]{1,0:T(8,128)}, /*index=5*...) while((s32[]{:T(128)}, f32[8,32,128]{2,1,0:T(8,128)}, ...), condition=%wide.region_41.42_spmd, body=%wide.region_39.41_spmd.sunk | while | flops 60029960 | bytes 30318748 | solution.py:318
  700.8 4.6 convolution_convert_fusion.2
  715.0 4.7 copy.228
  721.7 35.9 %reduce-scatter.32.cloned.1.call-done = bf16[64,2]{1,0:T(8,128)(2,1)} async-done(((bf16[1024,2]{1,0:T(8,128)(2,1)}), bf16[64,2]{1,0:T(8,128)(2,1)}) %reduce-scatter.32.cloned.1.call-update) | async-done | bytes 272
  759.0 56.8 %reduce-scatter.34.cloned.1.call-done = bf16[64,4]{1,0:T(8,128)(2,1)} async-done(((bf16[1024,4]{1,0:T(8,128)(2,1)}), bf16[64,4]{1,0:T(8,128)(2,1)}) %reduce-scatter.34.cloned.1.call-update) | async-done | bytes 528
  817.2 56.8 %reduce-scatter.36.cloned.1.call-done = bf16[64,8]{1,0:T(8,128)(2,1)} async-done(((bf16[1024,8]{1,0:T(8,128)(2,1)}), bf16[64,8]{1,0:T(8,128)(2,1)}) %reduce-scatter.36.cloned.1.call-update) | async-done | bytes 1040
  875.4 58.9 %reduce-scatter.26.cloned.1.call-done = bf16[512,64]{0,1:T(8,128)(2,1)} async-done(((bf16[512,1024]{0,1:T(8,128)(2,1)}), bf16[512,64]{0,1:T(8,128)(2,1)}) %reduce-scatter.26.cloned.1.call-update) | async-done | bytes 65552 | tf_op jit(solution)/shard_map/reduce_scatter | solution.py:360
  936.3 58.4 %all-reduce.14 = (bf16[3,8,64]{1,0,2:T(4,128)(2,1)S(1)}, bf16[32,64]{1,0:T(8,128)(2,1)S(1)}) all-reduce(bf16[3,8,64]{1,0,2:T(4,128)(2,1)S(1)} %copy.229, bf16[32,64]{1,0:T(8,128)(2,1)S(1)} %convert_element_type.451), channel_id=6, replica_groups=mesh['dp'=8,'heads'=2,'feat'=2] {'dp','feat'}, use_global_device_ids=true, to_apply=%region_50.51.clone | all-reduce | flops 3584 | bytes 14336
  998.2 43.0 %reduce-scatter.28.cloned.1.call-done = bf16[64,2048]{1,0:T(8,128)(2,1)} async-done(((bf16[1024,2048]{1,0:T(8,128)(2,1)}), bf16[64,2048]{1,0:T(8,128)(2,1)}) %reduce-scatter.28.cloned.1.call-update) | async-done | bytes 262160 | tf_op jit(solution)/shard_map/reduce_scatter | solution.py:363
  1043.0 73.4 %reduce-scatter.30.cloned.1.call-done = bf16[2048,64]{0,1:T(8,128)(2,1)} async-done(((bf16[2048,1024]{0,1:T(8,128)(2,1)}), bf16[2048,64]{0,1:T(8,128)(2,1)}) %reduce-scatter.30.cloned.1.call-update) | async-done | bytes 262160 | tf_op jit(solution)/shard_map/reduce_scatter | solution.py:366
  1118.2 67.8 %reduce-scatter.24.cloned.1.call-done = bf16[64,3,512]{2,0,1:T(8,128)(2,1)} async-done(((bf16[1024,3,512]{2,0,1:T(8,128)(2,1)}), bf16[64,3,512]{2,0,1:T(8,128)(2,1)}) %reduce-scatter.24.cloned.1.call-update) | async-done | bytes 196624 | tf_op jit(solution)/shard_map/reduce_scatter | solution.py:357
  (992 shorter events, 407.8 us)
Async XLA Ops:
  7.2 83.8 %copy-start = (bf16[8,64,32]{1,2,0:T(8,128)(2,1)S(1)}, bf16[8,64,32]{1,2,0:T(8,128)(2,1)}, u32[]{:S(2)}) copy-start(bf16[8,64,32]{1,2,0:T(8,128)(2,1)} %param.39) | copy-start | bytes 98308
  7.2 51.0 %all-gather.10.cloned.1.call-start = ((), (), s32[]{:S(2)}) async-start(), calls=%async_computation.10 | async-start | bytes 3342336 | tf_op jit(solution)/shard_map/all_gather | solution.py:100
  7.9 79.6 %all-gather.12.cloned.1.call-start = ((), (), s32[]{:S(2)}) async-start(), calls=%async_computation.11 | async-start | bytes 2359296 | tf_op jit(solution)/shard_map/all_gather | solution.py:128
  32.1 30.8 %copy-start.6 = (bf16[256,1024]{1,0:T(8,128)(2,1)S(1)}, bf16[256,1024]{1,0:T(8,128)(2,1)}, u32[]{:S(2)}) copy-start(bf16[256,1024]{1,0:T(8,128)(2,1)} %param.29) | copy-start | bytes 1572868
  66.7 96.4 %reduce-scatter.20.cloned.1.call-start = ((), (), s32[]{:S(2)}) async-start(), calls=%async_computation.13 | async-start | bytes 12288 | tf_op jit(solution)/shard_map/reduce_scatter | solution.py:178
  158.3 16.6 %reduce-scatter.18.cloned.1.call-start = ((), (), s32[]{:S(2)}) async-start(), calls=%async_computation.12 | async-start | bytes 786432 | tf_op jit(solution)/shard_map/reduce_scatter | solution.py:175
  160.3 60.1 %copy-start.71 = (bf16[4,64]{1,0:T(4,128)(2,1)S(1)}, bf16[4,64]{1,0:T(4,128)(2,1)}, u32[]{:S(2)}) copy-start(bf16[4,64]{1,0:T(4,128)(2,1)} %param.34) | copy-start | bytes 1540
  160.3 79.6 %copy-start.73 = (bf16[2,64]{1,0:T(2,128)(2,1)S(1)}, bf16[2,64]{1,0:T(2,128)(2,1)}, u32[]{:S(2)}) copy-start(bf16[2,64]{1,0:T(2,128)(2,1)} %param.33) | copy-start | bytes 772
  160.3 97.0 %copy-start.72 = (bf16[32,4]{0,1:T(4,128)(2,1)S(1)}, bf16[32,4]{0,1:T(4,128)(2,1)}, u32[]{:S(2)}) copy-start(bf16[32,4]{0,1:T(4,128)(2,1)} %param.36) | copy-start | bytes 772
  160.3 56.0 %all-gather.14.cloned.1.call-start = ((), (), s32[]{:S(2)}) async-start(), calls=%async_computation.14 | async-start | bytes 1114112 | tf_op jit(solution)/shard_map/all_gather | solution.py:101
  160.9 115.4 %all-reduce.20.cloned.1.call-start = ((), (), s32[]{:S(2)}) async-start(), calls=%async_computation.15 | async-start | bytes 1048576 | tf_op jit(solution)/shard_map/psum | solution.py:186
  176.0 101.7 %copy-start.40 = (bf16[256,512]{0,1:T(8,128)(2,1)}, bf16[256,512]{0,1:T(8,128)(2,1)S(1)}, u32[]{:S(2)}) copy-start(bf16[256,512]{0,1:T(8,128)(2,1)S(1)} %divide_convert_fusion.1) | copy-start | bytes 786436
  218.9 80.8 %all-gather.16.cloned.1.call-start = ((), (), s32[]{:S(2)}) async-start(), calls=%async_computation.16 | async-start | bytes 4456448 | tf_op jit(solution)/shard_map/all_gather | solution.py:102
  219.6 131.3 %all-gather.18.cloned.1.call-start = ((), (), s32[]{:S(2)}) async-start(), calls=%async_computation.17 | async-start | bytes 4456448 | tf_op jit(solution)/shard_map/all_gather | solution.py:103
  220.4 162.1 %all-reduce.22.cloned.1.call-start = ((), (), s32[]{:S(2)}) async-start(), calls=%async_computation.18 | async-start | bytes 1048576 | tf_op jit(solution)/shard_map/psum | solution.py:197
  276.2 151.2 %copy-start.52 = (f32[1,1024]{1,0:T(1,128)}, f32[1,1024]{1,0:T(1,128)S(1)}, u32[]{:S(2)}) copy-start(f32[1,1024]{1,0:T(1,128)S(1)} %get-tuple-element.2013) | copy-start | bytes 12292
  276.3 106.2 %copy-start.54 = (f32[1,1024]{1,0:T(1,128)}, f32[1,1024]{1,0:T(1,128)S(1)}, u32[]{:S(2)}) copy-start(f32[1,1024]{1,0:T(1,128)S(1)} %get-tuple-element.2006) | copy-start | bytes 12292
  276.3 151.1 %copy-start.48 = (f32[1,1024]{1,0:T(1,128)}, f32[1,1024]{1,0:T(1,128)S(1)}, u32[]{:S(2)}) copy-start(f32[1,1024]{1,0:T(1,128)S(1)} %get-tuple-element.2007) | copy-start | bytes 12292
  277.7 149.7 %copy-start.58 = (f32[256]{0:T(256)}, f32[256]{0:T(256)S(1)}, u32[]{:S(2)}) copy-start(f32[256]{0:T(256)S(1)} %broadcast_multiply_fusion.7) | copy-start | bytes 3076
  279.1 148.4 %copy-start.60 = (f32[256]{0:T(256)}, f32[256]{0:T(256)S(1)}, u32[]{:S(2)}) copy-start(f32[256]{0:T(256)S(1)} %add_rsqrt_fusion.3) | copy-start | bytes 3076
  308.6 46.5 %copy-start.39 = (bf16[256,2048]{1,0:T(8,128)(2,1)}, bf16[256,2048]{1,0:T(8,128)(2,1)S(1)}, u32[]{:S(2)}) copy-start(bf16[256,2048]{1,0:T(8,128)(2,1)S(1)} %get-tuple-element.1974) | copy-start | bytes 3145732
  355.2 69.8 %all-reduce.24.cloned.1.call-start = ((), (), s32[]{:S(2)}) async-start(), calls=%async_computation.19 | async-start | bytes 1048576 | tf_op jit(solution)/shard_map/psum | solution.py:223
  396.2 28.8 %copy-start.13 = (f32[256,1024]{1,0:T(8,128)S(1)}, f32[256,1024]{1,0:T(8,128)}, u32[]{:S(2)}) copy-start(f32[256,1024]{1,0:T(8,128)} %copy-done.12) | copy-start | bytes 3145732
  396.3 300.4 %reduce-scatter.22.cloned.1.call-start = ((), (), s32[]{:S(2)}) async-start(), calls=%async_computation.20 | async-start | bytes 2359296 | tf_op jit(solution)/shard_map/reduce_scatter | solution.py:328
  689.3 68.3 %reduce-scatter.32.cloned.1.call-start = ((), (), s32[]{:S(2)}) async-start(), calls=%async_computation.26 | async-start | bytes 278528
  690.4 125.4 %reduce-scatter.34.cloned.1.call-start = ((), (), s32[]{:S(2)}) async-start(), calls=%async_computation.27 | async-start | bytes 278528
  691.4 182.5 %reduce-scatter.36.cloned.1.call-start = ((), (), s32[]{:S(2)}) async-start(), calls=%async_computation.28 | async-start | bytes 278528
  692.4 241.9 %reduce-scatter.26.cloned.1.call-start = ((), (), s32[]{:S(2)}) async-start(), calls=%async_computation.23 | async-start | bytes 1114112 | tf_op jit(solution)/shard_map/reduce_scatter | solution.py:360
  694.3 301.8 %all-reduce.26.cloned.1.call-start = ((), (), s32[]{:S(2)}) async-start(), calls=%async_computation.21 | async-start | bytes 1048576 | tf_op jit(solution)/shard_map/psum | solution.py:341
  700.6 340.6 %reduce-scatter.28.cloned.1.call-start = ((), (), s32[]{:S(2)}) async-start(), calls=%async_computation.24 | async-start | bytes 4456448 | tf_op jit(solution)/shard_map/reduce_scatter | solution.py:363
  705.4 411.0 %reduce-scatter.30.cloned.1.call-start = ((), (), s32[]{:S(2)}) async-start(), calls=%async_computation.25 | async-start | bytes 4456448 | tf_op jit(solution)/shard_map/reduce_scatter | solution.py:366
  711.2 474.8 %reduce-scatter.24.cloned.1.call-start = ((), (), s32[]{:S(2)}) async-start(), calls=%async_computation.22 | async-start | bytes 3342336 | tf_op jit(solution)/shard_map/reduce_scatter | solution.py:357
  (131 other events, 570.5 us)
Sparse Core Ops, SparseCore 0:
  10.2 47.9 all-gather.9
  66.9 8.6 all-gather.11
  158.5 4.6 reduce-scatter.19
  165.8 9.1 reduce-scatter.17
  177.2 39.0 all-gather.13
  219.2 27.5 all-reduce.19
  248.9 50.7 all-gather.15
  301.8 49.0 all-gather.17
  355.3 27.0 all-reduce.21
  396.4 28.5 all-reduce.23
  689.4 7.2 reduce-scatter.21
  701.0 56.5 reduce-scatter.31
  761.5 54.2 reduce-scatter.33
  819.6 54.3 reduce-scatter.35
  877.9 56.3 reduce-scatter.25
  937.0 27.5 all-reduce.25
  968.8 72.3 reduce-scatter.27
  1045.0 71.4 reduce-scatter.29
  1120.7 65.2 reduce-scatter.23
where the time goes:
time: 1210 us; the launch traced here: 1190 us
  waiting for transfers between devices  593 us (49%)
  local copies, waits for them, and re-layouts  188 us (16%)
  matrix products  179 us (15%)
  blocking collectives  160 us (13%)
  other arithmetic  50.4 us (4%)
  between operations  16.8 us (1%)
    unnamed x22, waiting for transfers between devices  152 us
    reduce_scatter x1, waiting for transfers between devices, local(): lax.psum_scatter(grad_down.astype(jnp.bfloat16), ('dp', 'feat'), scatter_...  73.4 us
    reduce_scatter x1, waiting for transfers between devices, local(): lax.psum_scatter(grad_qkv_weight.astype(jnp.bfloat16), ('dp', 'feat'), sc...  67.8 us
    reduce_scatter x1, waiting for transfers between devices, local(): lax.psum_scatter(grad_out.astype(jnp.bfloat16), ('dp', 'feat'), scatter_d...  58.9 us
    unnamed x1, blocking collectives  58.4 us
    reduce_scatter x1, waiting for transfers between devices, local(): lax.psum_scatter(grad_up.astype(jnp.bfloat16), ('dp', 'feat'), scatter_di...  43 us
    all_gather x1, waiting for transfers between devices, local(): lax.all_gather(down_weight, ('dp', 'feat'), axis=1, tiled=True)  42.2 us
    while x288, local copies, waits for them, and re-layouts  42.2 us
  transfers between devices with their start and end apart: 19, of which 16 were waited for; matrix products, arithmetic and copies ran while one was open for 5% of the time, Pallas kernels for 0%

commit v1 on v0

--- a/solution.py
+++ b/solution.py
@@ -1,6 +1,10 @@
+import functools
+
 import jax
 import jax.numpy as jnp
 from jax import lax
+from jax.experimental import pallas as pl
+from jax.experimental.pallas import tpu as pltpu
 from jax.sharding import PartitionSpec as P
 
 HEAD = 64
@@ -397,9 +401,774 @@
     )
 
 
+MESH = pl.DeviceIdType.MESH
+PLANES = 4
+F32 = jnp.float32
+BF16 = jnp.bfloat16
+SCALE = HEAD ** (-0.25)
+NT = (((1,), (1,)), ((), ()))
+TN = (((0,), (0,)), ((), ()))
+NN = (((1,), (0,)), ((), ()))
+
+
+def dot(left, right, dims=NN):
+    return lax.dot_general(left, right, dims, preferred_element_type=F32)
+
+
+def split_dot(left, right, dims=NN):
+    high = left.astype(BF16)
+    rest = (left - high.astype(F32)).astype(BF16)
+    return dot(high, right, dims) + dot(rest, right, dims)
+
+
+def iota(shape, axis):
+    return lax.broadcasted_iota(jnp.int32, shape, axis)
+
+
+class Sems:
+    def __init__(self):
+        self.used = 0
+
+    def take(self, count=1):
+        first = self.used
+        self.used += count
+        return first
+
+
+def layer_kernel(
+    tok, cot, wq_in, wo_in, wu_in, wd_in, small_in, omega_in,
+    mixed_o, gtok_o, gq_o, go_o, gu_o, gd_o, dvec_o, tvec_o,
+    wq, wo, wu, wd, small, om2, xg, cotb,
+    qkv, phi, ex, unit, inv, r0, pp, num, den, quo, att,
+    pb, rb_z, rb_f, rb_d, rb_i, fb, hid, dgel, efb, dub, dzb,
+    fst, n1, i1, dr,
+    dn, dd, ds_, gg, dph, dvv, dqkv, anti, ones64, rows_v,
+    g_q, g_o, g_u, g_d, r1_q, r1_o, r1_u, r1_d, t_q, t_o, t_u, t_d,
+    rz_q, rz_o, rz_u, rz_d, cb_q, cb_o, cb_u, cb_d, fs, xs, xr_q, xr_o, xr_u, xr_d,
+    sd, sd_r, st, st_r, mix_s, mix_r, gt_s, gt_r,
+    ss, rs,
+):
+    dp, y, c = lax.axis_index("dp"), lax.axis_index("heads"), lax.axis_index("feat")
+    z, x = dp // 2, dp % 2
+    sems = Sems()
+    pending = []
+
+    def dev(zz, xx, yy, cc):
+        return {"dp": zz * 2 + xx, "heads": yy, "feat": cc}
+
+    sib, xn, yn, dg = dev(z, x, y, 1 - c), dev(z, 1 - x, y, c), dev(z, x, 1 - y, c), dev(z, 1 - x, 1 - y, c)
+    xs_dev, ds_dev = dev(z, 1 - x, y, 1 - c), dev(z, 1 - x, 1 - y, 1 - c)
+    plane = (dg, xn, yn)
+    own_block = 2 * x + y
+    plane_block = (2 * (1 - x) + 1 - y, 2 * (1 - x) + y, 2 * x + 1 - y)
+
+    def rc(src, dst, s, r, device):
+        return pltpu.make_async_remote_copy(
+            src_ref=src, dst_ref=dst, send_sem=ss.at[s], recv_sem=rs.at[r], device_id=device, device_id_type=MESH
+        )
+
+    def send(src, dst, s, r, device, cond=None):
+        def go():
+            rc(src, dst, s, r, device).start()
+
+        def done():
+            rc(src, dst, s, r, device).wait_send()
+
+        if cond is None:
+            go()
+            pending.append(done)
+        else:
+            pl.when(cond)(go)
+            pending.append(lambda: pl.when(cond)(done))
+
+    def got(dst, r):
+        rc(dst, dst, r, r, sib).wait_recv()
+
+    def valid(dz):
+        return jnp.logical_and(z + dz >= 0, z + dz < PLANES)
+
+    barrier = pltpu.get_barrier_semaphore()
+    for other in (sib, xn, yn, dg, xs_dev, ds_dev):
+        pl.semaphore_signal(barrier, inc=1, device_id=other, device_id_type=MESH)
+    for zz in range(PLANES):
+        @pl.when(z != zz)
+        def _(zz=zz):
+            pl.semaphore_signal(barrier, inc=1, device_id=dev(zz, x, y, c), device_id_type=MESH)
+    pl.semaphore_wait(barrier, 9)
+
+    class Item:
+        def __init__(self, ref, kind):
+            self.ref, self.kind = ref, kind
+            self.zs, self.fw, self.sb = sems.take(PLANES), sems.take(), sems.take(PLANES)
+
+        def block(self, zz, cc):
+            if self.kind == "both":
+                return self.ref.at[pl.ds(2 * zz, 2), cc]
+            return self.ref.at[2 * zz + (x if self.kind == "own" else 1 - x), cc]
+
+        def start(self):
+            mine = self.block(z, c)
+            for dz in (1, -1, 2, -2):
+                send(mine, mine, self.zs + z + dz, self.zs + z, dev(z + dz, x, y, c), valid(dz))
+            send(mine, mine, self.sb + z, self.sb + z, sib)
+
+        def pump(self):
+            for dz in (1, -1, 2, -2, 3, -3):
+                here = self.block(z + dz, c)
+                cond = valid(dz)
+                pl.when(cond)(lambda here=here, dz=dz: got(here, self.zs + z + dz))
+                if dz == 2:
+                    send(here, here, self.fw, self.zs + z + dz, dev(z - 1, x, y, c), z == 1)
+                if dz == -2:
+                    send(here, here, self.fw, self.zs + z + dz, dev(z + 1, x, y, c), z == 2)
+                send(here, here, self.sb + z + dz, self.sb + z + dz, sib, cond)
+
+        def need(self):
+            for zz in range(PLANES):
+                got(self.block(zz, 1 - c), self.sb + zz)
+
+    def weight(ref, rows=None):
+        return ref
+
+    half_of = {}
+
+    def give_half(name, src, ref):
+        i = sems.take()
+        half_of[name] = (ref, i)
+        ref[2 * z + x, c] = src[x]
+        send(src.at[1 - x], ref.at[2 * z + x, c], i, i, xn)
+
+    def have_half(name):
+        ref, i = half_of[name]
+        got(ref.at[2 * z + 1 - x, c], i)
+
+    give_half("q", wq_in, wq)
+    it_qa, it_s, it_qb = Item(wq, "own"), Item(small, "both"), Item(wq, "other")
+    it_o, it_u, it_d = Item(wo, "both"), Item(wu, "both"), Item(wd, "both")
+    it_qa.start()
+    give_half("s", small_in, small)
+    i_om = sems.take()
+    send(omega_in, om2, i_om, i_om, sib)
+    t1, t2 = sems.take(), sems.take(2)
+    mine_rows = xg.at[pl.ds(c * 256, 256)]
+    send(tok, mine_rows, t1, t1, sib, c != x)
+    send(tok, mine_rows, t2 + c, t2 + c, dev(z, 1 - x, y, x))
+    give_half("o", wo_in, wo)
+    give_half("u", wu_in, wu)
+    give_half("d", wd_in, wd)
+    t3 = sems.take()
+    cot_part = cot.at[pl.ds(pl.multiple_of(y * 128, 128), 128)]
+    send(cot_part, cotb, t3, t3, xs_dev, c != x)
+
+    @pl.when(c == x)
+    def _():
+        xg[pl.ds(pl.multiple_of(c * 256, 256), 256)] = tok[...]
+        cotb[...] = cot[pl.ds(pl.multiple_of(y * 128, 128), 128)]
+
+    same = (iota((256, 256), 0) // HEAD) == (iota((256, 256), 1) // HEAD)
+    ones64[...] = jnp.where(same, 1.0, 0.0).astype(BF16)
+    anti[...] = jnp.where(iota((512, 512), 0) + iota((512, 512), 1) == 511, 1.0, 0.0).astype(BF16)
+
+    have_half("s")
+    it_s.start()
+    have_half("q")
+    it_qb.start()
+    it_qa.pump()
+    have_half("o")
+    it_o.start()
+    it_s.pump()
+    it_qb.pump()
+
+    it_s.need()
+    for t in range(8):
+        tile = small[t, 0].astype(F32) + small[t, 1].astype(F32)
+        rows_v[0:8, t * 128 : (t + 1) * 128] = tile[0:8]
+        rows_v[8:16, (7 - t) * 128 : (8 - t) * 128] = tile[8:16]
+        total = tile[16:32] if t == 0 else total + tile[16:32]
+    for r in range(6):
+        rows_v[16:17, r * 128 : (r + 1) * 128] = total[r : r + 1]
+    for r in range(8):
+        rows_v[17:18, r * 128 : (r + 1) * 128] = total[8 + r : 9 + r]
+    level = small[2 * z + c, 0][6:7].astype(F32)
+    wide1 = jnp.where(level > 0.5, 1.0, 0.0)
+    wide2 = jnp.where(level > 1.5, 1.0, 0.0)
+    one_row = jnp.ones((1, 128), F32)
+
+    def mask_row(bi):
+        parts = [one_row if bj == bi else (wide1 if bj // 2 == bi // 2 else wide2) for bj in range(4)]
+        return jnp.concatenate(parts, axis=1)
+
+    masks = [mask_row(bi) for bi in range(4)]
+
+    def coeff_body(h, carry):
+        row = jnp.exp(rows_v[pl.ds(8 + h, 1), :])
+        r0[h] = pltpu.roll(jnp.broadcast_to(row, (128, 1024)), 1, 1, stride=1, stride_axis=0)
+        return carry
+
+    lax.fori_loop(0, 4, coeff_body, 0)
+
+    have_half("u")
+    it_u.start()
+    pl.when(c == x)(lambda: got(xg.at[pl.ds(pl.multiple_of((1 - c) * 256, 256), 256)], t1))
+
+    @pl.when(c != x)
+    def _():
+        got(xg.at[pl.ds(0, 256)], t2)
+        got(xg.at[pl.ds(256, 256)], t2 + 1)
+        got(cotb, t3)
+
+    it_qa.need()
+    it_qb.need()
+
+    def qkv_body(p, carry):
+        cols = pl.ds(pl.multiple_of(p * 256, 256), 256)
+        qkv[p] = (dot(xg[...], wq[:, :, :, cols].reshape(1024, 256)) + rows_v[16:17, cols]).astype(BF16)
+        return carry
+
+    lax.fori_loop(0, 3, qkv_body, 0)
+    got(om2, i_om)
+    om2[...] = om2[...] + omega_in[...]
+
+    def feature_body(t, carry):
+        wide = qkv[t].astype(F32)
+        sums = split_dot(wide * wide, ones64[...])
+        inverse = lax.rsqrt(sums * (1.0 / HEAD) + UNIT_EPS)
+        units = wide * inverse
+        logits = SCALE * split_dot(units, om2[...]) - 0.5 * SCALE * SCALE * (sums * inverse * inverse)
+        value = jnp.exp(logits) * M ** (-0.5)
+        ex[t] = value
+        unit[t] = units
+        inv[t] = inverse
+        phi[t] = value.astype(BF16)
+        return carry
+
+    lax.fori_loop(0, 2, feature_body, 0)
+    have_half("d")
+    it_d.start()
+    it_o.pump()
+
+    lane_head = iota((1, 128), 1) // HEAD
+    num[...] = jnp.zeros_like(num)
+    den[...] = jnp.zeros_like(den)
+
+    def head_cols(h):
+        return pl.ds(pl.multiple_of((h // 2) * 128, 128), 128), (lane_head == h % 2)
+
+    def head_body(h, carry):
+        cols, mine = head_cols(h)
+        keep = jnp.where(mine, 1.0, 0.0).astype(BF16)
+        scores = dot(phi[0, :, cols] * keep, phi[1, :, cols], NT)
+        for b in range(4):
+            coefficient = r0[h, :, 512 - 128 * b : 1024 - 128 * b] * masks[b]
+            pp[h, b * 128 : (b + 1) * 128] = (scores[b * 128 : (b + 1) * 128] * coefficient).astype(BF16)
+        right = jnp.concatenate([qkv[2, :, cols] * keep, jnp.broadcast_to(keep, (512, 128))], axis=1)
+        both = dot(pp[h], right)
+        num[:, cols] += both[:, :128]
+        den[:, cols] += both[:, 128:]
+        return carry
+
+    lax.fori_loop(0, 4, head_body, 0)
+    quo[...] = num[...] / den[...]
+    att[...] = quo[...].astype(BF16)
+
+    class Scatter:
+        def __init__(self, ref):
+            self.ref, self.base = ref, sems.take(12)
+
+        def part(self, n):
+            cols = pl.ds(pl.multiple_of(n * 256, 256), 256)
+            for slot in range(3):
+                i = self.base + slot * 4 + n
+                rc(pb.at[plane_block[slot], :, cols], self.ref.at[slot, :, cols], i, i, plane[slot]).start()
+
+        def total(self):
+            for slot in range(3):
+                for n in range(4):
+                    got(self.ref.at[slot, :, n * 256 : (n + 1) * 256], self.base + slot * 4 + n)
+            value = pb[own_block].astype(F32)
+            for slot in range(3):
+                value = value + self.ref[slot].astype(F32)
+            return value
+
+        def sent(self):
+            for slot in range(3):
+                for n in range(4):
+                    i = self.base + slot * 4 + n
+                    src = pb.at[plane_block[slot], :, n * 256 : (n + 1) * 256]
+                    rc(src, src, i, i, plane[slot]).wait_send()
+
+    class Gather:
+        def __init__(self, ref):
+            self.ref, self.base = ref, sems.take(3)
+
+        def start(self):
+            mine = self.ref.at[own_block]
+            for slot in range(3):
+                send(mine, mine, self.base + slot, self.base + slot, plane[slot])
+
+        def need(self):
+            for slot in range(3):
+                got(self.ref.at[plane_block[slot]], self.base + slot)
+
+    def scatter(ref, part):
+        s = Scatter(ref)
+
+        def body(n, carry):
+            cols = pl.ds(pl.multiple_of(n * 256, 256), 256)
+            pb[:, :, cols] = part(n).astype(BF16).reshape(4, 128, 256)
+            s.part(n)
+            return carry
+
+        lax.fori_loop(0, 4, body, 0)
+        return s
+
+    it_o.need()
+    sc_z = scatter(rb_z, lambda n: dot(att[...], wo[pl.ds(2 * n, 2)].reshape(256, 256), NT))
+    it_u.pump()
+    it_u.need()
+
+    def norm(values):
+        centred = values - jnp.mean(values, axis=-1, keepdims=True)
+        inverse = lax.rsqrt(jnp.mean(centred * centred, axis=-1, keepdims=True) + EPSILON)
+        return centred * inverse, inverse
+
+    own_rows = pl.ds(pl.multiple_of(own_block * 128, 128), 128)
+    residual = sc_z.total() + xg[own_rows].astype(F32) + rows_v[2:3, :]
+    normed, inverse = norm(residual)
+    first = normed * rows_v[0:1, :] + rows_v[3:4, :]
+    fst[...] = first
+    n1[...] = normed
+    i1[...] = jnp.broadcast_to(inverse, (128, 128))
+    fb[own_block] = first.astype(BF16)
+    g_first = Gather(fb)
+    g_first.start()
+    sc_z.sent()
+    g_first.need()
+
+    def hidden_body(n, carry):
+        cols = pl.ds(pl.multiple_of(n * 256, 256), 256)
+        pre = dot(fb[...].reshape(512, 1024), wu[:, :, :, cols].reshape(1024, 256)) + rows_v[17:18, cols]
+        cdf = 0.5 * (1.0 + lax.erf(pre * 0.7071067811865476))
+        hid[:, cols] = (pre * cdf).astype(BF16)
+        dgel[:, cols] = cdf + pre * (0.3989422804014327 * jnp.exp(-0.5 * pre * pre))
+        return carry
+
+    lax.fori_loop(0, 4, hidden_body, 0)
+    it_d.pump()
+    it_d.need()
+    sc_f = scatter(rb_f, lambda n: dot(hid[...], wd[pl.ds(2 * n, 2)].reshape(256, 1024), NT))
+    second = fst[...] + sc_f.total() + rows_v[4:5, :]
+    normed2, inverse2 = norm(second)
+    mix_s[...] = (normed2 * rows_v[1:2, :] + rows_v[5:6, :]).astype(BF16)
+
+    def norm_back(upstream, normed, inverse, gain):
+        scaled = upstream * gain
+        mean = jnp.mean(scaled, axis=-1, keepdims=True)
+        slope = jnp.mean(scaled * normed, axis=-1, keepdims=True)
+        return inverse * (scaled - mean - normed * slope)
+
+    def down(values):
+        return jnp.sum(values, axis=0, keepdims=True)
+
+    upstream = cotb[...].astype(F32)
+    sd[1:2, :] = down(upstream * normed2)
+    sd[5:6, :] = down(upstream)
+    err = norm_back(upstream, normed2, inverse2, rows_v[1:2, :])
+    efb[own_block] = err.astype(BF16)
+    sd[4:5, :] = down(efb[own_block].astype(F32))
+    g_ef = Gather(efb)
+    g_ef.start()
+    dr[...] = err
+    sc_f.sent()
+
+    i_mix, i_gt = sems.take(2), sems.take(2)
+
+    def to_owner(src, dst, i):
+        rows = pl.ds(pl.multiple_of(y * 128, 128), 128)
+        home = c == x
+
+        @pl.when(home)
+        def _():
+            dst[rows] = src[...]
+
+        send(src, dst.at[rows], i + 1, i + 1, yn, home)
+        away = jnp.logical_not(home)
+        send(src, dst.at[rows], i, i + y, xs_dev, away)
+        send(src, dst.at[rows], i + 1, i + y, ds_dev, away)
+
+    def from_owner(dst, i):
+        for half in range(2):
+            part = dst.at[half * 128 : (half + 1) * 128]
+
+            @pl.when(jnp.logical_and(c == x, y != half))
+            def _(part=part):
+                got(part, i + 1)
+
+            @pl.when(c != x)
+            def _(part=part, half=half):
+                got(part, i + half)
+
+    to_owner(mix_s, mixed_o, i_mix)
+    g_ef.need()
+
+    class Grad:
+        def __init__(self, g, r1, t, rz, cb, xr):
+            self.g, self.r1, self.t, self.rz, self.cb, self.xr = g, r1, t, rz, cb, xr
+            self.d, self.z, self.k, self.x = sems.take(4), sems.take(PLANES), sems.take(), sems.take()
+
+        def make(self, part):
+            def body(m, carry):
+                part(m)
+                i = self.d + m
+                rc(self.g.at[m, :, 1 - c], self.r1.at[m], i, i, sib).start()
+                return carry
+
+            lax.fori_loop(0, PLANES, body, 0)
+
+            def done():
+                for m in range(PLANES):
+                    src = self.g.at[m, :, 1 - c]
+                    rc(src, src, self.d + m, self.d + m, sib).wait_send()
+
+            pending.append(done)
+
+        def pair(self):
+            def body(m, carry):
+                got(self.r1.at[m], self.d + m)
+                self.t[m] = (self.g[m, :, c].astype(F32) + self.r1[m].astype(F32)).astype(BF16)
+                return carry
+
+            lax.fori_loop(0, PLANES, body, 0)
+            send(self.t.at[PLANES - 1], self.cb, self.k, self.k, dev(1, x, y, c), z == 0)
+            send(self.t.at[0], self.cb, self.k, self.k, dev(2, x, y, c), z == 3)
+            for dz in (1, -1):
+                send(self.t.at[z + dz], self.rz.at[z], self.z + z + dz, self.z + z, dev(z + dz, x, y, c), valid(dz))
+            for dz, at in ((2, 0), (-2, 3)):
+                send(self.t.at[z + dz], self.rz.at[z], self.z + z + dz, self.z + z, dev(z + dz, x, y, c), z == at)
+
+        def relay(self):
+            for dz, at in ((2, 1), (-2, 2)):
+                @pl.when(z == at)
+                def _(dz=dz):
+                    got(self.cb, self.k)
+                    self.t[z + dz] = (self.t[z + dz].astype(F32) + self.cb[...].astype(F32)).astype(BF16)
+
+                send(self.t.at[z + dz], self.rz.at[z], self.z + z + dz, self.z + z, dev(z + dz, x, y, c), z == at)
+
+        def finish(self):
+            width = self.t.shape[-1]
+            acc = fs.at[:, :, 0:width]
+            acc[...] = self.t[z].astype(F32)
+            for dz in (1, -1, 2, -2):
+                @pl.when(valid(dz))
+                def _(dz=dz):
+                    got(self.rz.at[z + dz], self.z + z + dz)
+                    acc[...] += self.rz[z + dz].astype(F32)
+            keep = xs.at[self.slot, :, 0:width]
+            keep[...] = fs[1 - x, :, 0:width].astype(BF16)
+            send(keep, self.xr, self.x, self.x, xn)
+
+        def columns(self, out, half, parts, value):
+            width = self.t.shape[-1]
+            step = width // parts
+            for p in range(parts):
+                at = pl.multiple_of(p * 2 * step + half * step, 128)
+                out[:, pl.ds(at, step)] = value[:, p * step : (p + 1) * step]
+
+        def write_own(self, out, parts=1):
+            width = self.t.shape[-1]
+            self.columns(out, x, parts, fs[x, :, 0:width])
+
+        def write_other(self, out, parts=1):
+            got(self.xr, self.x)
+            self.columns(out, 1 - x, parts, self.xr[...].astype(F32))
+
+    gr_d = Grad(g_d, r1_d, t_d, rz_d, cb_d, xr_d)
+    gr_u = Grad(g_u, r1_u, t_u, rz_u, cb_u, xr_u)
+    gr_o = Grad(g_o, r1_o, t_o, rz_o, cb_o, xr_o)
+    gr_q = Grad(g_q, r1_q, t_q, rz_q, cb_q, xr_q)
+    for slot, gr in enumerate((gr_d, gr_u, gr_o, gr_q)):
+        gr.slot = slot
+
+    def d_cols(ref, m):
+        return ref[:, :, pl.ds(pl.multiple_of(m * 256, 256), 256)].reshape(512, 256)
+
+    def make_down(m):
+        g_d[m] = dot(d_cols(efb, m), hid[...], TN).astype(BF16).reshape(2, 2, 64, 1024)
+
+    gr_d.make(make_down)
+
+    def du_body(n, carry):
+        cols = pl.ds(pl.multiple_of(n * 256, 256), 256)
+        dact = dot(efb[...].reshape(512, 1024), wd[:, :, :, cols].reshape(1024, 256))
+        du = (dact * dgel[:, cols]).astype(BF16)
+        dub[:, cols] = du
+        st[0:1, cols] = down(du.astype(F32))
+        return carry
+
+    lax.fori_loop(0, 4, du_body, 0)
+    sc_d = scatter(rb_d, lambda n: dot(dub[...], wu[pl.ds(2 * n, 2)].reshape(256, 1024), NT))
+    gr_d.pair()
+
+    def make_up(m):
+        g_u[m] = dot(d_cols(fb, m), dub[...], TN).astype(BF16).reshape(2, 2, 64, 1024)
+
+    gr_u.make(make_up)
+    gr_u.pair()
+    gr_d.relay()
+    dfirst = dr[...] + sc_d.total()
+    sd[0:1, :] = down(dfirst * n1[...])
+    sd[3:4, :] = down(dfirst)
+    back = norm_back(dfirst, n1[...], i1[:, 0:1], rows_v[0:1, :])
+    dr[...] = back
+    dzb[own_block] = back.astype(BF16)
+    sd[2:3, :] = down(dzb[own_block].astype(F32))
+    g_dz = Gather(dzb)
+    g_dz.start()
+    sc_d.sent()
+
+    class Small:
+        def __init__(self, ref, recv):
+            self.ref, self.recv, self.base = ref, recv, sems.take(7)
+
+        def swap(self, device, i):
+            send(self.ref.at[self.at], self.recv.at[i], self.base + i, self.base + i, device)
+
+        def add(self, i):
+            got(self.recv.at[i], self.base + i)
+
+    def small_sum(now, recv, base, device, count):
+        pass
+
+    i_sd = sems.take(3)
+    sd[6:8, :] = jnp.zeros((2, 1024), F32)
+    for k, device in enumerate(plane):
+        send(sd, sd_r.at[k], i_sd + k, i_sd + k, device)
+    g_dz.need()
+
+    dattn = dot(dzb[...].reshape(512, 1024), wo[...].reshape(1024, 256))
+
+    def make_out(m):
+        g_o[m] = dot(d_cols(dzb, m), att[...], TN).astype(BF16).reshape(2, 2, 64, 256)
+
+    gr_o.make(make_out)
+    recip = 1.0 / den[...]
+    dn[...] = (dattn * recip).astype(BF16)
+    dsum = split_dot(dattn * quo[...], ones64[...])
+    dd[...] = ((-dsum * recip).astype(BF16).astype(F32) * (1.0 / HEAD)).astype(BF16)
+    gr_o.pair()
+    gr_u.relay()
+    dph[...] = jnp.zeros_like(dph)
+    dvv[...] = jnp.zeros_like(dvv)
+
+    def head_back(h, carry):
+        cols, mine = head_cols(h)
+        keep = jnp.where(mine, 1.0, 0.0).astype(BF16)
+        dnum = dn[:, cols] * keep
+        left = jnp.concatenate([dnum, dd[:, cols] * keep], axis=1)
+        right = jnp.concatenate([qkv[2, :, cols], jnp.ones((512, 128), BF16)], axis=1)
+        grad_p = dot(left, right, NT)
+        for b in range(4):
+            rows = slice(b * 128, (b + 1) * 128)
+            coefficient = r0[h, :, 512 - 128 * b : 1024 - 128 * b] * masks[b]
+            part = grad_p[rows]
+            ds_[rows] = (part * coefficient).astype(BF16)
+            gg[rows] = (part * pp[h, rows].astype(F32)).astype(BF16)
+        dvv[:, cols] += dot(pp[h], dnum, TN)
+        dph[0, :, cols] += dot(ds_[...], phi[1, :, cols] * keep)
+        dph[1, :, cols] += dot(ds_[...], phi[0, :, cols] * keep, TN)
+        flipped = dot(anti[...], gg[...])
+        sums = jnp.zeros((1, 1024), F32)
+        for b in range(4):
+            wide = jnp.concatenate([flipped[b * 128 : (b + 1) * 128], jnp.zeros((128, 128), F32)], axis=1)
+            line = down(pltpu.roll(wide, 0, 1, stride=1, stride_axis=0))
+            pieces = [line]
+            if b > 0:
+                pieces = [jnp.zeros((1, 128 * b), F32)] + pieces
+            if b < 3:
+                pieces = pieces + [jnp.zeros((1, 384 - 128 * b), F32)]
+            sums = sums + jnp.concatenate(pieces, axis=1)
+        st[pl.ds(2 + h, 1), :] = sums
+        return carry
+
+    lax.fori_loop(0, 4, head_back, 0)
+    gr_o.relay()
+
+    def feature_back_body(t, carry):
+        dlog = (dph[t] * ex[t]).astype(BF16)
+        units = unit[t]
+        dunit = SCALE * dot(dlog, om2[...], NT) - SCALE * SCALE * dot(dlog, ones64[...]) * units
+        mean = split_dot(dunit * units, ones64[...]) * (1.0 / HEAD)
+        dqkv[t] = (inv[t] * (dunit - units * mean)).astype(BF16)
+        return carry
+
+    lax.fori_loop(0, 2, feature_back_body, 0)
+    dqkv[2] = dvv[...].astype(BF16)
+
+    def input_part(n):
+        value = jnp.zeros((512, 256), F32)
+        for p in range(3):
+            value = value + dot(dqkv[p], wq[pl.ds(2 * n, 2), :, :, p * 256 : (p + 1) * 256].reshape(256, 256), NT)
+        return value
+
+    sc_i = scatter(rb_i, input_part)
+
+    def make_qkv(m):
+        left = xg[:, pl.ds(pl.multiple_of(m * 256, 256), 256)]
+        for p in range(3):
+            value = dot(left, dqkv[p], TN).astype(BF16).reshape(2, 2, 64, 256)
+            g_q[m, :, :, :, p * 256 : (p + 1) * 256] = value
+
+    gr_q.make(make_qkv)
+    for p in range(3):
+        st[1:2, p * 256 : (p + 1) * 256] = down(dqkv[p].astype(F32))
+    st[1:2, 768:1024] = jnp.zeros((1, 256), F32)
+    st[6:8, :] = jnp.zeros((2, 1024), F32)
+    gr_q.pair()
+
+    i_c, i_zz, i_h = sems.take(), sems.take(PLANES), sems.take()
+    for k in range(3):
+        got(sd_r.at[k], i_sd + k)
+    st[8:16, :] = sd[...] + sd_r[0] + sd_r[1] + sd_r[2]
+    send(st, st_r.at[0], i_c, i_c, sib)
+    got(st_r.at[0], i_c)
+    st_r[1] = st[...] + st_r[0]
+    for zz in range(PLANES):
+        send(st_r.at[1], st_r.at[2 + z], i_zz + zz, i_zz + z, dev(zz, x, y, c), z != zz)
+
+    gr_d.finish()
+    gr_d.write_own(gd_o)
+    gr_u.finish()
+    gr_u.write_own(gu_o)
+    gr_o.finish()
+    gr_o.write_own(go_o)
+    back = dr[...] + sc_i.total()
+    gt_s[...] = back.astype(BF16)
+    to_owner(gt_s, gt_r, i_gt)
+    sc_i.sent()
+    gr_q.relay()
+    total = st_r[1]
+    for zz in range(PLANES):
+        @pl.when(z != zz)
+        def _(zz=zz):
+            got(st_r.at[2 + zz], i_zz + zz)
+
+        @pl.when(z == zz)
+        def _(zz=zz):
+            st_r[2 + zz] = jnp.zeros((16, 1024), F32)
+        total = total + st_r[2 + zz]
+    tvec_o[x] = total[0:8]
+    dvec_o[...] = total[8:16]
+    send(tvec_o.at[x], tvec_o.at[x], i_h, i_h, xn)
+    gr_d.write_other(gd_o)
+    gr_u.write_other(gu_o)
+    gr_o.write_other(go_o)
+    gr_q.finish()
+    gr_q.write_own(gq_o, 3)
+    from_owner(mixed_o, i_mix)
+    from_owner(gt_r, i_gt)
+    gtok_o[...] = gt_r[...].astype(F32)
+    got(tvec_o.at[1 - x], i_h)
+    gr_q.write_other(gq_o, 3)
+    for done in pending:
+        done()
+
+
+def fast_local(
+    tokens, qkv_weight, qkv_bias, out_weight, norm_gains, row_biases, up_weight, up_bias, down_weight, rpe_bias, omega,
+    bucket, cotangent,
+):
+    dp, feat = lax.axis_index("dp"), lax.axis_index("feat")
+    x = dp % 2
+    shard = dp * 2 + feat
+
+    def halves(weight):
+        return weight.reshape(64, 2, -1).transpose(1, 0, 2)
+
+    wq = qkv_weight.reshape(64, 3, 2, 256).transpose(2, 0, 1, 3).reshape(2, 64, 768)
+    wo, wu, wd = halves(out_weight.T), halves(up_weight), halves(down_weight.T)
+
+    def beside(values, at):
+        blank = jnp.zeros_like(values)
+        return jnp.where(
+            at == 0, jnp.concatenate([values, blank], -1), jnp.concatenate([blank, values], -1)
+        )
+
+    def two(rows):
+        return jnp.broadcast_to(rows, (2,) + rows.shape)
+
+    vectors = beside(jnp.concatenate([norm_gains, row_biases], 0), feat)
+    level = jnp.broadcast_to(bucket.astype(BF16)[:, None], (1, 128))
+    top = two(jnp.concatenate([vectors, level, jnp.zeros((1, 128), BF16)], 0))
+    position = beside(rpe_bias[:, ::-1], 1 - feat).reshape(2, 4, 128)
+    spread = lax.dynamic_update_slice(jnp.zeros((3, 8, 64), BF16), qkv_bias, (0, 0, 4 * shard))
+    spread = spread.reshape(3, 2, 256).transpose(1, 0, 2).reshape(2, 6, 128)
+    spread_up = lax.dynamic_update_slice(jnp.zeros((32, 64), BF16), up_bias, (0, 4 * shard)).reshape(2, 8, 128)
+    small = jnp.concatenate(
+        [top, position, jnp.zeros((2, 4, 128), BF16), spread, jnp.zeros((2, 2, 128), BF16), spread_up], 1
+    )
+    mine = lax.dynamic_slice(omega, (4 * x, 0, 0), (4, 64, 32))
+    both = beside(mine, feat) if False else jnp.where(
+        feat == 0,
+        jnp.concatenate([mine, jnp.zeros_like(mine)], -1),
+        jnp.concatenate([jnp.zeros_like(mine), mine], -1),
+    )
+    blocks = jnp.eye(4, dtype=BF16)[:, None, :, None] * both[:, :, None, :]
+    omega_blocks = blocks.reshape(256, 256)
+
+    def vm(shape, dtype=BF16):
+        return pltpu.VMEM(shape, dtype)
+
+    widths = (768, 256, 1024, 1024)
+    scratch = [vm((8, 2, 64, n)) for n in widths]
+    scratch += [vm((8, 2, 32, 128)), vm((256, 256)), vm((512, 1024)), vm((128, 1024))]
+    scratch += [vm((3, 512, 256)), vm((2, 512, 256))] + [vm((2, 512, 256), F32)] * 3
+    scratch += [vm((4, 128, 1024), F32), vm((4, 512, 512))] + [vm((512, 256), F32)] * 3 + [vm((512, 256))]
+    scratch += [vm((4, 128, 1024))] + [vm((3, 128, 1024))] * 4
+    scratch += [vm((4, 128, 1024)), vm((512, 1024)), vm((512, 1024), F32)]
+    scratch += [vm((4, 128, 1024)), vm((512, 1024)), vm((4, 128, 1024))]
+    scratch += [vm((128, 1024), F32)] * 2 + [vm((128, 128), F32), vm((128, 1024), F32)]
+    scratch += [vm((512, 256))] * 2 + [vm((512, 512))] * 2 + [vm((2, 512, 256), F32), vm((512, 256), F32)]
+    scratch += [vm((3, 512, 256)), vm((512, 512)), vm((256, 256)), vm((24, 1024), F32)]
+    scratch += [vm((4, 2, 2, 64, n)) for n in widths]
+    scratch += [vm((4, 2, 64, n)) for n in widths] * 2
+    scratch += [vm((4, 2, 64, n)) for n in widths] + [vm((2, 64, n)) for n in widths]
+    scratch += [vm((2, 64, 1024), F32), vm((4, 64, 1024))] + [vm((64, n)) for n in widths]
+    scratch += [vm((8, 1024), F32), vm((3, 8, 1024), F32), vm((16, 1024), F32), vm((6, 16, 1024), F32)]
+    scratch += [vm((128, 1024)), vm((16, 128)), vm((128, 1024)), vm((256, 1024))]
+    scratch += [pltpu.SemaphoreType.DMA((320,)), pltpu.SemaphoreType.DMA((320,))]
+
+    def out(shape, dtype=F32):
+        return jax.ShapeDtypeStruct(shape, dtype)
+
+    mixed, gtok, gq, go, gu, gd, dvec, tvec = pl.pallas_call(
+        layer_kernel,
+        out_shape=(
+            out((256, 1024), BF16), out((256, 1024)), out((64, 1536)), out((64, 512)), out((64, 2048)), out((64, 2048)),
+            out((8, 1024)), out((2, 8, 1024)),
+        ),
+        in_specs=[pl.BlockSpec(memory_space=pltpu.VMEM)] * 8,
+        out_specs=(pl.BlockSpec(memory_space=pltpu.VMEM),) * 8,
+        scratch_shapes=scratch,
+        compiler_params=pltpu.CompilerParams(
+            collective_id=0, has_side_effects=True, vmem_limit_bytes=63 * 2**20
+        ),
+        name="layer",
+    )(tokens, cotangent, wq, wo, wu, wd, small, omega_blocks)
+    own = lax.dynamic_slice(dvec, (0, 64 * shard), (8, 64))
+    grad_up_bias = lax.dynamic_slice(tvec[:, 0].reshape(32, 64), (0, 4 * shard), (32, 4))
+    qkv_rows = tvec[:, 1, :768].reshape(2, 3, 4, 64).transpose(1, 0, 2, 3).reshape(3, 8, 64)
+    grad_qkv_bias = lax.dynamic_slice(qkv_rows, (0, 0, 4 * shard), (3, 8, 4))
+    grad_rpe = lax.dynamic_slice(tvec[:, 2:6].reshape(8, 1024), (0, 64 * (15 - shard)), (8, 64))[:, ::-1]
+    return (
+        mixed, gtok, gq.reshape(64, 3, 512), grad_qkv_bias, go.T, own[0:2], own[2:6], gu, grad_up_bias, gd.T, grad_rpe,
+    )
+
+
 def solution(mesh):
+    sizes = (mesh.shape["dp"], mesh.shape["heads"], mesh.shape["feat"])
     return jax.shard_map(
-        local,
+        fast_local if sizes == (2 * PLANES, 2, 2) else local,
         mesh=mesh,
         in_specs=(
             P(("dp", "feat"), None),

time: 1210 us -> 214 us (0.18); the launches traced: 1190 us -> 213 us
  waiting for transfers between devices: 593 us -> 0 us
  Pallas kernels: 0 us -> 190 us
  matrix products: 179 us -> 0 us
  local copies, waits for them, and re-layouts: 188 us -> 21.9 us
  blocking collectives: 160 us -> 0 us
  other arithmetic: 50.4 us -> 0.43 us
  between operations: 16.8 us -> 1.47 us
    reduce_scatter x7 -> x0, waiting for transfers between devices: 258 us -> none  [the longest x1 73.4 us: local(): lax.psum_scatter(grad_down.astype(jnp.bfloat16), ('dp', 'feat'), scatter_...]
    pallas_call x0 -> x1, Pallas kernels: none -> 190 us  [fast_local(): pl.pallas_call(layer_kernel, out_shape=(out((256, 1024), BF16), out((256,...]
    dot_general x128 -> x0, matrix products: 179 us -> none  [the longest x16 32.6 us: visit_back(): jnp.einsum('hij,ihe->jhe', weights, numer_rows, preferred_element_type=jn...]
    unnamed x22 -> x0, waiting for transfers between devices: 152 us -> none
    all_gather x5 -> x0, waiting for transfers between devices: 129 us -> none  [the longest x1 42.2 us: local(): lax.all_gather(down_weight, ('dp', 'feat'), axis=1, tiled=True)]
    all_gather x7 -> x0, blocking collectives: 102 us -> none  [the longest x1 23.2 us: local(): lax.all_gather(qkv_bias, ('dp', 'feat'), axis=2, tiled=True)]
    unnamed x1 -> x0, blocking collectives: 58.4 us -> none
    psum x4 -> x0, waiting for transfers between devices: 52.8 us -> none  [the longest x1 27.2 us: local(): lax.psum(ffn_part.astype(jnp.bfloat16), 'heads').astype(jnp.float32)]
  transfers between devices with their start and end apart: 19 -> 0, of which waited for: 16 -> 0; matrix products, arithmetic and copies ran while one was open for 5% -> 0% of each run, Pallas kernels for 0% -> 0%
where the time goes in v1:
time: 214 us; the launch traced here: 213 us
  Pallas kernels  190 us (89%)
  local copies, waits for them, and re-layouts  21.9 us (10%)
    pallas_call x1, Pallas kernels, fast_local(): pl.pallas_call(layer_kernel, out_shape=(out((256, 1024), BF16), out((256,...  190 us
    unnamed x41, local copies, waits for them, and re-layouts  9.5 us

profile of v1, /device:TPU:0, one launch (start us, length us, event | category | flops | bytes accessed | tf_op | source)
XLA Modules:
  0.0 213.4 jit_solution(6212935149347284560)
XLA Ops:
  1.5 0.7 copy-done.13
  2.3 0.7 copy-done.12
  3.2 0.6 copy-done.11
  3.8 0.1 copy.34
  3.9 0.1 dynamic_update_slice.6
  4.2 0.7 copy-done.14
  4.8 0.1 copy.36
  4.9 0.1 dynamic_update_slice.7
  5.2 2.4 %concatenate.33.small_in = bf16[2,32,128]{2,1,0:T(8,128)(2,1)} concatenate(bf16[2,8,128]{2,1,0:T(8,128)(2,1)S(1)} %broadcast_in_dim.33, bf16[2,4,128]{2,1,0:T(4,128)(2,1)S(1)} %bitcast.48, bf16[2,4,128]{2,1,0:T(4,128)(2,1)S(1)} %broadcast_in_dim.34, bf16[2,6,128]{2,1,0:T(8,128)(2,1)S(1)} %reshape.81, bf16[2,2,128]{2,1,0:T(2,128)(2,1)S(1)} %broadcast_in_dim.36, ...), dimensions={1} | concatenate | bytes 32768 | tf_op jit(solution)/shard_map/concatenate | solution.py:1107
  7.6 0.1 copy.37
  7.8 0.7 copy-done.9
  8.5 0.6 copy.54
  9.1 0.2 broadcast_multiply_fusion
  9.3 0.9 mul.41.omega_in
  10.3 0.2 copy.53
  10.5 0.9 reshape.75.wq_in
  11.4 0.8 bitcast_bitcast_fusion
  12.3 189.7 %layer.1 = (bf16[256,1024]{1,0:T(8,128)(2,1)}, f32[256,1024]{1,0:T(8,128)}, f32[64,1536]{1,0:T(8,128)}, f32[64,512]{1,0:T(8,128)}, f32[64,2048]{1,0:T(8,128)}, /...) custom-call(bf16[256,1024]{1,0:T(8,128)(2,1)} %tok.1, bf16[256,1024]{1,0:T(8,128)(2,1)} %cot.1, ...), custom_call_target="tpu_custom_call" | custom-call | tf_op jit(solution)/shard_map/layer/pallas_call | solution.py:1144
  201.9 0.8 constant_dynamic-slice_fusion.2
  202.7 0.6 slice.16
  203.3 0.6 slice.17
  203.9 0.8 slice_reduce_fusion.1
  204.9 0.7 copy.41
  205.7 0.7 rev.7
  206.5 0.7 copy.42
  207.2 1.8 copy.52
  209.0 0.8 copy.63
  209.8 1.0 copy.64
  210.8 0.7 copy.65
  211.4 0.8 copy.66
  212.2 0.4 copy-done.2
  212.6 0.8 copy.67
  (55 shorter events, 1.4 us)
Async XLA Ops:
  0.6 7.0 %copy-start = (bf16[8,64,32]{1,2,0:T(8,128)(2,1)S(1)}, bf16[8,64,32]{1,2,0:T(8,128)(2,1)}, u32[]{:S(2)}) copy-start(bf16[8,64,32]{1,2,0:T(8,128)(2,1)} %param.23) | copy-start | bytes 98308
  1.5 0.7 copy-start.13
  1.5 0.7 copy-start.15
  2.3 0.7 copy-start.12
  3.1 0.7 copy-start.11
  4.2 0.7 copy-start.14
  7.6 0.8 copy-start.9
  9.3 0.9 copy-start.7
  10.3 1.1 copy-start.6
  10.5 1.0 copy-start.5
  201.9 3.6 %copy-start.10 = (f32[2,8,1024]{2,1,0:T(8,128)S(1)}, f32[2,8,1024]{2,1,0:T(8,128)}, u32[]{:S(2)}) copy-start(f32[2,8,1024]{2,1,0:T(8,128)} %get-tuple-element.22) | copy-start | bytes 196612
  204.8 4.2 %copy-start.4 = (bf16[256,1024]{1,0:T(8,128)(2,1)S(1)}, bf16[256,1024]{1,0:T(8,128)(2,1)}, u32[]{:S(2)}) copy-start(bf16[256,1024]{1,0:T(8,128)(2,1)} %get-tuple-element.62) | copy-start | bytes 1572868
  204.9 4.9 %copy-start.1 = (f32[256,1024]{1,0:T(8,128)S(1)}, f32[256,1024]{1,0:T(8,128)}, u32[]{:S(2)}) copy-start(f32[256,1024]{1,0:T(8,128)} %get-tuple-element.63) | copy-start | bytes 3145732
  209.8 1.0 copy-start.8
  209.8 1.7 copy-start.3
  211.4 1.2 copy-start.2

commit v2 on v1

--- a/solution.py
+++ b/solution.py
@@ -436,8 +436,10 @@
 
 
 def layer_kernel(
-    tok, cot, wq_in, wo_in, wu_in, wd_in, small_in, omega_in,
-    mixed_o, gtok_o, gq_o, go_o, gu_o, gd_o, dvec_o, tvec_o,
+    tok, wq_h, qb_h, wo_h, gain_h, bias_h, wu_h, ub_h, wd_h, rpe_h, om_h, bk_h, cot,
+    mixed_h, gtok_h, gq_h, gqb_h, go_h, ggain_h, gbias_h, gu_h, gub_h, gd_h, grpe_h,
+    qb_v, gain_v, bias_v, ub_v, rpe_v, om_v, bk_v, small_s, om_s,
+    mixed_o, gtok_o, gq_o, gqb_o, go_o, ggain_o, gbias_o, gu_o, gub_o, gd_o, grpe_o, tvec_o,
     wq, wo, wu, wd, small, om2, xg, cotb,
     qkv, phi, ex, unit, inv, r0, pp, num, den, quo, att,
     pb, rb_z, rb_f, rb_d, rb_i, fb, hid, dgel, efb, dub, dzb,
@@ -445,13 +447,40 @@
     dn, dd, ds_, gg, dph, dvv, dqkv, anti, ones64, rows_v,
     g_q, g_o, g_u, g_d, r1_q, r1_o, r1_u, r1_d, t_q, t_o, t_u, t_d,
     rz_q, rz_o, rz_u, rz_d, cb_q, cb_o, cb_u, cb_d, fs, xs, xr_q, xr_o, xr_u, xr_d,
-    sd, sd_r, st, st_r, mix_s, mix_r, gt_s, gt_r,
-    ss, rs,
+    sd, sd_r, st, st_r, mix_s, gt_s, gt_r,
+    ss, rs, ls,
 ):
     dp, y, c = lax.axis_index("dp"), lax.axis_index("heads"), lax.axis_index("feat")
     z, x = dp // 2, dp % 2
-    sems = Sems()
+    shard = 2 * dp + c
+    sems, locals_ = Sems(), Sems()
     pending = []
+
+    def bring(src, dst, cond=None):
+        copy = pltpu.make_async_copy(src, dst, ls.at[locals_.take()])
+        if cond is None:
+            copy.start()
+            return copy.wait
+        pl.when(cond)(copy.start)
+        return lambda: pl.when(cond)(copy.wait)
+
+    home = c == x
+
+    def half_cols(half, width):
+        return pl.ds(pl.multiple_of(half * width, width), width)
+
+    in_q = bring(wq_h.at[:, :, half_cols(x, 256)], wq.at[:, 2 * z + x, c])
+    in_small = [
+        bring(src, dst)
+        for src, dst in (
+            (gain_h, gain_v), (bias_h, bias_v), (rpe_h, rpe_v), (qb_h, qb_v), (ub_h, ub_v), (om_h, om_v), (bk_h, bk_v),
+        )
+    ]
+    in_o = bring(wo_h.at[:, half_cols(x, 256)], wo.at[2 * z + x, c])
+    in_tok = bring(tok, xg.at[pl.ds(pl.multiple_of(c * 256, 256), 256)], home)
+    in_cot = bring(cot.at[pl.ds(pl.multiple_of(y * 128, 128), 128)], cotb, home)
+    in_u = bring(wu_h.at[:, half_cols(x, 1024)], wu.at[2 * z + x, c])
+    in_d = bring(wd_h.at[:, half_cols(x, 1024)], wd.at[2 * z + x, c])
 
     def dev(zz, xx, yy, cc):
         return {"dp": zz * 2 + xx, "heads": yy, "feat": cc}
@@ -504,7 +533,7 @@
         def block(self, zz, cc):
             if self.kind == "both":
                 return self.ref.at[pl.ds(2 * zz, 2), cc]
-            return self.ref.at[2 * zz + (x if self.kind == "own" else 1 - x), cc]
+            return self.ref.at[:, 2 * zz + (x if self.kind == "own" else 1 - x), cc]
 
         def start(self):
             mine = self.block(z, c)
@@ -527,43 +556,72 @@
             for zz in range(PLANES):
                 got(self.block(zz, 1 - c), self.sb + zz)
 
-    def weight(ref, rows=None):
-        return ref
-
     half_of = {}
+
+    def place(ref, xx):
+        return ref.at[:, 2 * z + xx, c] if len(ref.shape) == 5 else ref.at[2 * z + xx, c]
 
     def give_half(name, src, ref):
         i = sems.take()
         half_of[name] = (ref, i)
-        ref[2 * z + x, c] = src[x]
-        send(src.at[1 - x], ref.at[2 * z + x, c], i, i, xn)
+        send(src, place(ref, x), i, i, xn)
 
     def have_half(name):
         ref, i = half_of[name]
-        got(ref.at[2 * z + 1 - x, c], i)
-
-    give_half("q", wq_in, wq)
+        got(place(ref, 1 - x), i)
+
+    give_half("q", wq_h.at[:, :, half_cols(1 - x, 256)], wq)
+    in_q()
     it_qa, it_s, it_qb = Item(wq, "own"), Item(small, "both"), Item(wq, "other")
     it_o, it_u, it_d = Item(wo, "both"), Item(wu, "both"), Item(wd, "both")
     it_qa.start()
-    give_half("s", small_in, small)
+
+    for done in in_small:
+        done()
+
+    def pick(shape, hit):
+        return jnp.where(hit(iota(shape, 0), iota(shape, 1)), 1.0, 0.0)
+
+    vec_sel = pick((64, 128), lambda k, l: l == c * 64 + k).astype(BF16)
+    rpe_sel = pick((64, 128), lambda k, l: l == (1 - c) * 64 + 63 - k).astype(BF16)
+    bias_sel = [pick((4, 128), lambda k, l, par=par: l == par * 64 + 4 * shard + k).astype(BF16) for par in range(2)]
+    small_s[...] = jnp.zeros_like(small_s)
+    rpe_rows = dot(rpe_v[...], rpe_sel)
+    level = jnp.full((1, 128), bk_v[0].astype(F32))
+    top = jnp.concatenate(
+        [dot(gain_v[...], vec_sel), dot(bias_v[...], vec_sel), level, jnp.zeros((1, 128), F32)], axis=0
+    )
+
+    def spread(values):
+        rows = values.shape[1]
+        even = (iota((rows, 1), 0) % 2) == 0
+        wide = jnp.where(even, dot(values, bias_sel[0], TN), dot(values, bias_sel[1], TN))
+        return dot(pick((rows // 2, rows), lambda k, l: l // 2 == k).astype(BF16), wide.astype(BF16))
+
+    up_rows = spread(ub_v[...])
+    qkv_rows = [spread(qb_v[p]) for p in range(3)]
+    for half in range(2):
+        mine = [rows[2 * half : 2 * half + 2] for rows in qkv_rows] + [jnp.zeros((2, 128), F32)]
+        position = jnp.concatenate([rpe_rows[4 * half : 4 * half + 4], jnp.zeros((4, 128), F32)], axis=0)
+        small_s[half] = jnp.concatenate(
+            [top, position] + mine + [up_rows[8 * half : 8 * half + 8]], axis=0
+        ).astype(BF16)
+    small[2 * z + x, c] = small_s[x]
+    give_half("s", small_s.at[1 - x], small)
+    for h in range(4):
+        sel = pick((32, 256), lambda k, l: l == h * 64 + c * 32 + k).astype(BF16)
+        om_s[h * 64 : (h + 1) * 64] = dot(om_v[4 * x + h], sel, TN).astype(BF16)
     i_om = sems.take()
-    send(omega_in, om2, i_om, i_om, sib)
+    send(om_s, om2, i_om, i_om, sib)
     t1, t2 = sems.take(), sems.take(2)
-    mine_rows = xg.at[pl.ds(c * 256, 256)]
+    mine_rows = xg.at[pl.ds(pl.multiple_of(c * 256, 256), 256)]
     send(tok, mine_rows, t1, t1, sib, c != x)
     send(tok, mine_rows, t2 + c, t2 + c, dev(z, 1 - x, y, x))
-    give_half("o", wo_in, wo)
-    give_half("u", wu_in, wu)
-    give_half("d", wd_in, wd)
+    give_half("o", wo_h.at[:, half_cols(1 - x, 256)], wo)
+    give_half("u", wu_h.at[:, half_cols(1 - x, 1024)], wu)
+    give_half("d", wd_h.at[:, half_cols(1 - x, 1024)], wd)
     t3 = sems.take()
-    cot_part = cot.at[pl.ds(pl.multiple_of(y * 128, 128), 128)]
-    send(cot_part, cotb, t3, t3, xs_dev, c != x)
-
-    @pl.when(c == x)
-    def _():
-        xg[pl.ds(pl.multiple_of(c * 256, 256), 256)] = tok[...]
-        cotb[...] = cot[pl.ds(pl.multiple_of(y * 128, 128), 128)]
+    send(cot.at[pl.ds(pl.multiple_of(y * 128, 128), 128)], cotb, t3, t3, xs_dev, c != x)
 
     same = (iota((256, 256), 0) // HEAD) == (iota((256, 256), 1) // HEAD)
     ones64[...] = jnp.where(same, 1.0, 0.0).astype(BF16)
@@ -575,6 +633,7 @@
     it_qb.start()
     it_qa.pump()
     have_half("o")
+    in_o()
     it_o.start()
     it_s.pump()
     it_qb.pump()
@@ -608,7 +667,10 @@
     lax.fori_loop(0, 4, coeff_body, 0)
 
     have_half("u")
+    in_u()
     it_u.start()
+    in_tok()
+    in_cot()
     pl.when(c == x)(lambda: got(xg.at[pl.ds(pl.multiple_of((1 - c) * 256, 256), 256)], t1))
 
     @pl.when(c != x)
@@ -622,12 +684,12 @@
 
     def qkv_body(p, carry):
         cols = pl.ds(pl.multiple_of(p * 256, 256), 256)
-        qkv[p] = (dot(xg[...], wq[:, :, :, cols].reshape(1024, 256)) + rows_v[16:17, cols]).astype(BF16)
+        qkv[p] = (dot(xg[...], wq[p].reshape(1024, 256)) + rows_v[16:17, cols]).astype(BF16)
         return carry
 
     lax.fori_loop(0, 3, qkv_body, 0)
     got(om2, i_om)
-    om2[...] = om2[...] + omega_in[...]
+    om2[...] = om2[...] + om_s[...]
 
     def feature_body(t, carry):
         wide = qkv[t].astype(F32)
@@ -644,6 +706,7 @@
 
     lax.fori_loop(0, 2, feature_body, 0)
     have_half("d")
+    in_d()
     it_d.start()
     it_o.pump()
 
@@ -868,20 +931,20 @@
             keep[...] = fs[1 - x, :, 0:width].astype(BF16)
             send(keep, self.xr, self.x, self.x, xn)
 
-        def columns(self, out, half, parts, value):
+        def columns(self, out, half, value):
+            if len(out.shape) == 3:
+                for p in range(3):
+                    out[p, :, half_cols(half, 256)] = value[:, p * 256 : (p + 1) * 256]
+            else:
+                out[:, half_cols(half, self.t.shape[-1])] = value
+
+        def write_own(self, out):
             width = self.t.shape[-1]
-            step = width // parts
-            for p in range(parts):
-                at = pl.multiple_of(p * 2 * step + half * step, 128)
-                out[:, pl.ds(at, step)] = value[:, p * step : (p + 1) * step]
-
-        def write_own(self, out, parts=1):
-            width = self.t.shape[-1]
-            self.columns(out, x, parts, fs[x, :, 0:width])
-
-        def write_other(self, out, parts=1):
+            self.columns(out, x, fs[x, :, 0:width])
+
+        def write_other(self, out):
             got(self.xr, self.x)
-            self.columns(out, 1 - x, parts, self.xr[...].astype(F32))
+            self.columns(out, 1 - x, self.xr[...].astype(F32))
 
     gr_d = Grad(g_d, r1_d, t_d, rz_d, cb_d, xr_d)
     gr_u = Grad(g_u, r1_u, t_u, rz_u, cb_u, xr_u)
@@ -926,19 +989,6 @@
     g_dz = Gather(dzb)
     g_dz.start()
     sc_d.sent()
-
-    class Small:
-        def __init__(self, ref, recv):
-            self.ref, self.recv, self.base = ref, recv, sems.take(7)
-
-        def swap(self, device, i):
-            send(self.ref.at[self.at], self.recv.at[i], self.base + i, self.base + i, device)
-
-        def add(self, i):
-            got(self.recv.at[i], self.base + i)
-
-    def small_sum(now, recv, base, device, count):
-        pass
 
     i_sd = sems.take(3)
     sd[6:8, :] = jnp.zeros((2, 1024), F32)
@@ -1008,7 +1058,7 @@
     def input_part(n):
         value = jnp.zeros((512, 256), F32)
         for p in range(3):
-            value = value + dot(dqkv[p], wq[pl.ds(2 * n, 2), :, :, p * 256 : (p + 1) * 256].reshape(256, 256), NT)
+            value = value + dot(dqkv[p], wq[p, pl.ds(2 * n, 2)].reshape(256, 256), NT)
         return value
 
     sc_i = scatter(rb_i, input_part)
@@ -1042,6 +1092,11 @@
     gr_u.write_own(gu_o)
     gr_o.finish()
     gr_o.write_own(go_o)
+    outs = []
+    from_owner(mixed_o, i_mix)
+    outs.append(bring(mixed_o, mixed_h))
+    gr_d.write_other(gd_o)
+    outs.append(bring(gd_o, gd_h))
     back = dr[...] + sc_i.total()
     gt_s[...] = back.astype(BF16)
     to_owner(gt_s, gt_r, i_gt)
@@ -1057,70 +1112,86 @@
         def _(zz=zz):
             st_r[2 + zz] = jnp.zeros((16, 1024), F32)
         total = total + st_r[2 + zz]
+    st_r[0] = total
     tvec_o[x] = total[0:8]
-    dvec_o[...] = total[8:16]
     send(tvec_o.at[x], tvec_o.at[x], i_h, i_h, xn)
-    gr_d.write_other(gd_o)
     gr_u.write_other(gu_o)
+    outs.append(bring(gu_o, gu_h))
     gr_o.write_other(go_o)
-    gr_q.finish()
-    gr_q.write_own(gq_o, 3)
-    from_owner(mixed_o, i_mix)
+    outs.append(bring(go_o, go_h))
+
+    def exact(left, right):
+        return lax.dot_general(left, right, NN, precision=lax.Precision.HIGHEST, preferred_element_type=F32)
+
+    own = exact(
+        st_r[0, 8:16, pl.ds(pl.multiple_of(dp * 128, 128), 128)], pick((128, 64), lambda k, l: k == c * 64 + l)
+    )
+    ggain_o[...] = own[0:2]
+    gbias_o[...] = own[2:6]
+    outs.append(bring(ggain_o, ggain_h))
+    outs.append(bring(gbias_o, gbias_h))
+    got(tvec_o.at[1 - x], i_h)
+    tile = pl.ds(pl.multiple_of((7 - dp) * 128, 128), 128)
+    lines = jnp.concatenate([tvec_o[0, 2:6, tile], tvec_o[1, 2:6, tile]], axis=0)
+    grpe_o[...] = exact(lines, pick((128, 64), lambda k, l: k == (1 - c) * 64 + 63 - l))
+    outs.append(bring(grpe_o, grpe_h))
+    lines = [
+        tvec_o[half, 1:2, p * 256 + t * 128 : p * 256 + (t + 1) * 128]
+        for p in range(3) for half in range(2) for t in range(2)
+    ] + [tvec_o[half, 0:1, t * 128 : (t + 1) * 128] for half in range(2) for t in range(8)]
+    lines = jnp.concatenate(lines + [jnp.zeros((4, 128), F32)], axis=0)
+    found = jnp.zeros((4, 56), F32)
+    for par in range(2):
+        hit = pick((4, 128), lambda k, l: l == par * 64 + 4 * shard + k)
+        values = lax.dot_general(hit, lines, NT, precision=lax.Precision.HIGHEST, preferred_element_type=F32)
+        found = found + exact(values, pick((32, 56), lambda k, l: (l // 2 == k) & (l % 2 == par)))
+    for p in range(3):
+        gqb_o[p] = found[:, 8 * p : 8 * p + 8]
+    gub_o[...] = found[:, 24:56]
+    outs.append(bring(gqb_o, gqb_h))
+    outs.append(bring(gub_o, gub_h))
     from_owner(gt_r, i_gt)
     gtok_o[...] = gt_r[...].astype(F32)
-    got(tvec_o.at[1 - x], i_h)
-    gr_q.write_other(gq_o, 3)
-    for done in pending:
+    outs.append(bring(gtok_o, gtok_h))
+    gr_q.finish()
+    gr_q.write_own(gq_o)
+    gr_q.write_other(gq_o)
+    outs.append(bring(gq_o, gq_h))
+    for done in pending + outs:
         done()
+
+
+def copy_kernel(*refs):
+    count = len(refs) // 3
+    sem = refs[-1]
+    ins = [pltpu.make_async_copy(refs[i], refs[2 * count + i], sem.at[0, i]) for i in range(count)]
+    outs = [pltpu.make_async_copy(refs[2 * count + i], refs[count + i], sem.at[1, i]) for i in range(count)]
+    for copy in ins:
+        copy.start()
+    for one, two in zip(ins, outs):
+        one.wait()
+        two.start()
+    for copy in outs:
+        copy.wait()
 
 
 def fast_local(
     tokens, qkv_weight, qkv_bias, out_weight, norm_gains, row_biases, up_weight, up_bias, down_weight, rpe_bias, omega,
     bucket, cotangent,
 ):
-    dp, feat = lax.axis_index("dp"), lax.axis_index("feat")
-    x = dp % 2
-    shard = dp * 2 + feat
-
-    def halves(weight):
-        return weight.reshape(64, 2, -1).transpose(1, 0, 2)
-
-    wq = qkv_weight.reshape(64, 3, 2, 256).transpose(2, 0, 1, 3).reshape(2, 64, 768)
-    wo, wu, wd = halves(out_weight.T), halves(up_weight), halves(down_weight.T)
-
-    def beside(values, at):
-        blank = jnp.zeros_like(values)
-        return jnp.where(
-            at == 0, jnp.concatenate([values, blank], -1), jnp.concatenate([blank, values], -1)
-        )
-
-    def two(rows):
-        return jnp.broadcast_to(rows, (2,) + rows.shape)
-
-    vectors = beside(jnp.concatenate([norm_gains, row_biases], 0), feat)
-    level = jnp.broadcast_to(bucket.astype(BF16)[:, None], (1, 128))
-    top = two(jnp.concatenate([vectors, level, jnp.zeros((1, 128), BF16)], 0))
-    position = beside(rpe_bias[:, ::-1], 1 - feat).reshape(2, 4, 128)
-    spread = lax.dynamic_update_slice(jnp.zeros((3, 8, 64), BF16), qkv_bias, (0, 0, 4 * shard))
-    spread = spread.reshape(3, 2, 256).transpose(1, 0, 2).reshape(2, 6, 128)
-    spread_up = lax.dynamic_update_slice(jnp.zeros((32, 64), BF16), up_bias, (0, 4 * shard)).reshape(2, 8, 128)
-    small = jnp.concatenate(
-        [top, position, jnp.zeros((2, 4, 128), BF16), spread, jnp.zeros((2, 2, 128), BF16), spread_up], 1
-    )
-    mine = lax.dynamic_slice(omega, (4 * x, 0, 0), (4, 64, 32))
-    both = beside(mine, feat) if False else jnp.where(
-        feat == 0,
-        jnp.concatenate([mine, jnp.zeros_like(mine)], -1),
-        jnp.concatenate([jnp.zeros_like(mine), mine], -1),
-    )
-    blocks = jnp.eye(4, dtype=BF16)[:, None, :, None] * both[:, :, None, :]
-    omega_blocks = blocks.reshape(256, 256)
-
     def vm(shape, dtype=BF16):
         return pltpu.VMEM(shape, dtype)
 
     widths = (768, 256, 1024, 1024)
-    scratch = [vm((8, 2, 64, n)) for n in widths]
+    scratch = [vm((3, 4, 8)), vm((2, 64)), vm((4, 64)), vm((4, 32)), vm((8, 64)), vm((8, 32, 64))]
+    scratch += [pltpu.SMEM((1,), jnp.int32)]
+    scratch += [vm((2, 32, 128)), vm((256, 256))]
+    results = (
+        ((256, 1024), BF16), ((256, 1024), F32), ((3, 64, 512), F32), ((3, 4, 8), F32), ((64, 512), F32), ((2, 64), F32),
+        ((4, 64), F32), ((64, 2048), F32), ((4, 32), F32), ((64, 2048), F32), ((8, 64), F32),
+    )
+    scratch += [vm(*result) for result in results]
+    scratch += [vm((2, 8, 1024), F32), vm((3, 8, 2, 64, 256))] + [vm((8, 2, 64, n)) for n in widths[1:]]
     scratch += [vm((8, 2, 32, 128)), vm((256, 256)), vm((512, 1024)), vm((128, 1024))]
     scratch += [vm((3, 512, 256)), vm((2, 512, 256))] + [vm((2, 512, 256), F32)] * 3
     scratch += [vm((4, 128, 1024), F32), vm((4, 512, 512))] + [vm((512, 256), F32)] * 3 + [vm((512, 256))]
@@ -1135,33 +1206,36 @@
     scratch += [vm((4, 2, 64, n)) for n in widths] + [vm((2, 64, n)) for n in widths]
     scratch += [vm((2, 64, 1024), F32), vm((4, 64, 1024))] + [vm((64, n)) for n in widths]
     scratch += [vm((8, 1024), F32), vm((3, 8, 1024), F32), vm((16, 1024), F32), vm((6, 16, 1024), F32)]
-    scratch += [vm((128, 1024)), vm((16, 128)), vm((128, 1024)), vm((256, 1024))]
-    scratch += [pltpu.SemaphoreType.DMA((320,)), pltpu.SemaphoreType.DMA((320,))]
-
-    def out(shape, dtype=F32):
-        return jax.ShapeDtypeStruct(shape, dtype)
-
-    mixed, gtok, gq, go, gu, gd, dvec, tvec = pl.pallas_call(
+    scratch += [vm((128, 1024)), vm((128, 1024)), vm((256, 1024))]
+    scratch += [pltpu.SemaphoreType.DMA((320,)), pltpu.SemaphoreType.DMA((320,)), pltpu.SemaphoreType.DMA((40,))]
+
+    shapes = tuple(jax.ShapeDtypeStruct(*result) for result in results)
+    anywhere = pl.BlockSpec(memory_space=pl.ANY)
+    made = pl.pallas_call(
         layer_kernel,
-        out_shape=(
-            out((256, 1024), BF16), out((256, 1024)), out((64, 1536)), out((64, 512)), out((64, 2048)), out((64, 2048)),
-            out((8, 1024)), out((2, 8, 1024)),
-        ),
-        in_specs=[pl.BlockSpec(memory_space=pltpu.VMEM)] * 8,
-        out_specs=(pl.BlockSpec(memory_space=pltpu.VMEM),) * 8,
+        out_shape=shapes,
+        in_specs=[anywhere] * 13,
+        out_specs=(anywhere,) * len(shapes),
         scratch_shapes=scratch,
         compiler_params=pltpu.CompilerParams(
             collective_id=0, has_side_effects=True, vmem_limit_bytes=63 * 2**20
         ),
         name="layer",
-    )(tokens, cotangent, wq, wo, wu, wd, small, omega_blocks)
-    own = lax.dynamic_slice(dvec, (0, 64 * shard), (8, 64))
-    grad_up_bias = lax.dynamic_slice(tvec[:, 0].reshape(32, 64), (0, 4 * shard), (32, 4))
-    qkv_rows = tvec[:, 1, :768].reshape(2, 3, 4, 64).transpose(1, 0, 2, 3).reshape(3, 8, 64)
-    grad_qkv_bias = lax.dynamic_slice(qkv_rows, (0, 0, 4 * shard), (3, 8, 4))
-    grad_rpe = lax.dynamic_slice(tvec[:, 2:6].reshape(8, 1024), (0, 64 * (15 - shard)), (8, 64))[:, ::-1]
+    )(
+        tokens, qkv_weight.transpose(1, 0, 2), qkv_bias.transpose(0, 2, 1), out_weight.T, norm_gains, row_biases, up_weight,
+        up_bias.T, down_weight.T, rpe_bias, omega.transpose(0, 2, 1), bucket, cotangent,
+    )
+    mixed, gtok, gq, gqb, go, ggain, gbias, gu, gub, gd, grpe = pl.pallas_call(
+        copy_kernel,
+        out_shape=shapes,
+        in_specs=[anywhere] * len(shapes),
+        out_specs=(anywhere,) * len(shapes),
+        scratch_shapes=[vm(*result) for result in results] + [pltpu.SemaphoreType.DMA((2, len(shapes)))],
+        compiler_params=pltpu.CompilerParams(vmem_limit_bytes=63 * 2**20),
+        name="results",
+    )(*made)
     return (
-        mixed, gtok, gq.reshape(64, 3, 512), grad_qkv_bias, go.T, own[0:2], own[2:6], gu, grad_up_bias, gd.T, grad_rpe,
+        mixed, gtok, gq.transpose(1, 0, 2), gqb.transpose(0, 2, 1), go.T, ggain, gbias, gu, gub.T, gd.T, grpe,
     )
 
 

time: 214 us -> 192 us (0.90)
  local copies, waits for them, and re-layouts: 21.9 us -> 0 us
    unnamed x41 -> x0, local copies, waits for them, and re-layouts: 9.5 us -> none
    reshape x9 -> x0, local copies, waits for them, and re-layouts: 3.73 us -> none  [the longest x1 1.77 us: fast_local(): gq.reshape(64, 3, 512)]
    concatenate x3 -> x0, local copies, waits for them, and re-layouts: 2.57 us -> none  [the longest x1 2.42 us: fast_local(): jnp.concatenate([top, position, jnp.zeros((2, 4, 128), BF16), spread, jnp...]
    pallas_call x1 -> x2, Pallas kernels: 190 us -> 190 us  [the longest x1 187 us: fast_local(): pl.pallas_call(layer_kernel, out_shape=shapes, in_specs=[anywhere] * 13,...]
where the time goes in v2:
time: 192 us; the launch traced here: 191 us
  Pallas kernels  190 us (99%)
    pallas_call x1, Pallas kernels, fast_local(): pl.pallas_call(layer_kernel, out_shape=shapes, in_specs=[anywhere] * 13,...  187 us

profile of v2, /device:TPU:0, one launch (start us, length us, event | category | flops | bytes accessed | tf_op | source)
XLA Modules:
  0.0 191.4 jit_solution(9370646600268758475)
XLA Ops:
  1.3 187.0 %layer.1 = (bf16[256,1024]{1,0:T(8,128)(2,1)}, f32[256,1024]{1,0:T(8,128)}, f32[3,64,512]{2,1,0:T(8,128)}, f32[3,4,8]{2,1,0:T(4,128)}, f32[64,512]{1,0:T(8,128)}...) custom-call(bf16[256,1024]{1,0:T(8,128)(2,1)} %tok.1, ...), custom_call_target="tpu_custom_call" | custom-call | tf_op jit(solution)/shard_map/layer/pallas_call | solution.py:1214
  188.3 3.1 %results.1 = (bf16[256,1024]{1,0:T(8,128)(2,1)}, f32[256,1024]{1,0:T(8,128)}, f32[3,64,512]{2,1,0:T(8,128)}, f32[3,4,8]{2,1,0:T(4,128)}, f32[64,512]{1,0:T(8,128...) custom-call(bf16[256,1024]{1,0:T(8,128)(2,1)} %get-tuple-element.33., ...), custom_call_target="tpu_custom_call" | custom-call | tf_op jit(solution)/shard_map/results/pallas_call | solution.py:1228

commit v3 on v2

--- a/solution.py
+++ b/solution.py
@@ -441,12 +441,12 @@
     qb_v, gain_v, bias_v, ub_v, rpe_v, om_v, bk_v, small_s, om_s,
     mixed_o, gtok_o, gq_o, gqb_o, go_o, ggain_o, gbias_o, gu_o, gub_o, gd_o, grpe_o, tvec_o,
     wq, wo, wu, wd, small, om2, xg, cotb,
-    qkv, phi, ex, unit, inv, r0, pp, num, den, quo, att,
-    pb, rb_z, rb_f, rb_d, rb_i, fb, hid, dgel, efb, dub, dzb,
-    fst, n1, i1, dr,
-    dn, dd, ds_, gg, dph, dvv, dqkv, anti, ones64, rows_v,
-    g_q, g_o, g_u, g_d, r1_q, r1_o, r1_u, r1_d, t_q, t_o, t_u, t_d,
-    rz_q, rz_o, rz_u, rz_d, cb_q, cb_o, cb_u, cb_d, fs, xs, xr_q, xr_o, xr_u, xr_d,
+    qkv, phi, ex, unit, inv, r0, pp, num, den, quo, att, attf,
+    pb, rb_f, rb_d, rb_i, fb, hid, dgel, efb, dub, dzb, acc,
+    fst, n1, i1, dr, dat_s, dat, out_s, anti, ones64, rows_v,
+    dn, dd, ds_, gg, dph, dvv, dqkv,
+    g_k, g_v, g_o, g_u, g_d, r_k, r_v, r_o, r_u, r_d, rz_k, rz_v, rz_o, rz_u, rz_d, cb_k, cb_v, cb_o, cb_u, cb_d,
+    fs, xs_k, xs_v, xs_o, xs_u, xs_d, xr_k, xr_v, xr_o, xr_u, xr_d,
     sd, sd_r, st, st_r, mix_s, gt_s, gt_r,
     ss, rs, ls,
 ):
@@ -465,10 +465,16 @@
         return lambda: pl.when(cond)(copy.wait)
 
     home = c == x
+    away = c != x
+    own_block = 2 * x + y
 
     def half_cols(half, width):
         return pl.ds(pl.multiple_of(half * width, width), width)
 
+    def rows_of(index, count):
+        return pl.ds(pl.multiple_of(index * count, count), count)
+
+    in_o = bring(wo_h.at[:, half_cols(x, 256)], wo.at[own_block, 2 * z + x, c])
     in_q = bring(wq_h.at[:, :, half_cols(x, 256)], wq.at[:, 2 * z + x, c])
     in_small = [
         bring(src, dst)
@@ -476,11 +482,10 @@
             (gain_h, gain_v), (bias_h, bias_v), (rpe_h, rpe_v), (qb_h, qb_v), (ub_h, ub_v), (om_h, om_v), (bk_h, bk_v),
         )
     ]
-    in_o = bring(wo_h.at[:, half_cols(x, 256)], wo.at[2 * z + x, c])
-    in_tok = bring(tok, xg.at[pl.ds(pl.multiple_of(c * 256, 256), 256)], home)
-    in_cot = bring(cot.at[pl.ds(pl.multiple_of(y * 128, 128), 128)], cotb, home)
+    in_tok = bring(tok, xg.at[rows_of(c, 256)], home)
     in_u = bring(wu_h.at[:, half_cols(x, 1024)], wu.at[2 * z + x, c])
     in_d = bring(wd_h.at[:, half_cols(x, 1024)], wd.at[2 * z + x, c])
+    in_cot = bring(cot.at[rows_of(y, 128)], cotb, home)
 
     def dev(zz, xx, yy, cc):
         return {"dp": zz * 2 + xx, "heads": yy, "feat": cc}
@@ -488,7 +493,6 @@
     sib, xn, yn, dg = dev(z, x, y, 1 - c), dev(z, 1 - x, y, c), dev(z, x, 1 - y, c), dev(z, 1 - x, 1 - y, c)
     xs_dev, ds_dev = dev(z, 1 - x, y, 1 - c), dev(z, 1 - x, 1 - y, 1 - c)
     plane = (dg, xn, yn)
-    own_block = 2 * x + y
     plane_block = (2 * (1 - x) + 1 - y, 2 * (1 - x) + y, 2 * x + 1 - y)
 
     def rc(src, dst, s, r, device):
@@ -515,6 +519,27 @@
 
     def valid(dz):
         return jnp.logical_and(z + dz >= 0, z + dz < PLANES)
+
+    def by_plane(table):
+        found = []
+        for k in range(PLANES):
+            block = jnp.int32(table[0][k])
+            for zz in range(1, PLANES):
+                block = jnp.where(z == zz, table[zz][k], block)
+            found.append(block)
+        return found
+
+    arrive = by_plane(((0, 1, 2, 3), (1, 0, 2, 3), (2, 1, 3, 0), (3, 2, 1, 0)))
+    leave = by_plane(((3, 2, 1, 0), (3, 2, 0, 1), (0, 1, 3, 2), (0, 1, 2, 3)))
+
+    def at_step(blocks, k):
+        block = blocks[0]
+        for i in range(1, PLANES):
+            block = jnp.where(k == i, blocks[i], block)
+        return block
+
+    def cols256(n):
+        return pl.ds(pl.multiple_of(n * 256, 256), 256)
 
     barrier = pltpu.get_barrier_semaphore()
     for other in (sib, xn, yn, dg, xs_dev, ds_dev):
@@ -541,20 +566,39 @@
                 send(mine, mine, self.zs + z + dz, self.zs + z, dev(z + dz, x, y, c), valid(dz))
             send(mine, mine, self.sb + z, self.sb + z, sib)
 
+        def pump_step(self, n):
+            here = self.block(n, c)
+
+            def relay(device):
+                rc(here, here, self.fw, self.zs + n, device).start()
+
+            @pl.when(n != z)
+            def _():
+                got(here, self.zs + n)
+                pl.when(jnp.logical_and(z == 1, n == 3))(lambda: relay(dev(z - 1, x, y, c)))
+                pl.when(jnp.logical_and(z == 2, n == 0))(lambda: relay(dev(z + 1, x, y, c)))
+                rc(here, here, self.sb + n, self.sb + n, sib).start()
+
+        def pump_done(self):
+            mine = self.block(z, c)
+            pending.append(
+                lambda: pl.when((z == 1) | (z == 2))(lambda: rc(mine, mine, self.fw, self.fw, sib).wait_send())
+            )
+            for dz in (1, -1, 2, -2, 3, -3):
+                i = self.sb + z + dz
+                pending.append(lambda i=i, dz=dz: pl.when(valid(dz))(lambda: rc(mine, mine, i, i, sib).wait_send()))
+
         def pump(self):
-            for dz in (1, -1, 2, -2, 3, -3):
-                here = self.block(z + dz, c)
-                cond = valid(dz)
-                pl.when(cond)(lambda here=here, dz=dz: got(here, self.zs + z + dz))
-                if dz == 2:
-                    send(here, here, self.fw, self.zs + z + dz, dev(z - 1, x, y, c), z == 1)
-                if dz == -2:
-                    send(here, here, self.fw, self.zs + z + dz, dev(z + 1, x, y, c), z == 2)
-                send(here, here, self.sb + z + dz, self.sb + z + dz, sib, cond)
+            for k in range(1, PLANES):
+                self.pump_step(arrive[k])
+            self.pump_done()
+
+        def need_step(self, n):
+            got(self.block(n, 1 - c), self.sb + n)
 
         def need(self):
             for zz in range(PLANES):
-                got(self.block(zz, 1 - c), self.sb + zz)
+                self.need_step(zz)
 
     half_of = {}
 
@@ -570,10 +614,15 @@
         ref, i = half_of[name]
         got(place(ref, 1 - x), i)
 
+    wo_own = wo.at[own_block]
+    i_oh = sems.take()
+    send(
+        wo_h.at[:, half_cols(1 - x, 256)], wo.at[2 * (1 - x) + y, 2 * z + x, c], i_oh, i_oh, xn
+    )
     give_half("q", wq_h.at[:, :, half_cols(1 - x, 256)], wq)
+    it_qa, it_s, it_qb = Item(wq, "own"), Item(small, "both"), Item(wq, "other")
+    it_o, it_u, it_d = Item(wo_own, "both"), Item(wu, "both"), Item(wd, "both")
     in_q()
-    it_qa, it_s, it_qb = Item(wq, "own"), Item(small, "both"), Item(wq, "other")
-    it_o, it_u, it_d = Item(wo, "both"), Item(wu, "both"), Item(wd, "both")
     it_qa.start()
 
     for done in in_small:
@@ -585,7 +634,6 @@
     vec_sel = pick((64, 128), lambda k, l: l == c * 64 + k).astype(BF16)
     rpe_sel = pick((64, 128), lambda k, l: l == (1 - c) * 64 + 63 - k).astype(BF16)
     bias_sel = [pick((4, 128), lambda k, l, par=par: l == par * 64 + 4 * shard + k).astype(BF16) for par in range(2)]
-    small_s[...] = jnp.zeros_like(small_s)
     rpe_rows = dot(rpe_v[...], rpe_sel)
     level = jnp.full((1, 128), bk_v[0].astype(F32))
     top = jnp.concatenate(
@@ -614,29 +662,35 @@
     i_om = sems.take()
     send(om_s, om2, i_om, i_om, sib)
     t1, t2 = sems.take(), sems.take(2)
-    mine_rows = xg.at[pl.ds(pl.multiple_of(c * 256, 256), 256)]
-    send(tok, mine_rows, t1, t1, sib, c != x)
-    send(tok, mine_rows, t2 + c, t2 + c, dev(z, 1 - x, y, x))
-    give_half("o", wo_h.at[:, half_cols(1 - x, 256)], wo)
+    send(tok, xg.at[rows_of(c, 256)], t1, t1, sib, away)
+    send(tok, xg.at[rows_of(c, 256)], t2 + c, t2 + c, dev(z, 1 - x, y, x))
     give_half("u", wu_h.at[:, half_cols(1 - x, 1024)], wu)
-    give_half("d", wd_h.at[:, half_cols(1 - x, 1024)], wd)
-    t3 = sems.take()
-    send(cot.at[pl.ds(pl.multiple_of(y * 128, 128), 128)], cotb, t3, t3, xs_dev, c != x)
 
     same = (iota((256, 256), 0) // HEAD) == (iota((256, 256), 1) // HEAD)
     ones64[...] = jnp.where(same, 1.0, 0.0).astype(BF16)
     anti[...] = jnp.where(iota((512, 512), 0) + iota((512, 512), 1) == 511, 1.0, 0.0).astype(BF16)
 
+    have_half("q")
+    it_qb.start()
+    got(wo.at[own_block, 2 * z + 1 - x, c], i_oh)
+    in_o()
+    it_o.start()
     have_half("s")
     it_s.start()
-    have_half("q")
-    it_qb.start()
     it_qa.pump()
-    have_half("o")
-    in_o()
-    it_o.start()
+    it_qb.pump()
+    it_o.pump()
+    i_oq, i_os = sems.take(3), sems.take(3)
+    quarter = wo.at[own_block, :, c]
+    for slot in range(3):
+        send(quarter, quarter, i_oq + slot, i_oq + slot, plane[slot])
+    give_half("d", wd_h.at[:, half_cols(1 - x, 1024)], wd)
+    t3 = sems.take()
+    send(cot.at[rows_of(y, 128)], cotb, t3, t3, xs_dev, away)
+    have_half("u")
+    in_u()
+    it_u.start()
     it_s.pump()
-    it_qb.pump()
 
     it_s.need()
     for t in range(8):
@@ -665,26 +719,22 @@
         return carry
 
     lax.fori_loop(0, 4, coeff_body, 0)
-
-    have_half("u")
-    in_u()
-    it_u.start()
+    num[...] = jnp.zeros_like(num)
+    den[...] = jnp.zeros_like(den)
+
     in_tok()
-    in_cot()
-    pl.when(c == x)(lambda: got(xg.at[pl.ds(pl.multiple_of((1 - c) * 256, 256), 256)], t1))
-
-    @pl.when(c != x)
+    pl.when(home)(lambda: got(xg.at[rows_of(1 - c, 256)], t1))
+
+    @pl.when(away)
     def _():
         got(xg.at[pl.ds(0, 256)], t2)
         got(xg.at[pl.ds(256, 256)], t2 + 1)
-        got(cotb, t3)
 
     it_qa.need()
     it_qb.need()
 
     def qkv_body(p, carry):
-        cols = pl.ds(pl.multiple_of(p * 256, 256), 256)
-        qkv[p] = (dot(xg[...], wq[p].reshape(1024, 256)) + rows_v[16:17, cols]).astype(BF16)
+        qkv[p] = (dot(xg[...], wq[p].reshape(1024, 256)) + rows_v[16:17, cols256(p)]).astype(BF16)
         return carry
 
     lax.fori_loop(0, 3, qkv_body, 0)
@@ -705,14 +755,7 @@
         return carry
 
     lax.fori_loop(0, 2, feature_body, 0)
-    have_half("d")
-    in_d()
-    it_d.start()
-    it_o.pump()
-
     lane_head = iota((1, 128), 1) // HEAD
-    num[...] = jnp.zeros_like(num)
-    den[...] = jnp.zeros_like(den)
 
     def head_cols(h):
         return pl.ds(pl.multiple_of((h // 2) * 128, 128), 128), (lane_head == h % 2)
@@ -732,21 +775,54 @@
 
     lax.fori_loop(0, 4, head_body, 0)
     quo[...] = num[...] / den[...]
-    att[...] = quo[...].astype(BF16)
+    att[...] = quo[...].astype(BF16).reshape(4, 128, 256)
+
+    i_at = sems.take(3)
+    for slot in range(3):
+        send(att.at[plane_block[slot]], attf.at[own_block], i_at + slot, i_at + slot, plane[slot])
+    attf[own_block] = att[own_block]
+    for slot in range(3):
+        part = wo.at[plane_block[slot], :, c]
+        got(part, i_oq + slot)
+        send(part, part, i_os + slot, i_os + slot, sib)
+    have_half("d")
+    in_d()
+    it_d.start()
+    it_o.need()
+    for slot in range(3):
+        got(attf.at[plane_block[slot]], i_at + slot)
+    for slot in range(3):
+        got(wo.at[plane_block[slot], :, 1 - c], i_os + slot)
+
+    def out_body(q, carry):
+        return carry + dot(attf[q], wo[q].reshape(1024, 256), NT)
+
+    mixed_z = lax.fori_loop(0, 4, out_body, jnp.zeros((128, 1024), F32))
+
+    def norm(values):
+        centred = values - jnp.mean(values, axis=-1, keepdims=True)
+        inverse = lax.rsqrt(jnp.mean(centred * centred, axis=-1, keepdims=True) + EPSILON)
+        return centred * inverse, inverse
+
+    residual = mixed_z + xg[rows_of(own_block, 128)].astype(F32) + rows_v[2:3, :]
+    normed, inverse = norm(residual)
+    first = normed * rows_v[0:1, :] + rows_v[3:4, :]
+    fb[own_block] = first.astype(BF16)
 
     class Scatter:
         def __init__(self, ref):
             self.ref, self.base = ref, sems.take(12)
 
-        def part(self, n):
-            cols = pl.ds(pl.multiple_of(n * 256, 256), 256)
+        def part(self, n, value):
+            cols = cols256(n)
+            pb[:, :, cols] = value.astype(BF16).reshape(4, 128, 256)
             for slot in range(3):
                 i = self.base + slot * 4 + n
                 rc(pb.at[plane_block[slot], :, cols], self.ref.at[slot, :, cols], i, i, plane[slot]).start()
 
         def total(self):
-            for slot in range(3):
-                for n in range(4):
+            for n in range(4):
+                for slot in range(3):
                     got(self.ref.at[slot, :, n * 256 : (n + 1) * 256], self.base + slot * 4 + n)
             value = pb[own_block].astype(F32)
             for slot in range(3):
@@ -761,68 +837,74 @@
                     rc(src, src, i, i, plane[slot]).wait_send()
 
     class Gather:
-        def __init__(self, ref):
-            self.ref, self.base = ref, sems.take(3)
+        def __init__(self, ref, order):
+            self.ref, self.base, self.order = ref, sems.take(12), order
 
         def start(self):
-            mine = self.ref.at[own_block]
+            for n in self.order:
+                for slot in range(3):
+                    mine = self.ref.at[own_block, :, cols256(n)]
+                    i = self.base + slot * 4 + n
+                    send(mine, mine, i, i, plane[slot])
+
+        def need(self, n):
             for slot in range(3):
-                send(mine, mine, self.base + slot, self.base + slot, plane[slot])
-
-        def need(self):
-            for slot in range(3):
-                got(self.ref.at[plane_block[slot]], self.base + slot)
-
-    def scatter(ref, part):
-        s = Scatter(ref)
-
-        def body(n, carry):
-            cols = pl.ds(pl.multiple_of(n * 256, 256), 256)
-            pb[:, :, cols] = part(n).astype(BF16).reshape(4, 128, 256)
-            s.part(n)
-            return carry
-
-        lax.fori_loop(0, 4, body, 0)
-        return s
-
-    it_o.need()
-    sc_z = scatter(rb_z, lambda n: dot(att[...], wo[pl.ds(2 * n, 2)].reshape(256, 256), NT))
-    it_u.pump()
-    it_u.need()
-
-    def norm(values):
-        centred = values - jnp.mean(values, axis=-1, keepdims=True)
-        inverse = lax.rsqrt(jnp.mean(centred * centred, axis=-1, keepdims=True) + EPSILON)
-        return centred * inverse, inverse
-
-    own_rows = pl.ds(pl.multiple_of(own_block * 128, 128), 128)
-    residual = sc_z.total() + xg[own_rows].astype(F32) + rows_v[2:3, :]
-    normed, inverse = norm(residual)
-    first = normed * rows_v[0:1, :] + rows_v[3:4, :]
+                got(self.ref.at[plane_block[slot], :, cols256(n)], self.base + slot * 4 + n)
+
+    g_first = Gather(fb, range(4))
+    g_first.start()
     fst[...] = first
     n1[...] = normed
     i1[...] = jnp.broadcast_to(inverse, (128, 128))
-    fb[own_block] = first.astype(BF16)
-    g_first = Gather(fb)
-    g_first.start()
-    sc_z.sent()
-    g_first.need()
+
+    def d_cols(ref, m):
+        return ref[:, :, cols256(m)].reshape(512, 256)
+
+    acc[...] = jnp.zeros_like(acc)
+    it_u.pump()
+    it_u.need()
+
+    def hidden_part(n, carry):
+        g_first.need(n)
+        left = d_cols(fb, n)
+        for j in range(4):
+            cols = slice(j * 256, (j + 1) * 256)
+            acc[:, cols] += dot(left, wu[pl.ds(2 * n, 2), :, :, cols].reshape(256, 256))
+        return carry
+
+    lax.fori_loop(0, 4, hidden_part, 0)
 
     def hidden_body(n, carry):
-        cols = pl.ds(pl.multiple_of(n * 256, 256), 256)
-        pre = dot(fb[...].reshape(512, 1024), wu[:, :, :, cols].reshape(1024, 256)) + rows_v[17:18, cols]
+        cols = cols256(n)
+        pre = acc[:, cols] + rows_v[17:18, cols]
         cdf = 0.5 * (1.0 + lax.erf(pre * 0.7071067811865476))
         hid[:, cols] = (pre * cdf).astype(BF16)
         dgel[:, cols] = cdf + pre * (0.3989422804014327 * jnp.exp(-0.5 * pre * pre))
         return carry
 
     lax.fori_loop(0, 4, hidden_body, 0)
-    it_d.pump()
-    it_d.need()
-    sc_f = scatter(rb_f, lambda n: dot(hid[...], wd[pl.ds(2 * n, 2)].reshape(256, 1024), NT))
+    sc_f = Scatter(rb_f)
+
+    def down_part(k, carry):
+        n = at_step(arrive, k)
+        it_d.pump_step(n)
+        it_d.need_step(n)
+        sc_f.part(n, dot(hid[...], wd[pl.ds(2 * n, 2)].reshape(256, 1024), NT))
+        return carry
+
+    lax.fori_loop(0, 4, down_part, 0)
+    it_d.pump_done()
+    pl.when(away)(lambda: got(cotb, t3))
+    in_cot()
+    upstream = cotb[...].astype(F32)
+
+    def down(values):
+        return jnp.sum(values, axis=0, keepdims=True)
+
+    sd[5:6, :] = down(upstream)
+    acc[...] = jnp.zeros_like(acc)
     second = fst[...] + sc_f.total() + rows_v[4:5, :]
     normed2, inverse2 = norm(second)
-    mix_s[...] = (normed2 * rows_v[1:2, :] + rows_v[5:6, :]).astype(BF16)
 
     def norm_back(upstream, normed, inverse, gain):
         scaled = upstream * gain
@@ -830,32 +912,26 @@
         slope = jnp.mean(scaled * normed, axis=-1, keepdims=True)
         return inverse * (scaled - mean - normed * slope)
 
-    def down(values):
-        return jnp.sum(values, axis=0, keepdims=True)
-
-    upstream = cotb[...].astype(F32)
-    sd[1:2, :] = down(upstream * normed2)
-    sd[5:6, :] = down(upstream)
     err = norm_back(upstream, normed2, inverse2, rows_v[1:2, :])
     efb[own_block] = err.astype(BF16)
-    sd[4:5, :] = down(efb[own_block].astype(F32))
-    g_ef = Gather(efb)
+    g_ef = Gather(efb, leave)
     g_ef.start()
     dr[...] = err
+    mix_s[...] = (normed2 * rows_v[1:2, :] + rows_v[5:6, :]).astype(BF16)
+    sd[1:2, :] = down(upstream * normed2)
+    sd[4:5, :] = down(err.astype(BF16).astype(F32))
     sc_f.sent()
 
     i_mix, i_gt = sems.take(2), sems.take(2)
 
     def to_owner(src, dst, i):
-        rows = pl.ds(pl.multiple_of(y * 128, 128), 128)
-        home = c == x
+        rows = rows_of(y, 128)
 
         @pl.when(home)
         def _():
             dst[rows] = src[...]
 
         send(src, dst.at[rows], i + 1, i + 1, yn, home)
-        away = jnp.logical_not(home)
         send(src, dst.at[rows], i, i + y, xs_dev, away)
         send(src, dst.at[rows], i + 1, i + y, ds_dev, away)
 
@@ -863,159 +939,196 @@
         for half in range(2):
             part = dst.at[half * 128 : (half + 1) * 128]
 
-            @pl.when(jnp.logical_and(c == x, y != half))
+            @pl.when(jnp.logical_and(home, y != half))
             def _(part=part):
                 got(part, i + 1)
 
-            @pl.when(c != x)
+            @pl.when(away)
             def _(part=part, half=half):
                 got(part, i + half)
 
-    to_owner(mix_s, mixed_o, i_mix)
-    g_ef.need()
-
     class Grad:
-        def __init__(self, g, r1, t, rz, cb, xr):
-            self.g, self.r1, self.t, self.rz, self.cb, self.xr = g, r1, t, rz, cb, xr
+        def __init__(self, g, r, rz, cb, xs, xr):
+            self.g, self.r, self.rz, self.cb, self.xs, self.xr = g, r, rz, cb, xs, xr
             self.d, self.z, self.k, self.x = sems.take(4), sems.take(PLANES), sems.take(), sems.take()
-
-        def make(self, part):
-            def body(m, carry):
-                part(m)
-                i = self.d + m
-                rc(self.g.at[m, :, 1 - c], self.r1.at[m], i, i, sib).start()
+            self.width = r.shape[-1]
+
+        def give(self, m):
+            i = self.d + m
+            rc(self.g.at[m, :, 1 - c], self.r.at[m], i, i, sib).start()
+
+        def pair_step(self, m):
+            got(self.r.at[m], self.d + m)
+            self.r[m] = (self.g[m, :, c].astype(F32) + self.r[m].astype(F32)).astype(BF16)
+            far = jnp.abs(m - z)
+            part = self.r.at[m]
+
+            def out(device):
+                rc(part, self.rz.at[z], self.z + m, self.z + z, device).start()
+
+            pl.when(far == 1)(lambda: out(dev(m, x, y, c)))
+            pl.when(jnp.logical_and(far == 2, (z == 0) | (z == 3)))(lambda: out(dev(m, x, y, c)))
+            pl.when(far == 3)(
+                lambda: rc(part, self.cb, self.k, self.k, dev(jnp.where(z == 0, 1, 2), x, y, c)).start()
+            )
+
+        def relay(self):
+            for at, m in ((1, 3), (2, 0)):
+                @pl.when(z == at)
+                def _(at=at, m=m):
+                    got(self.cb, self.k)
+                    self.r[m] = (self.r[m].astype(F32) + self.cb[...].astype(F32)).astype(BF16)
+                    rc(self.r.at[m], self.rz.at[at], self.z + m, self.z + at, dev(m, x, y, c)).start()
+
+        def run(self, make):
+            def body(k, carry):
+                m = at_step(leave, k)
+                make(m)
+                self.give(m)
+                pl.when(k > 0)(lambda: self.pair_step(at_step(leave, k - 1)))
                 return carry
 
             lax.fori_loop(0, PLANES, body, 0)
-
-            def done():
-                for m in range(PLANES):
-                    src = self.g.at[m, :, 1 - c]
-                    rc(src, src, self.d + m, self.d + m, sib).wait_send()
-
-            pending.append(done)
-
-        def pair(self):
-            def body(m, carry):
-                got(self.r1.at[m], self.d + m)
-                self.t[m] = (self.g[m, :, c].astype(F32) + self.r1[m].astype(F32)).astype(BF16)
-                return carry
-
-            lax.fori_loop(0, PLANES, body, 0)
-            send(self.t.at[PLANES - 1], self.cb, self.k, self.k, dev(1, x, y, c), z == 0)
-            send(self.t.at[0], self.cb, self.k, self.k, dev(2, x, y, c), z == 3)
-            for dz in (1, -1):
-                send(self.t.at[z + dz], self.rz.at[z], self.z + z + dz, self.z + z, dev(z + dz, x, y, c), valid(dz))
-            for dz, at in ((2, 0), (-2, 3)):
-                send(self.t.at[z + dz], self.rz.at[z], self.z + z + dz, self.z + z, dev(z + dz, x, y, c), z == at)
-
-        def relay(self):
-            for dz, at in ((2, 1), (-2, 2)):
-                @pl.when(z == at)
-                def _(dz=dz):
-                    got(self.cb, self.k)
-                    self.t[z + dz] = (self.t[z + dz].astype(F32) + self.cb[...].astype(F32)).astype(BF16)
-
-                send(self.t.at[z + dz], self.rz.at[z], self.z + z + dz, self.z + z, dev(z + dz, x, y, c), z == at)
+            self.pair_step(leave[3])
 
         def finish(self):
-            width = self.t.shape[-1]
-            acc = fs.at[:, :, 0:width]
-            acc[...] = self.t[z].astype(F32)
+            total = fs.at[:, :, 0 : self.width]
+            total[...] = self.r[z].astype(F32)
             for dz in (1, -1, 2, -2):
                 @pl.when(valid(dz))
                 def _(dz=dz):
                     got(self.rz.at[z + dz], self.z + z + dz)
-                    acc[...] += self.rz[z + dz].astype(F32)
-            keep = xs.at[self.slot, :, 0:width]
-            keep[...] = fs[1 - x, :, 0:width].astype(BF16)
-            send(keep, self.xr, self.x, self.x, xn)
-
-        def columns(self, out, half, value):
+                    total[...] += self.rz[z + dz].astype(F32)
+            self.xs[...] = fs[1 - x, :, 0 : self.width].astype(BF16)
+            send(self.xs, self.xr, self.x, self.x, xn)
+
+        def sent(self):
+            for m in range(PLANES):
+                i = self.d + m
+                rc(self.g.at[m, :, c], self.g.at[m, :, c], i, i, sib).wait_send()
+            part = self.r.at[0]
+            for dz in (1, -1, 2, -2):
+                i = self.z + z + dz
+                pl.when(valid(dz))(lambda i=i: rc(part, part, i, i, sib).wait_send())
+            pl.when((z == 0) | (z == 3))(lambda: rc(part, part, self.k, self.k, sib).wait_send())
+
+        def columns(self, out, half, value, at=0):
             if len(out.shape) == 3:
-                for p in range(3):
-                    out[p, :, half_cols(half, 256)] = value[:, p * 256 : (p + 1) * 256]
+                for p in range(self.width // 256):
+                    out[at + p, :, half_cols(half, 256)] = value[:, p * 256 : (p + 1) * 256]
             else:
-                out[:, half_cols(half, self.t.shape[-1])] = value
-
-        def write_own(self, out):
-            width = self.t.shape[-1]
-            self.columns(out, x, fs[x, :, 0:width])
-
-        def write_other(self, out):
+                out[:, half_cols(half, self.width)] = value
+
+        def write_own(self, out, at=0):
+            self.columns(out, x, fs[x, :, 0 : self.width], at)
+
+        def write_other(self, out, at=0):
             got(self.xr, self.x)
-            self.columns(out, 1 - x, self.xr[...].astype(F32))
-
-    gr_d = Grad(g_d, r1_d, t_d, rz_d, cb_d, xr_d)
-    gr_u = Grad(g_u, r1_u, t_u, rz_u, cb_u, xr_u)
-    gr_o = Grad(g_o, r1_o, t_o, rz_o, cb_o, xr_o)
-    gr_q = Grad(g_q, r1_q, t_q, rz_q, cb_q, xr_q)
-    for slot, gr in enumerate((gr_d, gr_u, gr_o, gr_q)):
-        gr.slot = slot
-
-    def d_cols(ref, m):
-        return ref[:, :, pl.ds(pl.multiple_of(m * 256, 256), 256)].reshape(512, 256)
+            self.columns(out, 1 - x, self.xr[...].astype(F32), at)
+
+    gr_d = Grad(g_d, r_d, rz_d, cb_d, xs_d, xr_d)
+    gr_u = Grad(g_u, r_u, rz_u, cb_u, xs_u, xr_u)
+    gr_o = Grad(g_o, r_o, rz_o, cb_o, xs_o, xr_o)
+    gr_v = Grad(g_v, r_v, rz_v, cb_v, xs_v, xr_v)
+    gr_k = Grad(g_k, r_k, rz_k, cb_k, xs_k, xr_k)
 
     def make_down(m):
-        g_d[m] = dot(d_cols(efb, m), hid[...], TN).astype(BF16).reshape(2, 2, 64, 1024)
-
-    gr_d.make(make_down)
-
+        g_ef.need(m)
+        left = d_cols(efb, m)
+        g_d[m] = dot(left, hid[...], TN).astype(BF16).reshape(2, 2, 64, 1024)
+        gr_d.give(m)
+        for j in range(4):
+            cols = slice(j * 256, (j + 1) * 256)
+            acc[:, cols] += dot(left, wd[pl.ds(2 * m, 2), :, :, cols].reshape(256, 256))
+
+    def down_grads(k, carry):
+        m = at_step(leave, k)
+        make_down(m)
+        pl.when(k > 0)(lambda: gr_d.pair_step(at_step(leave, k - 1)))
+        return carry
+
+    lax.fori_loop(0, PLANES, down_grads, 0)
     def du_body(n, carry):
-        cols = pl.ds(pl.multiple_of(n * 256, 256), 256)
-        dact = dot(efb[...].reshape(512, 1024), wd[:, :, :, cols].reshape(1024, 256))
-        du = (dact * dgel[:, cols]).astype(BF16)
+        cols = cols256(n)
+        du = (acc[:, cols] * dgel[:, cols]).astype(BF16)
         dub[:, cols] = du
         st[0:1, cols] = down(du.astype(F32))
         return carry
 
     lax.fori_loop(0, 4, du_body, 0)
-    sc_d = scatter(rb_d, lambda n: dot(dub[...], wu[pl.ds(2 * n, 2)].reshape(256, 1024), NT))
-    gr_d.pair()
+    sc_d = Scatter(rb_d)
+
+    def back_part(n, carry):
+        sc_d.part(n, dot(dub[...], wu[pl.ds(2 * n, 2)].reshape(256, 1024), NT))
+        return carry
+
+    lax.fori_loop(0, 4, back_part, 0)
+    gr_d.pair_step(leave[3])
 
     def make_up(m):
         g_u[m] = dot(d_cols(fb, m), dub[...], TN).astype(BF16).reshape(2, 2, 64, 1024)
 
-    gr_u.make(make_up)
-    gr_u.pair()
+    gr_u.run(make_up)
     gr_d.relay()
+    to_owner(mix_s, mixed_o, i_mix)
     dfirst = dr[...] + sc_d.total()
+    back = norm_back(dfirst, n1[...], i1[:, 0:1], rows_v[0:1, :])
+    dz = back.astype(BF16)
+    dzb[own_block] = dz
+
+    def dattn_body(q, carry):
+        dat_s[q] = dot(dz, wo[q].reshape(1024, 256)).astype(BF16)
+        return carry
+
+    lax.fori_loop(0, 4, dattn_body, 0)
+    i_da = sems.take(3)
+    for slot in range(3):
+        send(dat_s.at[plane_block[slot]], dat.at[own_block], i_da + slot, i_da + slot, plane[slot])
+    dat[own_block] = dat_s[own_block]
+    g_dz = Gather(dzb, leave)
+    g_dz.start()
     sd[0:1, :] = down(dfirst * n1[...])
     sd[3:4, :] = down(dfirst)
-    back = norm_back(dfirst, n1[...], i1[:, 0:1], rows_v[0:1, :])
-    dr[...] = back
-    dzb[own_block] = back.astype(BF16)
-    sd[2:3, :] = down(dzb[own_block].astype(F32))
-    g_dz = Gather(dzb)
-    g_dz.start()
-    sc_d.sent()
-
+    sd[2:3, :] = down(dz.astype(F32))
+    sd[6:8, :] = jnp.zeros((2, 1024), F32)
     i_sd = sems.take(3)
-    sd[6:8, :] = jnp.zeros((2, 1024), F32)
     for k, device in enumerate(plane):
         send(sd, sd_r.at[k], i_sd + k, i_sd + k, device)
-    g_dz.need()
-
-    dattn = dot(dzb[...].reshape(512, 1024), wo[...].reshape(1024, 256))
-
-    def make_out(m):
-        g_o[m] = dot(d_cols(dzb, m), att[...], TN).astype(BF16).reshape(2, 2, 64, 256)
-
-    gr_o.make(make_out)
+    dr[...] = back
+    sc_d.sent()
+    dph[...] = jnp.zeros_like(dph)
+    dvv[...] = jnp.zeros_like(dvv)
+    for slot in range(3):
+        got(dat.at[plane_block[slot]], i_da + slot)
+
+    dattn = dat[...].reshape(512, 256).astype(F32)
     recip = 1.0 / den[...]
     dn[...] = (dattn * recip).astype(BF16)
     dsum = split_dot(dattn * quo[...], ones64[...])
     dd[...] = ((-dsum * recip).astype(BF16).astype(F32) * (1.0 / HEAD)).astype(BF16)
-    gr_o.pair()
+
+    def value_back(h, carry):
+        cols, mine = head_cols(h)
+        keep = jnp.where(mine, 1.0, 0.0).astype(BF16)
+        dvv[:, cols] += dot(pp[h], dn[:, cols] * keep, TN)
+        return carry
+
+    lax.fori_loop(0, 4, value_back, 0)
+    dqkv[2] = dvv[...].astype(BF16)
+
+    def x_cols(m):
+        return xg[:, cols256(m)]
+
+    def make_v(m):
+        g_v[m] = dot(x_cols(m), dqkv[2], TN).astype(BF16).reshape(2, 2, 64, 256)
+
+    gr_v.run(make_v)
     gr_u.relay()
-    dph[...] = jnp.zeros_like(dph)
-    dvv[...] = jnp.zeros_like(dvv)
 
     def head_back(h, carry):
         cols, mine = head_cols(h)
         keep = jnp.where(mine, 1.0, 0.0).astype(BF16)
-        dnum = dn[:, cols] * keep
-        left = jnp.concatenate([dnum, dd[:, cols] * keep], axis=1)
+        left = jnp.concatenate([dn[:, cols] * keep, dd[:, cols] * keep], axis=1)
         right = jnp.concatenate([qkv[2, :, cols], jnp.ones((512, 128), BF16)], axis=1)
         grad_p = dot(left, right, NT)
         for b in range(4):
@@ -1023,11 +1136,50 @@
             coefficient = r0[h, :, 512 - 128 * b : 1024 - 128 * b] * masks[b]
             part = grad_p[rows]
             ds_[rows] = (part * coefficient).astype(BF16)
-            gg[rows] = (part * pp[h, rows].astype(F32)).astype(BF16)
-        dvv[:, cols] += dot(pp[h], dnum, TN)
+            gg[h, rows] = (part * pp[h, rows].astype(F32)).astype(BF16)
         dph[0, :, cols] += dot(ds_[...], phi[1, :, cols] * keep)
         dph[1, :, cols] += dot(ds_[...], phi[0, :, cols] * keep, TN)
-        flipped = dot(anti[...], gg[...])
+        return carry
+
+    lax.fori_loop(0, 4, head_back, 0)
+
+    def feature_back_body(t, carry):
+        dlog = (dph[t] * ex[t]).astype(BF16)
+        units = unit[t]
+        dunit = SCALE * dot(dlog, om2[...], NT) - SCALE * SCALE * dot(dlog, ones64[...]) * units
+        mean = split_dot(dunit * units, ones64[...]) * (1.0 / HEAD)
+        dqkv[t] = (inv[t] * (dunit - units * mean)).astype(BF16)
+        return carry
+
+    lax.fori_loop(0, 2, feature_back_body, 0)
+    sc_i = Scatter(rb_i)
+
+    def input_part(n, carry):
+        value = jnp.zeros((512, 256), F32)
+        for p in range(3):
+            value = value + dot(dqkv[p], wq[p, pl.ds(2 * n, 2)].reshape(256, 256), NT)
+        sc_i.part(n, value)
+        return carry
+
+    lax.fori_loop(0, 4, input_part, 0)
+
+    def make_k(m):
+        for p in range(2):
+            g_k[m, :, :, :, p * 256 : (p + 1) * 256] = (
+                dot(x_cols(m), dqkv[p], TN).astype(BF16).reshape(2, 2, 64, 256)
+            )
+
+    gr_k.run(make_k)
+
+    def make_out(m):
+        g_dz.need(m)
+        g_o[m] = dot(d_cols(dzb, m), att[...].reshape(512, 256), TN).astype(BF16).reshape(2, 2, 64, 256)
+
+    gr_o.run(make_out)
+    gr_v.relay()
+
+    def diagonal_body(h, carry):
+        flipped = dot(anti[...], gg[h])
         sums = jnp.zeros((1, 1024), F32)
         for b in range(4):
             wide = jnp.concatenate([flipped[b * 128 : (b + 1) * 128], jnp.zeros((128, 128), F32)], axis=1)
@@ -1041,67 +1193,36 @@
         st[pl.ds(2 + h, 1), :] = sums
         return carry
 
-    lax.fori_loop(0, 4, head_back, 0)
-    gr_o.relay()
-
-    def feature_back_body(t, carry):
-        dlog = (dph[t] * ex[t]).astype(BF16)
-        units = unit[t]
-        dunit = SCALE * dot(dlog, om2[...], NT) - SCALE * SCALE * dot(dlog, ones64[...]) * units
-        mean = split_dot(dunit * units, ones64[...]) * (1.0 / HEAD)
-        dqkv[t] = (inv[t] * (dunit - units * mean)).astype(BF16)
-        return carry
-
-    lax.fori_loop(0, 2, feature_back_body, 0)
-    dqkv[2] = dvv[...].astype(BF16)
-
-    def input_part(n):
-        value = jnp.zeros((512, 256), F32)
-        for p in range(3):
-            value = value + dot(dqkv[p], wq[p, pl.ds(2 * n, 2)].reshape(256, 256), NT)
-        return value
-
-    sc_i = scatter(rb_i, input_part)
-
-    def make_qkv(m):
-        left = xg[:, pl.ds(pl.multiple_of(m * 256, 256), 256)]
-        for p in range(3):
-            value = dot(left, dqkv[p], TN).astype(BF16).reshape(2, 2, 64, 256)
-            g_q[m, :, :, :, p * 256 : (p + 1) * 256] = value
-
-    gr_q.make(make_qkv)
+    lax.fori_loop(0, 4, diagonal_body, 0)
     for p in range(3):
         st[1:2, p * 256 : (p + 1) * 256] = down(dqkv[p].astype(F32))
     st[1:2, 768:1024] = jnp.zeros((1, 256), F32)
     st[6:8, :] = jnp.zeros((2, 1024), F32)
-    gr_q.pair()
-
     i_c, i_zz, i_h = sems.take(), sems.take(PLANES), sems.take()
     for k in range(3):
         got(sd_r.at[k], i_sd + k)
     st[8:16, :] = sd[...] + sd_r[0] + sd_r[1] + sd_r[2]
     send(st, st_r.at[0], i_c, i_c, sib)
+    gr_d.finish()
+    gr_d.write_own(gd_o)
     got(st_r.at[0], i_c)
     st_r[1] = st[...] + st_r[0]
     for zz in range(PLANES):
         send(st_r.at[1], st_r.at[2 + z], i_zz + zz, i_zz + z, dev(zz, x, y, c), z != zz)
-
-    gr_d.finish()
-    gr_d.write_own(gd_o)
-    gr_u.finish()
-    gr_u.write_own(gu_o)
-    gr_o.finish()
-    gr_o.write_own(go_o)
     outs = []
     from_owner(mixed_o, i_mix)
     outs.append(bring(mixed_o, mixed_h))
-    gr_d.write_other(gd_o)
-    outs.append(bring(gd_o, gd_h))
+    gr_k.relay()
+    gr_o.relay()
+    gr_u.finish()
+    gr_u.write_own(gu_o)
     back = dr[...] + sc_i.total()
     gt_s[...] = back.astype(BF16)
     to_owner(gt_s, gt_r, i_gt)
-    sc_i.sent()
-    gr_q.relay()
+    gr_d.write_other(gd_o)
+    outs.append(bring(gd_o, gd_h))
+    gr_v.finish()
+    gr_v.write_own(gq_o, 2)
     total = st_r[1]
     for zz in range(PLANES):
         @pl.when(z != zz)
@@ -1117,8 +1238,6 @@
     send(tvec_o.at[x], tvec_o.at[x], i_h, i_h, xn)
     gr_u.write_other(gu_o)
     outs.append(bring(gu_o, gu_h))
-    gr_o.write_other(go_o)
-    outs.append(bring(go_o, go_h))
 
     def exact(left, right):
         return lax.dot_general(left, right, NN, precision=lax.Precision.HIGHEST, preferred_element_type=F32)
@@ -1130,6 +1249,10 @@
     gbias_o[...] = own[2:6]
     outs.append(bring(ggain_o, ggain_h))
     outs.append(bring(gbias_o, gbias_h))
+    gr_k.finish()
+    gr_k.write_own(gq_o)
+    gr_o.finish()
+    gr_o.write_own(go_o)
     got(tvec_o.at[1 - x], i_h)
     tile = pl.ds(pl.multiple_of((7 - dp) * 128, 128), 128)
     lines = jnp.concatenate([tvec_o[0, 2:6, tile], tvec_o[1, 2:6, tile]], axis=0)
@@ -1153,10 +1276,14 @@
     from_owner(gt_r, i_gt)
     gtok_o[...] = gt_r[...].astype(F32)
     outs.append(bring(gtok_o, gtok_h))
-    gr_q.finish()
-    gr_q.write_own(gq_o)
-    gr_q.write_other(gq_o)
+    gr_v.write_other(gq_o, 2)
+    gr_k.write_other(gq_o)
     outs.append(bring(gq_o, gq_h))
+    gr_o.write_other(go_o)
+    outs.append(bring(go_o, go_h))
+    sc_i.sent()
+    for gr in (gr_d, gr_u, gr_o, gr_v, gr_k):
+        gr.sent()
     for done in pending + outs:
         done()
 
@@ -1182,32 +1309,31 @@
     def vm(shape, dtype=BF16):
         return pltpu.VMEM(shape, dtype)
 
-    widths = (768, 256, 1024, 1024)
+    widths = (512, 256, 256, 1024, 1024)
     scratch = [vm((3, 4, 8)), vm((2, 64)), vm((4, 64)), vm((4, 32)), vm((8, 64)), vm((8, 32, 64))]
-    scratch += [pltpu.SMEM((1,), jnp.int32)]
-    scratch += [vm((2, 32, 128)), vm((256, 256))]
+    scratch += [pltpu.SMEM((1,), jnp.int32), vm((2, 32, 128)), vm((256, 256))]
     results = (
         ((256, 1024), BF16), ((256, 1024), F32), ((3, 64, 512), F32), ((3, 4, 8), F32), ((64, 512), F32), ((2, 64), F32),
         ((4, 64), F32), ((64, 2048), F32), ((4, 32), F32), ((64, 2048), F32), ((8, 64), F32),
     )
-    scratch += [vm(*result) for result in results]
-    scratch += [vm((2, 8, 1024), F32), vm((3, 8, 2, 64, 256))] + [vm((8, 2, 64, n)) for n in widths[1:]]
+    scratch += [vm(*result) for result in results] + [vm((2, 8, 1024), F32)]
+    scratch += [vm((3, 8, 2, 64, 256)), vm((4, 8, 2, 64, 256)), vm((8, 2, 64, 1024)), vm((8, 2, 64, 1024))]
     scratch += [vm((8, 2, 32, 128)), vm((256, 256)), vm((512, 1024)), vm((128, 1024))]
     scratch += [vm((3, 512, 256)), vm((2, 512, 256))] + [vm((2, 512, 256), F32)] * 3
-    scratch += [vm((4, 128, 1024), F32), vm((4, 512, 512))] + [vm((512, 256), F32)] * 3 + [vm((512, 256))]
-    scratch += [vm((4, 128, 1024))] + [vm((3, 128, 1024))] * 4
+    scratch += [vm((4, 128, 1024), F32), vm((4, 512, 512))] + [vm((512, 256), F32)] * 3 + [vm((4, 128, 256))] * 2
+    scratch += [vm((4, 128, 1024))] + [vm((3, 128, 1024))] * 3
     scratch += [vm((4, 128, 1024)), vm((512, 1024)), vm((512, 1024), F32)]
-    scratch += [vm((4, 128, 1024)), vm((512, 1024)), vm((4, 128, 1024))]
+    scratch += [vm((4, 128, 1024)), vm((512, 1024)), vm((4, 128, 1024)), vm((512, 1024), F32)]
     scratch += [vm((128, 1024), F32)] * 2 + [vm((128, 128), F32), vm((128, 1024), F32)]
-    scratch += [vm((512, 256))] * 2 + [vm((512, 512))] * 2 + [vm((2, 512, 256), F32), vm((512, 256), F32)]
-    scratch += [vm((3, 512, 256)), vm((512, 512)), vm((256, 256)), vm((24, 1024), F32)]
+    scratch += [vm((4, 128, 256))] * 2 + [vm((16, 128)), vm((512, 512)), vm((256, 256)), vm((24, 1024), F32)]
+    scratch += [vm((512, 256))] * 2 + [vm((512, 512)), vm((4, 512, 512)), vm((2, 512, 256), F32), vm((512, 256), F32)]
+    scratch += [vm((3, 512, 256))]
     scratch += [vm((4, 2, 2, 64, n)) for n in widths]
-    scratch += [vm((4, 2, 64, n)) for n in widths] * 2
-    scratch += [vm((4, 2, 64, n)) for n in widths] + [vm((2, 64, n)) for n in widths]
-    scratch += [vm((2, 64, 1024), F32), vm((4, 64, 1024))] + [vm((64, n)) for n in widths]
+    scratch += [vm((4, 2, 64, n)) for n in widths] * 2 + [vm((2, 64, n)) for n in widths]
+    scratch += [vm((2, 64, 1024), F32)] + [vm((64, n)) for n in widths] * 2
     scratch += [vm((8, 1024), F32), vm((3, 8, 1024), F32), vm((16, 1024), F32), vm((6, 16, 1024), F32)]
     scratch += [vm((128, 1024)), vm((128, 1024)), vm((256, 1024))]
-    scratch += [pltpu.SemaphoreType.DMA((320,)), pltpu.SemaphoreType.DMA((320,)), pltpu.SemaphoreType.DMA((40,))]
+    scratch += [pltpu.SemaphoreType.DMA((400,)), pltpu.SemaphoreType.DMA((400,)), pltpu.SemaphoreType.DMA((40,))]
 
     shapes = tuple(jax.ShapeDtypeStruct(*result) for result in results)
     anywhere = pl.BlockSpec(memory_space=pl.ANY)

time: 192 us -> 166 us (0.86)
  Pallas kernels: 190 us -> 165 us
    pallas_call x1, Pallas kernels: 187 us -> 161 us  [fast_local(): pl.pallas_call(layer_kernel, out_shape=shapes, in_specs=[anywhere] * 13,...]
where the time goes in v3:
time: 166 us
  Pallas kernels  165 us (99%)
    pallas_call x1, Pallas kernels, fast_local(): pl.pallas_call(layer_kernel, out_shape=shapes, in_specs=[anywhere] * 13,...  161 us

profile of v3, /device:TPU:0, one launch (start us, length us, event | category | flops | bytes accessed | tf_op | source)
XLA Modules:
  0.0 166.0 jit_solution(3162916372542240951)
XLA Ops:
  1.3 161.5 %layer.1 = (bf16[256,1024]{1,0:T(8,128)(2,1)}, f32[256,1024]{1,0:T(8,128)}, f32[3,64,512]{2,1,0:T(8,128)}, f32[3,4,8]{2,1,0:T(4,128)}, f32[64,512]{1,0:T(8,128)}...) custom-call(bf16[256,1024]{1,0:T(8,128)(2,1)} %tok.1, ...), custom_call_target="tpu_custom_call" | custom-call | tf_op jit(solution)/shard_map/layer/pallas_call | solution.py:1340
  162.8 3.1 %results.1 = (bf16[256,1024]{1,0:T(8,128)(2,1)}, f32[256,1024]{1,0:T(8,128)}, f32[3,64,512]{2,1,0:T(8,128)}, f32[3,4,8]{2,1,0:T(4,128)}, f32[64,512]{1,0:T(8,128...) custom-call(bf16[256,1024]{1,0:T(8,128)(2,1)} %get-tuple-element.33., ...), custom_call_target="tpu_custom_call" | custom-call | tf_op jit(solution)/shard_map/results/pallas_call | solution.py:1354

commit v4 on v3

--- a/solution.py
+++ b/solution.py
@@ -403,6 +403,7 @@
 
 MESH = pl.DeviceIdType.MESH
 PLANES = 4
+SENDS, RECEIVES = 84, 204
 F32 = jnp.float32
 BF16 = jnp.bfloat16
 SCALE = HEAD ** (-0.25)
@@ -439,7 +440,7 @@
     tok, wq_h, qb_h, wo_h, gain_h, bias_h, wu_h, ub_h, wd_h, rpe_h, om_h, bk_h, cot,
     mixed_h, gtok_h, gq_h, gqb_h, go_h, ggain_h, gbias_h, gu_h, gub_h, gd_h, grpe_h,
     qb_v, gain_v, bias_v, ub_v, rpe_v, om_v, bk_v, small_s, om_s,
-    mixed_o, gtok_o, gq_o, gqb_o, go_o, ggain_o, gbias_o, gu_o, gub_o, gd_o, grpe_o, tvec_o,
+    mixed_o, gtok_o, gq_o, gqb_o, go_o, ggain_o, gbias_o, gu_o, gub_o, gd_o, grpe_o,
     wq, wo, wu, wd, small, om2, xg, cotb,
     qkv, phi, ex, unit, inv, r0, pp, num, den, quo, att, attf,
     pb, rb_f, rb_d, rb_i, fb, hid, dgel, efb, dub, dzb, acc,
@@ -447,13 +448,13 @@
     dn, dd, ds_, gg, dph, dvv, dqkv,
     g_k, g_v, g_o, g_u, g_d, r_k, r_v, r_o, r_u, r_d, rz_k, rz_v, rz_o, rz_u, rz_d, cb_k, cb_v, cb_o, cb_u, cb_d,
     fs, xs_k, xs_v, xs_o, xs_u, xs_d, xr_k, xr_v, xr_o, xr_u, xr_d,
-    sd, sd_r, st, st_r, mix_s, gt_s, gt_r,
+    sd, sd_r, st_a, st_b, work_a, work_b, mix_s, gt_r,
     ss, rs, ls,
 ):
     dp, y, c = lax.axis_index("dp"), lax.axis_index("heads"), lax.axis_index("feat")
     z, x = dp // 2, dp % 2
     shard = 2 * dp + c
-    sems, locals_ = Sems(), Sems()
+    s_sems, r_sems, locals_ = Sems(), Sems(), Sems()
     pending = []
 
     def bring(src, dst, cond=None):
@@ -517,6 +518,12 @@
     def got(dst, r):
         rc(dst, dst, r, r, sib).wait_recv()
 
+    def take(count=1):
+        return s_sems.take(count), r_sems.take(count)
+
+    def give(src, dst, pair, device, cond=None, s=0, r=0):
+        send(src, dst, pair[0] + s, pair[1] + r, device, cond)
+
     def valid(dz):
         return jnp.logical_and(z + dz >= 0, z + dz < PLANES)
 
@@ -529,8 +536,8 @@
             found.append(block)
         return found
 
-    arrive = by_plane(((0, 1, 2, 3), (1, 0, 2, 3), (2, 1, 3, 0), (3, 2, 1, 0)))
-    leave = by_plane(((3, 2, 1, 0), (3, 2, 0, 1), (0, 1, 3, 2), (0, 1, 2, 3)))
+    arrive = by_plane(((0, 1, 2, 3), (1, 2, 3, 0), (2, 1, 0, 3), (3, 2, 1, 0)))
+    leave = by_plane(((3, 2, 1, 0), (0, 3, 2, 1), (3, 0, 1, 2), (0, 1, 2, 3)))
 
     def at_step(blocks, k):
         block = blocks[0]
@@ -542,51 +549,60 @@
         return pl.ds(pl.multiple_of(n * 256, 256), 256)
 
     barrier = pltpu.get_barrier_semaphore()
-    for other in (sib, xn, yn, dg, xs_dev, ds_dev):
+    for other in (sib, xn, yn, dg, xs_dev, ds_dev, dev(z, x, 1 - y, 1 - c)):
         pl.semaphore_signal(barrier, inc=1, device_id=other, device_id_type=MESH)
     for zz in range(PLANES):
         @pl.when(z != zz)
         def _(zz=zz):
             pl.semaphore_signal(barrier, inc=1, device_id=dev(zz, x, y, c), device_id_type=MESH)
-    pl.semaphore_wait(barrier, 9)
+    pl.semaphore_wait(barrier, 10)
 
     class Item:
         def __init__(self, ref, kind):
             self.ref, self.kind = ref, kind
-            self.zs, self.fw, self.sb = sems.take(PLANES), sems.take(), sems.take(PLANES)
+            self.z_out, self.c_out = s_sems.take(), s_sems.take()
+            self.zs, self.sb = r_sems.take(PLANES), r_sems.take(PLANES)
 
         def block(self, zz, cc):
             if self.kind == "both":
                 return self.ref.at[pl.ds(2 * zz, 2), cc]
-            return self.ref.at[:, 2 * zz + (x if self.kind == "own" else 1 - x), cc]
+            at = 2 * zz + (x if self.kind == "own" else 1 - x)
+            return self.ref.at[:, at, cc] if len(self.ref.shape) == 5 else self.ref.at[at, cc]
+
+        def some(self, count):
+            if self.kind == "both":
+                return self.ref.at[pl.ds(0, count)]
+            return self.ref.at[:, pl.ds(0, count), 0] if len(self.ref.shape) == 5 else self.ref.at[pl.ds(0, count), 0]
+
+        def onward(self, n, step):
+            here = self.block(n, c)
+            rc(here, here, self.z_out, self.zs + n, dev(z + step, x, y, c)).start()
 
         def start(self):
+            pl.when(z == 0)(lambda: self.onward(z, 2))
+            pl.when(z == 3)(lambda: self.onward(z, -2))
+            pl.when(z > 0)(lambda: self.onward(z, -1))
+            pl.when(z < PLANES - 1)(lambda: self.onward(z, 1))
             mine = self.block(z, c)
-            for dz in (1, -1, 2, -2):
-                send(mine, mine, self.zs + z + dz, self.zs + z, dev(z + dz, x, y, c), valid(dz))
-            send(mine, mine, self.sb + z, self.sb + z, sib)
+            rc(mine, mine, self.c_out, self.sb + z, sib).start()
 
         def pump_step(self, n):
             here = self.block(n, c)
-
-            def relay(device):
-                rc(here, here, self.fw, self.zs + n, device).start()
 
             @pl.when(n != z)
             def _():
                 got(here, self.zs + n)
-                pl.when(jnp.logical_and(z == 1, n == 3))(lambda: relay(dev(z - 1, x, y, c)))
-                pl.when(jnp.logical_and(z == 2, n == 0))(lambda: relay(dev(z + 1, x, y, c)))
-                rc(here, here, self.sb + n, self.sb + n, sib).start()
+                pl.when(jnp.logical_and(z == 1, n > z))(lambda: self.onward(n, -1))
+                pl.when(jnp.logical_and(z == 2, n < z))(lambda: self.onward(n, 1))
+                rc(here, here, self.c_out, self.sb + n, sib).start()
 
         def pump_done(self):
-            mine = self.block(z, c)
-            pending.append(
-                lambda: pl.when((z == 1) | (z == 2))(lambda: rc(mine, mine, self.fw, self.fw, sib).wait_send())
-            )
-            for dz in (1, -1, 2, -2, 3, -3):
-                i = self.sb + z + dz
-                pending.append(lambda i=i, dz=dz: pl.when(valid(dz))(lambda: rc(mine, mine, i, i, sib).wait_send()))
+            def sent(sem, count):
+                rc(self.some(count), self.some(count), sem, 0, sib).wait_send()
+
+            pending.append(lambda: sent(self.c_out, 4))
+            pending.append(lambda: pl.when((z == 0) | (z == 3))(lambda: sent(self.z_out, 2)))
+            pending.append(lambda: pl.when((z == 1) | (z == 2))(lambda: sent(self.z_out, 4)))
 
         def pump(self):
             for k in range(1, PLANES):
@@ -606,22 +622,26 @@
         return ref.at[:, 2 * z + xx, c] if len(ref.shape) == 5 else ref.at[2 * z + xx, c]
 
     def give_half(name, src, ref):
-        i = sems.take()
-        half_of[name] = (ref, i)
-        send(src, place(ref, x), i, i, xn)
+        i = take()
+        half_of[name] = (ref, i[1])
+        give(src, place(ref, x), i, xn)
 
     def have_half(name):
         ref, i = half_of[name]
         got(place(ref, 1 - x), i)
 
     wo_own = wo.at[own_block]
-    i_oh = sems.take()
-    send(
-        wo_h.at[:, half_cols(1 - x, 256)], wo.at[2 * (1 - x) + y, 2 * z + x, c], i_oh, i_oh, xn
-    )
+    i_oh = take()
+    give(wo_h.at[:, half_cols(1 - x, 256)], wo.at[2 * (1 - x) + y, 2 * z + x, c], i_oh, xn)
     give_half("q", wq_h.at[:, :, half_cols(1 - x, 256)], wq)
+    i_tok, i_tx, i_ty = take(), take(2), take(2)
+    give(tok, xg.at[rows_of(c, 256)], i_tok, sib, away)
+    give(tok.at[rows_of(y, 128)], xg.at[rows_of(2 * c + y, 128)], i_tx, dev(z, 1 - x, y, x), None, 0, c)
+    it_oa, it_ob = Item(wo_own, "own"), Item(wo_own, "other")
     it_qa, it_s, it_qb = Item(wq, "own"), Item(small, "both"), Item(wq, "other")
-    it_o, it_u, it_d = Item(wo_own, "both"), Item(wu, "both"), Item(wd, "both")
+    it_ua, it_ub, it_da, it_db = Item(wu, "own"), Item(wu, "other"), Item(wd, "own"), Item(wd, "other")
+    in_o()
+    it_oa.start()
     in_q()
     it_qa.start()
 
@@ -659,37 +679,48 @@
     for h in range(4):
         sel = pick((32, 256), lambda k, l: l == h * 64 + c * 32 + k).astype(BF16)
         om_s[h * 64 : (h + 1) * 64] = dot(om_v[4 * x + h], sel, TN).astype(BF16)
-    i_om = sems.take()
-    send(om_s, om2, i_om, i_om, sib)
-    t1, t2 = sems.take(), sems.take(2)
-    send(tok, xg.at[rows_of(c, 256)], t1, t1, sib, away)
-    send(tok, xg.at[rows_of(c, 256)], t2 + c, t2 + c, dev(z, 1 - x, y, x))
+    i_om = take()
+    give(om_s, om2, i_om, sib)
     give_half("u", wu_h.at[:, half_cols(1 - x, 1024)], wu)
 
     same = (iota((256, 256), 0) // HEAD) == (iota((256, 256), 1) // HEAD)
     ones64[...] = jnp.where(same, 1.0, 0.0).astype(BF16)
     anti[...] = jnp.where(iota((512, 512), 0) + iota((512, 512), 1) == 511, 1.0, 0.0).astype(BF16)
 
+    got(wo.at[own_block, 2 * z + 1 - x, c], i_oh[1])
+    it_ob.start()
     have_half("q")
     it_qb.start()
-    got(wo.at[own_block, 2 * z + 1 - x, c], i_oh)
-    in_o()
-    it_o.start()
+    it_oa.pump()
+    it_qa.pump()
+    it_ob.pump()
+    i_oq, i_os = take(3), take(3)
+    quarter = wo.at[own_block, :, c]
+    give(quarter, quarter, i_oq, yn, None, 2, 2)
+    give(quarter, quarter, i_oq, xn, None, 1, 1)
     have_half("s")
     it_s.start()
-    it_qa.pump()
+    in_u()
+    it_ua.start()
+
+    @pl.when(away)
+    def _():
+        for f in range(2):
+            got(xg.at[rows_of(2 * f + y, 128)], i_tx[1] + f)
+
+    for f in range(2):
+        part = xg.at[rows_of(2 * f + y, 128)]
+        give(part, part, i_ty, yn, away, f, f)
     it_qb.pump()
-    it_o.pump()
-    i_oq, i_os = sems.take(3), sems.take(3)
-    quarter = wo.at[own_block, :, c]
-    for slot in range(3):
-        send(quarter, quarter, i_oq + slot, i_oq + slot, plane[slot])
-    give_half("d", wd_h.at[:, half_cols(1 - x, 1024)], wd)
-    t3 = sems.take()
-    send(cot.at[rows_of(y, 128)], cotb, t3, t3, xs_dev, away)
     have_half("u")
-    in_u()
-    it_u.start()
+    it_ub.start()
+
+    def other_quarter(slot):
+        part = wo.at[plane_block[slot], :, c]
+        got(part, i_oq[1] + slot)
+        give(part, part, i_os, sib, None, slot, slot)
+        return part
+
     it_s.pump()
 
     it_s.need()
@@ -723,13 +754,16 @@
     den[...] = jnp.zeros_like(den)
 
     in_tok()
-    pl.when(home)(lambda: got(xg.at[rows_of(1 - c, 256)], t1))
+    pl.when(home)(lambda: got(xg.at[rows_of(1 - c, 256)], i_tok[1]))
 
     @pl.when(away)
     def _():
-        got(xg.at[pl.ds(0, 256)], t2)
-        got(xg.at[pl.ds(256, 256)], t2 + 1)
-
+        for f in range(2):
+            got(xg.at[rows_of(2 * f + 1 - y, 128)], i_ty[1] + f)
+
+    other_quarter(2)
+    part = other_quarter(1)
+    give(part, part, i_oq, yn, None, 0, 0)
     it_qa.need()
     it_qb.need()
 
@@ -738,7 +772,7 @@
         return carry
 
     lax.fori_loop(0, 3, qkv_body, 0)
-    got(om2, i_om)
+    got(om2, i_om[1])
     om2[...] = om2[...] + om_s[...]
 
     def feature_body(t, carry):
@@ -755,6 +789,7 @@
         return carry
 
     lax.fori_loop(0, 2, feature_body, 0)
+    it_ua.pump()
     lane_head = iota((1, 128), 1) // HEAD
 
     def head_cols(h):
@@ -777,22 +812,22 @@
     quo[...] = num[...] / den[...]
     att[...] = quo[...].astype(BF16).reshape(4, 128, 256)
 
-    i_at = sems.take(3)
+    i_at = take(3)
     for slot in range(3):
-        send(att.at[plane_block[slot]], attf.at[own_block], i_at + slot, i_at + slot, plane[slot])
+        give(att.at[plane_block[slot]], attf.at[own_block], i_at, plane[slot], None, slot, slot)
     attf[own_block] = att[own_block]
+    in_d()
+    it_da.start()
+    other_quarter(0)
+    give_half("d", wd_h.at[:, half_cols(1 - x, 1024)], wd)
+    i_cot = take()
+    give(cot.at[rows_of(y, 128)], cotb, i_cot, xs_dev, away)
+    it_oa.need()
+    it_ob.need()
     for slot in range(3):
-        part = wo.at[plane_block[slot], :, c]
-        got(part, i_oq + slot)
-        send(part, part, i_os + slot, i_os + slot, sib)
-    have_half("d")
-    in_d()
-    it_d.start()
-    it_o.need()
+        got(wo.at[plane_block[slot], :, 1 - c], i_os[1] + slot)
     for slot in range(3):
-        got(attf.at[plane_block[slot]], i_at + slot)
-    for slot in range(3):
-        got(wo.at[plane_block[slot], :, 1 - c], i_os + slot)
+        got(attf.at[plane_block[slot]], i_at[1] + slot)
 
     def out_body(q, carry):
         return carry + dot(attf[q], wo[q].reshape(1024, 256), NT)
@@ -811,48 +846,74 @@
 
     class Scatter:
         def __init__(self, ref):
-            self.ref, self.base = ref, sems.take(12)
+            self.ref, self.out, self.base = ref, s_sems.take(), r_sems.take(4)
 
         def part(self, n, value):
             cols = cols256(n)
             pb[:, :, cols] = value.astype(BF16).reshape(4, 128, 256)
             for slot in range(3):
-                i = self.base + slot * 4 + n
-                rc(pb.at[plane_block[slot], :, cols], self.ref.at[slot, :, cols], i, i, plane[slot]).start()
+                rc(
+                    pb.at[plane_block[slot], :, cols], self.ref.at[slot, :, cols], self.out, self.base + n, plane[slot]
+                ).start()
+
+        def column(self, n):
+            cols = slice(n * 256, (n + 1) * 256)
+            got(self.ref.at[:, :, cols], self.base + n)
+            value = pb[own_block, :, cols].astype(F32)
+            for slot in range(3):
+                value = value + self.ref[slot, :, cols].astype(F32)
+            return value
 
         def total(self):
-            for n in range(4):
-                for slot in range(3):
-                    got(self.ref.at[slot, :, n * 256 : (n + 1) * 256], self.base + slot * 4 + n)
-            value = pb[own_block].astype(F32)
-            for slot in range(3):
-                value = value + self.ref[slot].astype(F32)
-            return value
+            return jnp.concatenate([self.column(n) for n in range(4)], axis=1)
 
         def sent(self):
-            for slot in range(3):
-                for n in range(4):
-                    i = self.base + slot * 4 + n
-                    src = pb.at[plane_block[slot], :, n * 256 : (n + 1) * 256]
-                    rc(src, src, i, i, plane[slot]).wait_send()
+            rc(self.ref, self.ref, self.out, 0, sib).wait_send()
 
     class Gather:
         def __init__(self, ref, order):
-            self.ref, self.base, self.order = ref, sems.take(12), order
+            self.ref, self.out, self.base, self.order = ref, s_sems.take(), r_sems.take(4), order
+            pending.append(lambda: rc(ref.at[pl.ds(0, 3)], ref.at[pl.ds(0, 3)], self.out, 0, sib).wait_send())
 
         def start(self):
             for n in self.order:
                 for slot in range(3):
                     mine = self.ref.at[own_block, :, cols256(n)]
-                    i = self.base + slot * 4 + n
-                    send(mine, mine, i, i, plane[slot])
+                    rc(mine, mine, self.out, self.base + n, plane[slot]).start()
 
         def need(self, n):
-            for slot in range(3):
-                got(self.ref.at[plane_block[slot], :, cols256(n)], self.base + slot * 4 + n)
+            got(self.ref.at[pl.ds(0, 3), :, cols256(n)], self.base + n)
+
+    class RelayGather:
+        def __init__(self, ref, order):
+            self.ref, self.out, self.base, self.order = ref, s_sems.take(), r_sems.take(12), order
+            pending.append(lambda: rc(ref.at[pl.ds(0, 3)], ref.at[pl.ds(0, 3)], self.out, 0, sib).wait_send())
+
+        def piece(self, slot, n):
+            return self.ref.at[plane_block[slot], :, cols256(n)]
+
+        def start(self):
+            for n in self.order:
+                mine = self.ref.at[own_block, :, cols256(n)]
+                for slot in (1, 2):
+                    rc(mine, mine, self.out, self.base + slot * 4 + n, plane[slot]).start()
+
+        def pass_on(self, k):
+            n, slot = self.order[k], 1 + k % 2
+            part = self.piece(slot, n)
+            got(part, self.base + slot * 4 + n)
+            rc(part, part, self.out, self.base + n, plane[3 - slot]).start()
+
+        def need(self, k):
+            n, slot = self.order[k], 2 - k % 2
+            got(self.piece(slot, n), self.base + slot * 4 + n)
+            got(self.piece(0, n), self.base + n)
 
     g_first = Gather(fb, range(4))
     g_first.start()
+    it_ub.pump()
+    have_half("d")
+    it_db.start()
     fst[...] = first
     n1[...] = normed
     i1[...] = jnp.broadcast_to(inverse, (128, 128))
@@ -861,8 +922,8 @@
         return ref[:, :, cols256(m)].reshape(512, 256)
 
     acc[...] = jnp.zeros_like(acc)
-    it_u.pump()
-    it_u.need()
+    it_ua.need()
+    it_ub.need()
 
     def hidden_part(n, carry):
         g_first.need(n)
@@ -872,7 +933,9 @@
             acc[:, cols] += dot(left, wu[pl.ds(2 * n, 2), :, :, cols].reshape(256, 256))
         return carry
 
-    lax.fori_loop(0, 4, hidden_part, 0)
+    lax.fori_loop(0, 2, hidden_part, 0)
+    it_da.pump()
+    lax.fori_loop(2, 4, hidden_part, 0)
 
     def hidden_body(n, carry):
         cols = cols256(n)
@@ -887,14 +950,15 @@
 
     def down_part(k, carry):
         n = at_step(arrive, k)
-        it_d.pump_step(n)
-        it_d.need_step(n)
+        it_db.pump_step(n)
+        it_da.need_step(n)
+        it_db.need_step(n)
         sc_f.part(n, dot(hid[...], wd[pl.ds(2 * n, 2)].reshape(256, 1024), NT))
         return carry
 
     lax.fori_loop(0, 4, down_part, 0)
-    it_d.pump_done()
-    pl.when(away)(lambda: got(cotb, t3))
+    it_db.pump_done()
+    pl.when(away)(lambda: got(cotb, i_cot[1]))
     in_cot()
     upstream = cotb[...].astype(F32)
 
@@ -916,69 +980,76 @@
     efb[own_block] = err.astype(BF16)
     g_ef = Gather(efb, leave)
     g_ef.start()
+    mix_s[...] = (normed2 * rows_v[1:2, :] + rows_v[5:6, :]).astype(BF16)
     dr[...] = err
-    mix_s[...] = (normed2 * rows_v[1:2, :] + rows_v[5:6, :]).astype(BF16)
     sd[1:2, :] = down(upstream * normed2)
     sd[4:5, :] = down(err.astype(BF16).astype(F32))
     sc_f.sent()
 
-    i_mix, i_gt = sems.take(2), sems.take(2)
-
-    def to_owner(src, dst, i):
-        rows = rows_of(y, 128)
-
-        @pl.when(home)
-        def _():
-            dst[rows] = src[...]
-
-        send(src, dst.at[rows], i + 1, i + 1, yn, home)
-        send(src, dst.at[rows], i, i + y, xs_dev, away)
-        send(src, dst.at[rows], i + 1, i + y, ds_dev, away)
-
-    def from_owner(dst, i):
-        for half in range(2):
-            part = dst.at[half * 128 : (half + 1) * 128]
-
-            @pl.when(jnp.logical_and(home, y != half))
-            def _(part=part):
-                got(part, i + 1)
-
-            @pl.when(away)
-            def _(part=part, half=half):
-                got(part, i + half)
+    class Owner:
+        def __init__(self, dst, pieces):
+            self.dst, self.width = dst, 1024 // pieces
+            self.ids = [take(2) for _ in range(pieces)]
+
+        def part(self, half, n):
+            return self.dst.at[rows_of(half, 128), n * self.width : (n + 1) * self.width]
+
+        def start(self, src, n):
+            cols = slice(n * self.width, (n + 1) * self.width)
+
+            @pl.when(home)
+            def _():
+                self.dst[rows_of(y, 128), cols] = src[:, cols]
+
+            give(src.at[:, cols], self.part(y, n), self.ids[n], yn, home, 1, 1)
+            give(src.at[:, cols], self.part(y, n), self.ids[n], xs_dev, away, 0, 0)
+
+        def pass_on(self, n):
+            part = self.part(y, n)
+            pl.when(away)(lambda: got(part, self.ids[n][1]))
+            give(part, part, self.ids[n], yn, away, 1, 1)
+
+        def need(self, n):
+            got(self.part(1 - y, n), self.ids[n][1] + 1)
+
+    own_mix = Owner(mixed_o, 1)
+    own_mix.start(mix_s, 0)
 
     class Grad:
         def __init__(self, g, r, rz, cb, xs, xr):
             self.g, self.r, self.rz, self.cb, self.xs, self.xr = g, r, rz, cb, xs, xr
-            self.d, self.z, self.k, self.x = sems.take(4), sems.take(PLANES), sems.take(), sems.take()
+            self.d, self.z, self.k, self.x = r_sems.take(4), r_sems.take(PLANES), r_sems.take(2), take()
+            self.d_out, self.z_out = s_sems.take(), s_sems.take()
             self.width = r.shape[-1]
 
         def give(self, m):
-            i = self.d + m
-            rc(self.g.at[m, :, 1 - c], self.r.at[m], i, i, sib).start()
+            rc(self.g.at[m, :, 1 - c], self.r.at[m], self.d_out, self.d + m, sib).start()
 
         def pair_step(self, m):
             got(self.r.at[m], self.d + m)
             self.r[m] = (self.g[m, :, c].astype(F32) + self.r[m].astype(F32)).astype(BF16)
             far = jnp.abs(m - z)
             part = self.r.at[m]
-
-            def out(device):
-                rc(part, self.rz.at[z], self.z + m, self.z + z, device).start()
-
-            pl.when(far == 1)(lambda: out(dev(m, x, y, c)))
-            pl.when(jnp.logical_and(far == 2, (z == 0) | (z == 3)))(lambda: out(dev(m, x, y, c)))
-            pl.when(far == 3)(
-                lambda: rc(part, self.cb, self.k, self.k, dev(jnp.where(z == 0, 1, 2), x, y, c)).start()
-            )
+            outer = (z == 0) | (z == 3)
+            beside = dev(jnp.where(z == 0, 1, jnp.where(z == 1, 0, jnp.where(z == 2, 3, 2))), x, y, c)
+
+            @pl.when(jnp.logical_or(outer, m == jnp.where(z == 1, 0, 3)) & (far == 1))
+            def _():
+                rc(part, self.rz.at[z], self.z_out, self.z + z, beside).start()
+
+            for slot in range(2):
+                @pl.when(outer & (far == 3 - slot))
+                def _(slot=slot):
+                    rc(part, self.cb.at[slot], self.z_out, self.k + slot, beside).start()
 
         def relay(self):
-            for at, m in ((1, 3), (2, 0)):
+            for at, blocks in ((1, (3, 2)), (2, (0, 1))):
                 @pl.when(z == at)
-                def _(at=at, m=m):
-                    got(self.cb, self.k)
-                    self.r[m] = (self.r[m].astype(F32) + self.cb[...].astype(F32)).astype(BF16)
-                    rc(self.r.at[m], self.rz.at[at], self.z + m, self.z + at, dev(m, x, y, c)).start()
+                def _(at=at, blocks=blocks):
+                    for slot, m in enumerate(blocks):
+                        got(self.cb.at[slot], self.k + slot)
+                        self.r[m] = (self.r[m].astype(F32) + self.cb[slot].astype(F32)).astype(BF16)
+                        rc(self.r.at[m], self.rz.at[at], self.z_out, self.z + at, dev(m, x, y, c)).start()
 
         def run(self, make):
             def body(k, carry):
@@ -995,22 +1066,17 @@
             total = fs.at[:, :, 0 : self.width]
             total[...] = self.r[z].astype(F32)
             for dz in (1, -1, 2, -2):
-                @pl.when(valid(dz))
+                @pl.when(valid(dz) if abs(dz) == 1 else z == (0 if dz > 0 else 3))
                 def _(dz=dz):
                     got(self.rz.at[z + dz], self.z + z + dz)
                     total[...] += self.rz[z + dz].astype(F32)
             self.xs[...] = fs[1 - x, :, 0 : self.width].astype(BF16)
-            send(self.xs, self.xr, self.x, self.x, xn)
+            give(self.xs, self.xr, self.x, xn)
 
         def sent(self):
-            for m in range(PLANES):
-                i = self.d + m
-                rc(self.g.at[m, :, c], self.g.at[m, :, c], i, i, sib).wait_send()
-            part = self.r.at[0]
-            for dz in (1, -1, 2, -2):
-                i = self.z + z + dz
-                pl.when(valid(dz))(lambda i=i: rc(part, part, i, i, sib).wait_send())
-            pl.when((z == 0) | (z == 3))(lambda: rc(part, part, self.k, self.k, sib).wait_send())
+            rc(self.r, self.r, self.d_out, 0, sib).wait_send()
+            part = self.r.at[pl.ds(0, 3)]
+            rc(part, part, self.z_out, 0, sib).wait_send()
 
         def columns(self, out, half, value, at=0):
             if len(out.shape) == 3:
@@ -1023,7 +1089,7 @@
             self.columns(out, x, fs[x, :, 0 : self.width], at)
 
         def write_other(self, out, at=0):
-            got(self.xr, self.x)
+            got(self.xr, self.x[1])
             self.columns(out, 1 - x, self.xr[...].astype(F32), at)
 
     gr_d = Grad(g_d, r_d, rz_d, cb_d, xs_d, xr_d)
@@ -1040,11 +1106,10 @@
         for j in range(4):
             cols = slice(j * 256, (j + 1) * 256)
             acc[:, cols] += dot(left, wd[pl.ds(2 * m, 2), :, :, cols].reshape(256, 256))
+        gr_d.pair_step(m)
 
     def down_grads(k, carry):
-        m = at_step(leave, k)
-        make_down(m)
-        pl.when(k > 0)(lambda: gr_d.pair_step(at_step(leave, k - 1)))
+        make_down(at_step(leave, k))
         return carry
 
     lax.fori_loop(0, PLANES, down_grads, 0)
@@ -1052,7 +1117,7 @@
         cols = cols256(n)
         du = (acc[:, cols] * dgel[:, cols]).astype(BF16)
         dub[:, cols] = du
-        st[0:1, cols] = down(du.astype(F32))
+        st_a[6:7, cols] = down(du.astype(F32))
         return carry
 
     lax.fori_loop(0, 4, du_body, 0)
@@ -1063,14 +1128,13 @@
         return carry
 
     lax.fori_loop(0, 4, back_part, 0)
-    gr_d.pair_step(leave[3])
+    own_mix.pass_on(0)
 
     def make_up(m):
         g_u[m] = dot(d_cols(fb, m), dub[...], TN).astype(BF16).reshape(2, 2, 64, 1024)
 
+    gr_d.relay()
     gr_u.run(make_up)
-    gr_d.relay()
-    to_owner(mix_s, mixed_o, i_mix)
     dfirst = dr[...] + sc_d.total()
     back = norm_back(dfirst, n1[...], i1[:, 0:1], rows_v[0:1, :])
     dz = back.astype(BF16)
@@ -1081,25 +1145,60 @@
         return carry
 
     lax.fori_loop(0, 4, dattn_body, 0)
-    i_da = sems.take(3)
+    i_da = take(3)
     for slot in range(3):
-        send(dat_s.at[plane_block[slot]], dat.at[own_block], i_da + slot, i_da + slot, plane[slot])
+        give(dat_s.at[plane_block[slot]], dat.at[own_block], i_da, plane[slot], None, slot, slot)
     dat[own_block] = dat_s[own_block]
-    g_dz = Gather(dzb, leave)
+    g_dz = RelayGather(dzb, leave)
     g_dz.start()
     sd[0:1, :] = down(dfirst * n1[...])
     sd[3:4, :] = down(dfirst)
     sd[2:3, :] = down(dz.astype(F32))
     sd[6:8, :] = jnp.zeros((2, 1024), F32)
-    i_sd = sems.take(3)
+    class Total:
+        def __init__(self, ref, work):
+            self.ref, self.work = ref, work
+            self.c, self.z, self.h = take(), take(PLANES), take()
+
+        def pair(self):
+            give(self.ref, self.work.at[0], self.c, sib)
+
+        def over_planes(self):
+            got(self.work.at[0], self.c[1])
+            self.work[1] = self.ref[...] + self.work[0]
+            for zz in range(PLANES):
+                give(self.work.at[1], self.work.at[2 + z], self.z, dev(zz, x, y, c), z != zz, zz, z)
+
+        def finish(self):
+            total = self.work[1]
+            for zz in range(PLANES):
+                @pl.when(z != zz)
+                def _(zz=zz):
+                    got(self.work.at[2 + zz], self.z[1] + zz)
+
+                @pl.when(z == zz)
+                def _(zz=zz):
+                    self.work[2 + zz] = jnp.zeros((8, 1024), F32)
+                total = total + self.work[2 + zz]
+            self.work[6] = total
+            give(self.work.at[6], self.work.at[7], self.h, xn)
+
+        def need(self):
+            got(self.work.at[7], self.h[1])
+
+        def of_half(self, half):
+            return jnp.where(x == half, self.work[6], self.work[7])
+
+    early, late = Total(st_a, work_a), Total(st_b, work_b)
+    i_sd = take(3)
     for k, device in enumerate(plane):
-        send(sd, sd_r.at[k], i_sd + k, i_sd + k, device)
+        give(sd, sd_r.at[k], i_sd, device, None, k, k)
     dr[...] = back
     sc_d.sent()
     dph[...] = jnp.zeros_like(dph)
     dvv[...] = jnp.zeros_like(dvv)
     for slot in range(3):
-        got(dat.at[plane_block[slot]], i_da + slot)
+        got(dat.at[plane_block[slot]], i_da[1] + slot)
 
     dattn = dat[...].reshape(512, 256).astype(F32)
     recip = 1.0 / den[...]
@@ -1121,9 +1220,6 @@
 
     def make_v(m):
         g_v[m] = dot(x_cols(m), dqkv[2], TN).astype(BF16).reshape(2, 2, 64, 256)
-
-    gr_v.run(make_v)
-    gr_u.relay()
 
     def head_back(h, carry):
         cols, mine = head_cols(h)
@@ -1141,7 +1237,13 @@
         dph[1, :, cols] += dot(ds_[...], phi[0, :, cols] * keep, TN)
         return carry
 
+    g_dz.pass_on(0)
     lax.fori_loop(0, 4, head_back, 0)
+    g_dz.pass_on(1)
+    g_dz.pass_on(2)
+    gr_v.run(make_v)
+    g_dz.pass_on(3)
+    gr_u.relay()
 
     def feature_back_body(t, carry):
         dlog = (dph[t] * ex[t]).astype(BF16)
@@ -1152,7 +1254,47 @@
         return carry
 
     lax.fori_loop(0, 2, feature_back_body, 0)
-    sc_i = Scatter(rb_i)
+    class Return:
+        def __init__(self, ref):
+            self.ref, self.out, self.base, self.last = ref, s_sems.take(), r_sems.take(4), take(4)
+            pending.append(lambda: pl.when(home)(lambda: rc(ref.at[0:3], ref.at[0:3], self.out, 0, sib).wait_send()))
+            pending.append(lambda: pl.when(away)(lambda: rc(ref, ref, self.out, 0, sib).wait_send()))
+
+        def part(self, n, value):
+            cols = cols256(n)
+            for b in range(4):
+                rows = value[b * 128 : (b + 1) * 128]
+                pb[b, :, cols] = jnp.where(own_block == b, rows + dr[:, cols], rows).astype(BF16)
+                here = home & (c == b // 2) & (y == b % 2)
+
+                @pl.when(here)
+                def _(b=b):
+                    self.ref[own_block, :, cols] = pb[b, :, cols]
+
+                @pl.when(jnp.logical_not(here))
+                def _(b=b):
+                    there = self.ref.at[own_block, :, cols]
+                    rc(pb.at[b, :, cols], there, self.out, self.base + n, dev(z, c, b % 2, b // 2)).start()
+
+        def column(self, n):
+            cols = slice(n * 256, (n + 1) * 256)
+            pl.when(home)(lambda: got(self.ref.at[0:3, :, cols], self.base + n))
+            pl.when(away)(lambda: got(self.ref.at[0:4, :, cols], self.base + n))
+            value = self.ref[0, :, cols].astype(F32)
+            for slot in range(1, 4):
+                value = value + self.ref[slot, :, cols].astype(F32)
+            mine = gt_r.at[rows_of(y, 128), cols]
+            mine[...] = value.astype(BF16)
+            give(mine, mine, self.last, yn, None, n, n)
+            gtok_o[rows_of(y, 128), cols] = value
+
+        def need(self, n):
+            cols = slice(n * 256, (n + 1) * 256)
+            rows = rows_of(1 - y, 128)
+            got(gt_r.at[rows, cols], self.last[1] + n)
+            gtok_o[rows, cols] = gt_r[rows, cols].astype(F32)
+
+    sc_i = Return(rb_i)
 
     def input_part(n, carry):
         value = jnp.zeros((512, 256), F32)
@@ -1162,21 +1304,13 @@
         return carry
 
     lax.fori_loop(0, 4, input_part, 0)
-
-    def make_k(m):
-        for p in range(2):
-            g_k[m, :, :, :, p * 256 : (p + 1) * 256] = (
-                dot(x_cols(m), dqkv[p], TN).astype(BF16).reshape(2, 2, 64, 256)
-            )
-
-    gr_k.run(make_k)
-
-    def make_out(m):
-        g_dz.need(m)
-        g_o[m] = dot(d_cols(dzb, m), att[...].reshape(512, 256), TN).astype(BF16).reshape(2, 2, 64, 256)
-
-    gr_o.run(make_out)
-    gr_v.relay()
+    for k in range(3):
+        got(sd_r.at[k], i_sd[1] + k)
+    st_a[0:6, :] = (sd[...] + sd_r[0] + sd_r[1] + sd_r[2])[0:6]
+    st_a[7:8, :] = jnp.zeros((1, 1024), F32)
+    early.pair()
+    gr_d.finish()
+    gr_d.write_own(gd_o)
 
     def diagonal_body(h, carry):
         flipped = dot(anti[...], gg[h])
@@ -1190,78 +1324,84 @@
             if b < 3:
                 pieces = pieces + [jnp.zeros((1, 384 - 128 * b), F32)]
             sums = sums + jnp.concatenate(pieces, axis=1)
-        st[pl.ds(2 + h, 1), :] = sums
+        st_b[pl.ds(1 + h, 1), :] = sums
         return carry
 
     lax.fori_loop(0, 4, diagonal_body, 0)
     for p in range(3):
-        st[1:2, p * 256 : (p + 1) * 256] = down(dqkv[p].astype(F32))
-    st[1:2, 768:1024] = jnp.zeros((1, 256), F32)
-    st[6:8, :] = jnp.zeros((2, 1024), F32)
-    i_c, i_zz, i_h = sems.take(), sems.take(PLANES), sems.take()
-    for k in range(3):
-        got(sd_r.at[k], i_sd + k)
-    st[8:16, :] = sd[...] + sd_r[0] + sd_r[1] + sd_r[2]
-    send(st, st_r.at[0], i_c, i_c, sib)
-    gr_d.finish()
-    gr_d.write_own(gd_o)
-    got(st_r.at[0], i_c)
-    st_r[1] = st[...] + st_r[0]
-    for zz in range(PLANES):
-        send(st_r.at[1], st_r.at[2 + z], i_zz + zz, i_zz + z, dev(zz, x, y, c), z != zz)
+        st_b[0:1, p * 256 : (p + 1) * 256] = down(dqkv[p].astype(F32))
+    st_b[0:1, 768:1024] = jnp.zeros((1, 256), F32)
+    st_b[5:8, :] = jnp.zeros((3, 1024), F32)
+    late.pair()
+    early.over_planes()
+
+    def make_k(m):
+        for p in range(2):
+            g_k[m, :, :, :, p * 256 : (p + 1) * 256] = (
+                dot(x_cols(m), dqkv[p], TN).astype(BF16).reshape(2, 2, 64, 256)
+            )
+
+    gr_k.run(make_k)
+
+    def make_out(m):
+        g_o[m] = dot(d_cols(dzb, m), att[...].reshape(512, 256), TN).astype(BF16).reshape(2, 2, 64, 256)
+
+    for k in range(4):
+        g_dz.need(k)
+    gr_o.run(make_out)
+
+    late.over_planes()
     outs = []
-    from_owner(mixed_o, i_mix)
+    own_mix.need(0)
     outs.append(bring(mixed_o, mixed_h))
-    gr_k.relay()
-    gr_o.relay()
+    gr_v.relay()
     gr_u.finish()
     gr_u.write_own(gu_o)
-    back = dr[...] + sc_i.total()
-    gt_s[...] = back.astype(BF16)
-    to_owner(gt_s, gt_r, i_gt)
+    early.finish()
+    sc_i.column(0)
+    sc_i.column(1)
+    gr_k.relay()
+    sc_i.column(2)
+    sc_i.column(3)
     gr_d.write_other(gd_o)
     outs.append(bring(gd_o, gd_h))
+    gr_o.relay()
     gr_v.finish()
     gr_v.write_own(gq_o, 2)
-    total = st_r[1]
-    for zz in range(PLANES):
-        @pl.when(z != zz)
-        def _(zz=zz):
-            got(st_r.at[2 + zz], i_zz + zz)
-
-        @pl.when(z == zz)
-        def _(zz=zz):
-            st_r[2 + zz] = jnp.zeros((16, 1024), F32)
-        total = total + st_r[2 + zz]
-    st_r[0] = total
-    tvec_o[x] = total[0:8]
-    send(tvec_o.at[x], tvec_o.at[x], i_h, i_h, xn)
     gr_u.write_other(gu_o)
     outs.append(bring(gu_o, gu_h))
 
     def exact(left, right):
         return lax.dot_general(left, right, NN, precision=lax.Precision.HIGHEST, preferred_element_type=F32)
 
-    own = exact(
-        st_r[0, 8:16, pl.ds(pl.multiple_of(dp * 128, 128), 128)], pick((128, 64), lambda k, l: k == c * 64 + l)
-    )
+    early.need()
+    mine = early.work[6, :, pl.ds(pl.multiple_of(dp * 128, 128), 128)]
+    own = exact(mine, pick((128, 64), lambda k, l: k == c * 64 + l))
     ggain_o[...] = own[0:2]
     gbias_o[...] = own[2:6]
     outs.append(bring(ggain_o, ggain_h))
     outs.append(bring(gbias_o, gbias_h))
+    late.finish()
     gr_k.finish()
     gr_k.write_own(gq_o)
     gr_o.finish()
     gr_o.write_own(go_o)
-    got(tvec_o.at[1 - x], i_h)
+    for n in range(4):
+        sc_i.need(n)
+    outs.append(bring(gtok_o, gtok_h))
+    late.need()
+    ups = [early.of_half(half) for half in range(2)]
+    rest = [late.of_half(half) for half in range(2)]
     tile = pl.ds(pl.multiple_of((7 - dp) * 128, 128), 128)
-    lines = jnp.concatenate([tvec_o[0, 2:6, tile], tvec_o[1, 2:6, tile]], axis=0)
+    sd_r[0] = rest[0]
+    sd_r[1] = rest[1]
+    lines = jnp.concatenate([sd_r[0, 1:5, tile], sd_r[1, 1:5, tile]], axis=0)
     grpe_o[...] = exact(lines, pick((128, 64), lambda k, l: k == (1 - c) * 64 + 63 - l))
     outs.append(bring(grpe_o, grpe_h))
     lines = [
-        tvec_o[half, 1:2, p * 256 + t * 128 : p * 256 + (t + 1) * 128]
+        rest[half][0:1, p * 256 + t * 128 : p * 256 + (t + 1) * 128]
         for p in range(3) for half in range(2) for t in range(2)
-    ] + [tvec_o[half, 0:1, t * 128 : (t + 1) * 128] for half in range(2) for t in range(8)]
+    ] + [ups[half][6:7, t * 128 : (t + 1) * 128] for half in range(2) for t in range(8)]
     lines = jnp.concatenate(lines + [jnp.zeros((4, 128), F32)], axis=0)
     found = jnp.zeros((4, 56), F32)
     for par in range(2):
@@ -1273,17 +1413,14 @@
     gub_o[...] = found[:, 24:56]
     outs.append(bring(gqb_o, gqb_h))
     outs.append(bring(gub_o, gub_h))
-    from_owner(gt_r, i_gt)
-    gtok_o[...] = gt_r[...].astype(F32)
-    outs.append(bring(gtok_o, gtok_h))
     gr_v.write_other(gq_o, 2)
     gr_k.write_other(gq_o)
     outs.append(bring(gq_o, gq_h))
     gr_o.write_other(go_o)
     outs.append(bring(go_o, go_h))
-    sc_i.sent()
     for gr in (gr_d, gr_u, gr_o, gr_v, gr_k):
         gr.sent()
+    assert (s_sems.used, r_sems.used, locals_.used) == (SENDS, RECEIVES, 24), (s_sems.used, r_sems.used, locals_.used)
     for done in pending + outs:
         done()
 
@@ -1316,12 +1453,12 @@
         ((256, 1024), BF16), ((256, 1024), F32), ((3, 64, 512), F32), ((3, 4, 8), F32), ((64, 512), F32), ((2, 64), F32),
         ((4, 64), F32), ((64, 2048), F32), ((4, 32), F32), ((64, 2048), F32), ((8, 64), F32),
     )
-    scratch += [vm(*result) for result in results] + [vm((2, 8, 1024), F32)]
+    scratch += [vm(*result) for result in results]
     scratch += [vm((3, 8, 2, 64, 256)), vm((4, 8, 2, 64, 256)), vm((8, 2, 64, 1024)), vm((8, 2, 64, 1024))]
     scratch += [vm((8, 2, 32, 128)), vm((256, 256)), vm((512, 1024)), vm((128, 1024))]
     scratch += [vm((3, 512, 256)), vm((2, 512, 256))] + [vm((2, 512, 256), F32)] * 3
     scratch += [vm((4, 128, 1024), F32), vm((4, 512, 512))] + [vm((512, 256), F32)] * 3 + [vm((4, 128, 256))] * 2
-    scratch += [vm((4, 128, 1024))] + [vm((3, 128, 1024))] * 3
+    scratch += [vm((4, 128, 1024))] + [vm((3, 128, 1024))] * 2 + [vm((4, 128, 1024))]
     scratch += [vm((4, 128, 1024)), vm((512, 1024)), vm((512, 1024), F32)]
     scratch += [vm((4, 128, 1024)), vm((512, 1024)), vm((4, 128, 1024)), vm((512, 1024), F32)]
     scratch += [vm((128, 1024), F32)] * 2 + [vm((128, 128), F32), vm((128, 1024), F32)]
@@ -1329,11 +1466,11 @@
     scratch += [vm((512, 256))] * 2 + [vm((512, 512)), vm((4, 512, 512)), vm((2, 512, 256), F32), vm((512, 256), F32)]
     scratch += [vm((3, 512, 256))]
     scratch += [vm((4, 2, 2, 64, n)) for n in widths]
-    scratch += [vm((4, 2, 64, n)) for n in widths] * 2 + [vm((2, 64, n)) for n in widths]
+    scratch += [vm((4, 2, 64, n)) for n in widths] * 2 + [vm((2, 2, 64, n)) for n in widths]
     scratch += [vm((2, 64, 1024), F32)] + [vm((64, n)) for n in widths] * 2
-    scratch += [vm((8, 1024), F32), vm((3, 8, 1024), F32), vm((16, 1024), F32), vm((6, 16, 1024), F32)]
-    scratch += [vm((128, 1024)), vm((128, 1024)), vm((256, 1024))]
-    scratch += [pltpu.SemaphoreType.DMA((400,)), pltpu.SemaphoreType.DMA((400,)), pltpu.SemaphoreType.DMA((40,))]
+    scratch += [vm((8, 1024), F32), vm((3, 8, 1024), F32)] + [vm((8, 1024), F32)] * 2 + [vm((8, 8, 1024), F32)] * 2
+    scratch += [vm((128, 1024)), vm((256, 1024))]
+    scratch += [pltpu.SemaphoreType.DMA((SENDS,)), pltpu.SemaphoreType.DMA((RECEIVES,)), pltpu.SemaphoreType.DMA((24,))]
 
     shapes = tuple(jax.ShapeDtypeStruct(*result) for result in results)
     anywhere = pl.BlockSpec(memory_space=pl.ANY)

time: 166 us -> 158 us (0.952)
  Pallas kernels: 165 us -> 157 us
    pallas_call x1, Pallas kernels: 161 us -> 154 us  [fast_local(): pl.pallas_call(layer_kernel, out_shape=shapes, in_specs=[anywhere] * 13,...]
where the time goes in v4:
time: 158 us
  Pallas kernels  157 us (99%)
    pallas_call x1, Pallas kernels, fast_local(): pl.pallas_call(layer_kernel, out_shape=shapes, in_specs=[anywhere] * 13,...  154 us

profile of v4, /device:TPU:0, one launch (start us, length us, event | category | flops | bytes accessed | tf_op | source)
XLA Modules:
  0.0 158.1 jit_solution(15403475977285641798)
XLA Ops:
  1.3 153.6 %layer.1 = (bf16[256,1024]{1,0:T(8,128)(2,1)}, f32[256,1024]{1,0:T(8,128)}, f32[3,64,512]{2,1,0:T(8,128)}, f32[3,4,8]{2,1,0:T(4,128)}, f32[64,512]{1,0:T(8,128)}...) custom-call(bf16[256,1024]{1,0:T(8,128)(2,1)} %tok.1, ...), custom_call_target="tpu_custom_call" | custom-call | tf_op jit(solution)/shard_map/layer/pallas_call | solution.py:1477
  154.9 3.1 %results.1 = (bf16[256,1024]{1,0:T(8,128)(2,1)}, f32[256,1024]{1,0:T(8,128)}, f32[3,64,512]{2,1,0:T(8,128)}, f32[3,4,8]{2,1,0:T(4,128)}, f32[64,512]{1,0:T(8,128...) custom-call(bf16[256,1024]{1,0:T(8,128)(2,1)} %get-tuple-element.33., ...), custom_call_target="tpu_custom_call" | custom-call | tf_op jit(solution)/shard_map/results/pallas_call | solution.py:1491

commit v5 on v4

--- a/solution.py
+++ b/solution.py
@@ -403,7 +403,7 @@
 
 MESH = pl.DeviceIdType.MESH
 PLANES = 4
-SENDS, RECEIVES = 84, 204
+SENDS, RECEIVES = 86, 214
 F32 = jnp.float32
 BF16 = jnp.bfloat16
 SCALE = HEAD ** (-0.25)
@@ -445,15 +445,30 @@
     qkv, phi, ex, unit, inv, r0, pp, num, den, quo, att, attf,
     pb, rb_f, rb_d, rb_i, fb, hid, dgel, efb, dub, dzb, acc,
     fst, n1, i1, dr, dat_s, dat, out_s, anti, ones64, rows_v,
-    dn, dd, ds_, gg, dph, dvv, dqkv,
+    dn, dd, ds_, gg, dph, dvv, dqkv, xt,
     g_k, g_v, g_o, g_u, g_d, r_k, r_v, r_o, r_u, r_d, rz_k, rz_v, rz_o, rz_u, rz_d, cb_k, cb_v, cb_o, cb_u, cb_d,
     fs, xs_k, xs_v, xs_o, xs_u, xs_d, xr_k, xr_v, xr_o, xr_u, xr_d,
-    sd, sd_r, st_a, st_b, work_a, work_b, mix_s, gt_r,
+    sd, sd_r, st_a, st_b, work_a, work_b, recv_a, recv_b, swap, mix_s, gt_r,
     ss, rs, ls,
 ):
     dp, y, c = lax.axis_index("dp"), lax.axis_index("heads"), lax.axis_index("feat")
     z, x = dp // 2, dp % 2
     shard = 2 * dp + c
+
+    def dev(zz, xx, yy, cc):
+        return {"dp": zz * 2 + xx, "heads": yy, "feat": cc}
+
+    sib, xn, yn, dg = dev(z, x, y, 1 - c), dev(z, 1 - x, y, c), dev(z, x, 1 - y, c), dev(z, 1 - x, 1 - y, c)
+    xs_dev, ds_dev = dev(z, 1 - x, y, 1 - c), dev(z, 1 - x, 1 - y, 1 - c)
+
+    barrier = pltpu.get_barrier_semaphore()
+    for other in (sib, xn, yn, dg, xs_dev, ds_dev, dev(z, x, 1 - y, 1 - c)):
+        pl.semaphore_signal(barrier, inc=1, device_id=other, device_id_type=MESH)
+    for zz in range(PLANES):
+        @pl.when(z != zz)
+        def _(zz=zz):
+            pl.semaphore_signal(barrier, inc=1, device_id=dev(zz, x, y, c), device_id_type=MESH)
+
     s_sems, r_sems, locals_ = Sems(), Sems(), Sems()
     pending = []
 
@@ -488,11 +503,6 @@
     in_d = bring(wd_h.at[:, half_cols(x, 1024)], wd.at[2 * z + x, c])
     in_cot = bring(cot.at[rows_of(y, 128)], cotb, home)
 
-    def dev(zz, xx, yy, cc):
-        return {"dp": zz * 2 + xx, "heads": yy, "feat": cc}
-
-    sib, xn, yn, dg = dev(z, x, y, 1 - c), dev(z, 1 - x, y, c), dev(z, x, 1 - y, c), dev(z, 1 - x, 1 - y, c)
-    xs_dev, ds_dev = dev(z, 1 - x, y, 1 - c), dev(z, 1 - x, 1 - y, 1 - c)
     plane = (dg, xn, yn)
     plane_block = (2 * (1 - x) + 1 - y, 2 * (1 - x) + y, 2 * x + 1 - y)
 
@@ -548,14 +558,9 @@
     def cols256(n):
         return pl.ds(pl.multiple_of(n * 256, 256), 256)
 
-    barrier = pltpu.get_barrier_semaphore()
-    for other in (sib, xn, yn, dg, xs_dev, ds_dev, dev(z, x, 1 - y, 1 - c)):
-        pl.semaphore_signal(barrier, inc=1, device_id=other, device_id_type=MESH)
-    for zz in range(PLANES):
-        @pl.when(z != zz)
-        def _(zz=zz):
-            pl.semaphore_signal(barrier, inc=1, device_id=dev(zz, x, y, c), device_id_type=MESH)
     pl.semaphore_wait(barrier, 10)
+
+    inner, outer = (z == 1) | (z == 2), (z == 0) | (z == 3)
 
     class Item:
         def __init__(self, ref, kind):
@@ -601,13 +606,17 @@
                 rc(self.some(count), self.some(count), sem, 0, sib).wait_send()
 
             pending.append(lambda: sent(self.c_out, 4))
-            pending.append(lambda: pl.when((z == 0) | (z == 3))(lambda: sent(self.z_out, 2)))
-            pending.append(lambda: pl.when((z == 1) | (z == 2))(lambda: sent(self.z_out, 4)))
-
-        def pump(self):
-            for k in range(1, PLANES):
-                self.pump_step(arrive[k])
-            self.pump_done()
+            pending.append(lambda: pl.when(outer)(lambda: sent(self.z_out, 2)))
+            pending.append(lambda: pl.when(inner)(lambda: sent(self.z_out, 4)))
+
+        def pump(self, where):
+            @pl.when(where)
+            def _():
+                for k in range(1, PLANES):
+                    self.pump_step(arrive[k])
+
+            if where is outer:
+                self.pump_done()
 
         def need_step(self, n):
             got(self.block(n, 1 - c), self.sb + n)
@@ -685,35 +694,43 @@
 
     same = (iota((256, 256), 0) // HEAD) == (iota((256, 256), 1) // HEAD)
     ones64[...] = jnp.where(same, 1.0, 0.0).astype(BF16)
-    anti[...] = jnp.where(iota((512, 512), 0) + iota((512, 512), 1) == 511, 1.0, 0.0).astype(BF16)
-
+    anti[...] = jnp.where(iota((128, 128), 0) + iota((128, 128), 1) == 127, 1.0, 0.0).astype(BF16)
+
+    it_oa.pump(inner)
     got(wo.at[own_block, 2 * z + 1 - x, c], i_oh[1])
     it_ob.start()
     have_half("q")
     it_qb.start()
-    it_oa.pump()
-    it_qa.pump()
-    it_ob.pump()
+    it_qa.pump(inner)
+    it_ob.pump(inner)
+    it_qb.pump(inner)
+
+    @pl.when(away)
+    def _():
+        for f in range(2):
+            got(xg.at[rows_of(2 * f + y, 128)], i_tx[1] + f)
+
+    for f in range(2):
+        part = xg.at[rows_of(2 * f + y, 128)]
+        give(part, part, i_ty, yn, away, f, f)
+    it_oa.pump(outer)
+    it_ob.pump(outer)
     i_oq, i_os = take(3), take(3)
     quarter = wo.at[own_block, :, c]
     give(quarter, quarter, i_oq, yn, None, 2, 2)
     give(quarter, quarter, i_oq, xn, None, 1, 1)
+    give_half("d", wd_h.at[:, half_cols(1 - x, 1024)], wd)
     have_half("s")
     it_s.start()
     in_u()
     it_ua.start()
-
-    @pl.when(away)
-    def _():
-        for f in range(2):
-            got(xg.at[rows_of(2 * f + y, 128)], i_tx[1] + f)
-
-    for f in range(2):
-        part = xg.at[rows_of(2 * f + y, 128)]
-        give(part, part, i_ty, yn, away, f, f)
-    it_qb.pump()
+    it_s.pump(inner)
+    it_qa.pump(outer)
     have_half("u")
     it_ub.start()
+    in_d()
+    it_da.start()
+    it_qb.pump(outer)
 
     def other_quarter(slot):
         part = wo.at[plane_block[slot], :, c]
@@ -721,7 +738,7 @@
         give(part, part, i_os, sib, None, slot, slot)
         return part
 
-    it_s.pump()
+    it_s.pump(outer)
 
     it_s.need()
     for t in range(8):
@@ -764,6 +781,7 @@
     other_quarter(2)
     part = other_quarter(1)
     give(part, part, i_oq, yn, None, 0, 0)
+    it_ua.pump(inner)
     it_qa.need()
     it_qb.need()
 
@@ -789,7 +807,6 @@
         return carry
 
     lax.fori_loop(0, 2, feature_body, 0)
-    it_ua.pump()
     lane_head = iota((1, 128), 1) // HEAD
 
     def head_cols(h):
@@ -808,31 +825,36 @@
         den[:, cols] += both[:, 128:]
         return carry
 
-    lax.fori_loop(0, 4, head_body, 0)
-    quo[...] = num[...] / den[...]
-    att[...] = quo[...].astype(BF16).reshape(4, 128, 256)
-
-    i_at = take(3)
-    for slot in range(3):
-        give(att.at[plane_block[slot]], attf.at[own_block], i_at, plane[slot], None, slot, slot)
-    attf[own_block] = att[own_block]
-    in_d()
-    it_da.start()
-    other_quarter(0)
-    give_half("d", wd_h.at[:, half_cols(1 - x, 1024)], wd)
+    i_at = [take(3), take(3)]
+
+    def tile_of(ref, block, t):
+        return ref.at[block, :, t * 128 : (t + 1) * 128]
+
+    for t in range(2):
+        lax.fori_loop(2 * t, 2 * t + 2, head_body, 0)
+        cols = slice(t * 128, (t + 1) * 128)
+        quo[:, cols] = num[:, cols] / den[:, cols]
+        att[:, :, cols] = quo[:, cols].astype(BF16).reshape(4, 128, 128)
+        for slot in range(3):
+            give(tile_of(att, plane_block[slot], t), tile_of(attf, own_block, t), i_at[t], plane[slot], None, slot, slot)
+    have_half("d")
+    it_db.start()
     i_cot = take()
     give(cot.at[rows_of(y, 128)], cotb, i_cot, xs_dev, away)
+    it_ub.pump(inner)
+    other_quarter(0)
     it_oa.need()
     it_ob.need()
-    for slot in range(3):
+
+    def out_part(rows, block):
+        return dot(rows, wo[block].reshape(1024, 256), NT)
+
+    mixed_z = out_part(att[own_block], own_block)
+    for slot in (2, 1, 0):
         got(wo.at[plane_block[slot], :, 1 - c], i_os[1] + slot)
-    for slot in range(3):
-        got(attf.at[plane_block[slot]], i_at[1] + slot)
-
-    def out_body(q, carry):
-        return carry + dot(attf[q], wo[q].reshape(1024, 256), NT)
-
-    mixed_z = lax.fori_loop(0, 4, out_body, jnp.zeros((128, 1024), F32))
+        for t in range(2):
+            got(tile_of(attf, plane_block[slot], t), i_at[t][1] + slot)
+        mixed_z = mixed_z + out_part(attf[plane_block[slot]], plane_block[slot])
 
     def norm(values):
         centred = values - jnp.mean(values, axis=-1, keepdims=True)
@@ -909,11 +931,15 @@
             got(self.piece(slot, n), self.base + slot * 4 + n)
             got(self.piece(0, n), self.base + n)
 
-    g_first = Gather(fb, range(4))
+    g_first = RelayGather(fb, range(4))
     g_first.start()
-    it_ub.pump()
-    have_half("d")
-    it_db.start()
+    it_da.pump(inner)
+    g_first.pass_on(0)
+    it_db.pump(inner)
+    for k in range(1, 4):
+        g_first.pass_on(k)
+    it_ua.pump(outer)
+    it_ub.pump(outer)
     fst[...] = first
     n1[...] = normed
     i1[...] = jnp.broadcast_to(inverse, (128, 128))
@@ -925,17 +951,18 @@
     it_ua.need()
     it_ub.need()
 
-    def hidden_part(n, carry):
-        g_first.need(n)
-        left = d_cols(fb, n)
-        for j in range(4):
-            cols = slice(j * 256, (j + 1) * 256)
-            acc[:, cols] += dot(left, wu[pl.ds(2 * n, 2), :, :, cols].reshape(256, 256))
-        return carry
-
-    lax.fori_loop(0, 2, hidden_part, 0)
-    it_da.pump()
-    lax.fori_loop(2, 4, hidden_part, 0)
+    for k in range(4):
+        g_first.need(k)
+        left = d_cols(fb, k)
+        if k == 2:
+            it_da.pump(outer)
+
+        def hidden_part(j, carry, k=k, left=left):
+            cols = cols256(j)
+            acc[:, cols] += dot(left, wu[2 * k : 2 * k + 2, :, :, cols].reshape(256, 256))
+            return carry
+
+        lax.fori_loop(0, 4, hidden_part, 0)
 
     def hidden_body(n, carry):
         cols = cols256(n)
@@ -950,7 +977,7 @@
 
     def down_part(k, carry):
         n = at_step(arrive, k)
-        it_db.pump_step(n)
+        pl.when(outer)(lambda: it_db.pump_step(n))
         it_da.need_step(n)
         it_db.need_step(n)
         sc_f.part(n, dot(hid[...], wd[pl.ds(2 * n, 2)].reshape(256, 1024), NT))
@@ -1016,7 +1043,8 @@
     own_mix.start(mix_s, 0)
 
     class Grad:
-        def __init__(self, g, r, rz, cb, xs, xr):
+        def __init__(self, g, r, rz, cb, xs, xr, first):
+            self.first = first
             self.g, self.r, self.rz, self.cb, self.xs, self.xr = g, r, rz, cb, xs, xr
             self.d, self.z, self.k, self.x = r_sems.take(4), r_sems.take(PLANES), r_sems.take(2), take()
             self.d_out, self.z_out = s_sems.take(), s_sems.take()
@@ -1030,10 +1058,9 @@
             self.r[m] = (self.g[m, :, c].astype(F32) + self.r[m].astype(F32)).astype(BF16)
             far = jnp.abs(m - z)
             part = self.r.at[m]
-            outer = (z == 0) | (z == 3)
             beside = dev(jnp.where(z == 0, 1, jnp.where(z == 1, 0, jnp.where(z == 2, 3, 2))), x, y, c)
 
-            @pl.when(jnp.logical_or(outer, m == jnp.where(z == 1, 0, 3)) & (far == 1))
+            @pl.when(jnp.logical_or(outer if self.first else False, m == jnp.where(z == 1, 0, 3)) & (far == 1))
             def _():
                 rc(part, self.rz.at[z], self.z_out, self.z + z, beside).start()
 
@@ -1041,6 +1068,12 @@
                 @pl.when(outer & (far == 3 - slot))
                 def _(slot=slot):
                     rc(part, self.cb.at[slot], self.z_out, self.k + slot, beside).start()
+
+        def near(self):
+            for at, m in ((0, 1), (3, 2)):
+                @pl.when(z == at)
+                def _(at=at, m=m):
+                    rc(self.r.at[m], self.rz.at[at], self.z_out, self.z + at, dev(m, x, y, c)).start()
 
         def relay(self):
             for at, blocks in ((1, (3, 2)), (2, (0, 1))):
@@ -1092,11 +1125,11 @@
             got(self.xr, self.x[1])
             self.columns(out, 1 - x, self.xr[...].astype(F32), at)
 
-    gr_d = Grad(g_d, r_d, rz_d, cb_d, xs_d, xr_d)
-    gr_u = Grad(g_u, r_u, rz_u, cb_u, xs_u, xr_u)
-    gr_o = Grad(g_o, r_o, rz_o, cb_o, xs_o, xr_o)
-    gr_v = Grad(g_v, r_v, rz_v, cb_v, xs_v, xr_v)
-    gr_k = Grad(g_k, r_k, rz_k, cb_k, xs_k, xr_k)
+    gr_d = Grad(g_d, r_d, rz_d, cb_d, xs_d, xr_d, True)
+    gr_u = Grad(g_u, r_u, rz_u, cb_u, xs_u, xr_u, True)
+    gr_o = Grad(g_o, r_o, rz_o, cb_o, xs_o, xr_o, False)
+    gr_v = Grad(g_v, r_v, rz_v, cb_v, xs_v, xr_v, False)
+    gr_k = Grad(g_k, r_k, rz_k, cb_k, xs_k, xr_k, False)
 
     def make_down(m):
         g_ef.need(m)
@@ -1117,7 +1150,8 @@
         cols = cols256(n)
         du = (acc[:, cols] * dgel[:, cols]).astype(BF16)
         dub[:, cols] = du
-        st_a[6:7, cols] = down(du.astype(F32))
+        for zz in range(PLANES):
+            st_b[zz, pl.ds(8 + n, 1), :] = down(du.astype(F32))
         return carry
 
     lax.fori_loop(0, 4, du_body, 0)
@@ -1129,6 +1163,8 @@
 
     lax.fori_loop(0, 4, back_part, 0)
     own_mix.pass_on(0)
+    for m in range(4):
+        xt[m * 256 : (m + 1) * 256] = xg[:, m * 256 : (m + 1) * 256].T
 
     def make_up(m):
         g_u[m] = dot(d_cols(fb, m), dub[...], TN).astype(BF16).reshape(2, 2, 64, 1024)
@@ -1140,14 +1176,15 @@
     dz = back.astype(BF16)
     dzb[own_block] = dz
 
-    def dattn_body(q, carry):
-        dat_s[q] = dot(dz, wo[q].reshape(1024, 256)).astype(BF16)
-        return carry
-
-    lax.fori_loop(0, 4, dattn_body, 0)
     i_da = take(3)
+
+    def attention_grad(block):
+        dat_s[block] = dot(dz, wo[block].reshape(1024, 256)).astype(BF16)
+
     for slot in range(3):
+        attention_grad(plane_block[slot])
         give(dat_s.at[plane_block[slot]], dat.at[own_block], i_da, plane[slot], None, slot, slot)
+    attention_grad(own_block)
     dat[own_block] = dat_s[own_block]
     g_dz = RelayGather(dzb, leave)
     g_dz.start()
@@ -1156,40 +1193,32 @@
     sd[2:3, :] = down(dz.astype(F32))
     sd[6:8, :] = jnp.zeros((2, 1024), F32)
     class Total:
-        def __init__(self, ref, work):
-            self.ref, self.work = ref, work
-            self.c, self.z, self.h = take(), take(PLANES), take()
+        def __init__(self, ref, work, recv):
+            self.ref, self.work, self.recv = ref, work, recv
+            self.c, self.z = take(), take(PLANES)
 
         def pair(self):
-            give(self.ref, self.work.at[0], self.c, sib)
+            give(self.ref, self.work, self.c, sib)
 
         def over_planes(self):
-            got(self.work.at[0], self.c[1])
-            self.work[1] = self.ref[...] + self.work[0]
+            got(self.work, self.c[1])
+            self.work[...] = self.ref[...] + self.work[...]
             for zz in range(PLANES):
-                give(self.work.at[1], self.work.at[2 + z], self.z, dev(zz, x, y, c), z != zz, zz, z)
+                give(self.work.at[zz], self.recv.at[z], self.z, dev(zz, x, y, c), z != zz, zz, z)
 
         def finish(self):
-            total = self.work[1]
             for zz in range(PLANES):
                 @pl.when(z != zz)
                 def _(zz=zz):
-                    got(self.work.at[2 + zz], self.z[1] + zz)
+                    got(self.recv.at[zz], self.z[1] + zz)
 
                 @pl.when(z == zz)
                 def _(zz=zz):
-                    self.work[2 + zz] = jnp.zeros((8, 1024), F32)
-                total = total + self.work[2 + zz]
-            self.work[6] = total
-            give(self.work.at[6], self.work.at[7], self.h, xn)
-
-        def need(self):
-            got(self.work.at[7], self.h[1])
-
-        def of_half(self, half):
-            return jnp.where(x == half, self.work[6], self.work[7])
-
-    early, late = Total(st_a, work_a), Total(st_b, work_b)
+                    self.recv[zz] = self.work[zz]
+            return self.recv[0] + self.recv[1] + self.recv[2] + self.recv[3]
+
+    early, late = Total(st_a, work_a, recv_a), Total(st_b, work_b, recv_b)
+    i_swap = take()
     i_sd = take(3)
     for k, device in enumerate(plane):
         give(sd, sd_r.at[k], i_sd, device, None, k, k)
@@ -1215,11 +1244,11 @@
     lax.fori_loop(0, 4, value_back, 0)
     dqkv[2] = dvv[...].astype(BF16)
 
-    def x_cols(m):
-        return xg[:, cols256(m)]
+    def x_rows(m):
+        return xt[rows_of(m, 256)]
 
     def make_v(m):
-        g_v[m] = dot(x_cols(m), dqkv[2], TN).astype(BF16).reshape(2, 2, 64, 256)
+        g_v[m] = dot(x_rows(m), dqkv[2]).astype(BF16).reshape(2, 2, 64, 256)
 
     def head_back(h, carry):
         cols, mine = head_cols(h)
@@ -1306,17 +1335,27 @@
     lax.fori_loop(0, 4, input_part, 0)
     for k in range(3):
         got(sd_r.at[k], i_sd[1] + k)
-    st_a[0:6, :] = (sd[...] + sd_r[0] + sd_r[1] + sd_r[2])[0:6]
-    st_a[7:8, :] = jnp.zeros((1, 1024), F32)
+    sums = sd[...] + sd_r[0] + sd_r[1] + sd_r[2]
+    for zz in range(PLANES):
+        st_a[zz] = sums[:, zz * 256 : (zz + 1) * 256]
     early.pair()
     gr_d.finish()
     gr_d.write_own(gd_o)
 
+    def make_k(m):
+        for p in range(2):
+            g_k[m, :, :, :, p * 256 : (p + 1) * 256] = (
+                dot(x_rows(m), dqkv[p]).astype(BF16).reshape(2, 2, 64, 256)
+            )
+
+    early.over_planes()
+    gr_k.run(make_k)
+
     def diagonal_body(h, carry):
-        flipped = dot(anti[...], gg[h])
         sums = jnp.zeros((1, 1024), F32)
         for b in range(4):
-            wide = jnp.concatenate([flipped[b * 128 : (b + 1) * 128], jnp.zeros((128, 128), F32)], axis=1)
+            flipped = dot(anti[...], gg[h, (3 - b) * 128 : (4 - b) * 128])
+            wide = jnp.concatenate([flipped, jnp.zeros((128, 128), F32)], axis=1)
             line = down(pltpu.roll(wide, 0, 1, stride=1, stride_axis=0))
             pieces = [line]
             if b > 0:
@@ -1324,40 +1363,36 @@
             if b < 3:
                 pieces = pieces + [jnp.zeros((1, 384 - 128 * b), F32)]
             sums = sums + jnp.concatenate(pieces, axis=1)
-        st_b[pl.ds(1 + h, 1), :] = sums
+        for zz in range(PLANES):
+            st_b[zz, pl.ds(h, 1), :] = sums[:, (3 - zz) * 256 : (4 - zz) * 256]
         return carry
 
     lax.fori_loop(0, 4, diagonal_body, 0)
     for p in range(3):
-        st_b[0:1, p * 256 : (p + 1) * 256] = down(dqkv[p].astype(F32))
-    st_b[0:1, 768:1024] = jnp.zeros((1, 256), F32)
-    st_b[5:8, :] = jnp.zeros((3, 1024), F32)
+        line = down(dqkv[p].astype(F32))
+        for zz in range(PLANES):
+            st_b[zz, 12 + p : 13 + p, :] = line
+    for zz in range(PLANES):
+        st_b[zz, 4:8, :] = jnp.zeros((4, 256), F32)
+        st_b[zz, 15:16, :] = jnp.zeros((1, 256), F32)
     late.pair()
-    early.over_planes()
-
-    def make_k(m):
-        for p in range(2):
-            g_k[m, :, :, :, p * 256 : (p + 1) * 256] = (
-                dot(x_cols(m), dqkv[p], TN).astype(BF16).reshape(2, 2, 64, 256)
-            )
-
-    gr_k.run(make_k)
+
 
     def make_out(m):
         g_o[m] = dot(d_cols(dzb, m), att[...].reshape(512, 256), TN).astype(BF16).reshape(2, 2, 64, 256)
 
     for k in range(4):
         g_dz.need(k)
+    late.over_planes()
     gr_o.run(make_out)
-
-    late.over_planes()
+    for gr in (gr_v, gr_k, gr_o):
+        gr.near()
     outs = []
     own_mix.need(0)
     outs.append(bring(mixed_o, mixed_h))
     gr_v.relay()
     gr_u.finish()
     gr_u.write_own(gu_o)
-    early.finish()
     sc_i.column(0)
     sc_i.column(1)
     gr_k.relay()
@@ -1374,14 +1409,15 @@
     def exact(left, right):
         return lax.dot_general(left, right, NN, precision=lax.Precision.HIGHEST, preferred_element_type=F32)
 
-    early.need()
-    mine = early.work[6, :, pl.ds(pl.multiple_of(dp * 128, 128), 128)]
+    sd_r[0, :, 0:256] = early.finish()
+    mine = sd_r[0, :, pl.ds(pl.multiple_of(x * 128, 128), 128)]
     own = exact(mine, pick((128, 64), lambda k, l: k == c * 64 + l))
     ggain_o[...] = own[0:2]
     gbias_o[...] = own[2:6]
     outs.append(bring(ggain_o, ggain_h))
     outs.append(bring(gbias_o, gbias_h))
-    late.finish()
+    swap[0] = late.finish()
+    give(swap.at[0], swap.at[1], i_swap, xn)
     gr_k.finish()
     gr_k.write_own(gq_o)
     gr_o.finish()
@@ -1389,19 +1425,18 @@
     for n in range(4):
         sc_i.need(n)
     outs.append(bring(gtok_o, gtok_h))
-    late.need()
-    ups = [early.of_half(half) for half in range(2)]
-    rest = [late.of_half(half) for half in range(2)]
-    tile = pl.ds(pl.multiple_of((7 - dp) * 128, 128), 128)
-    sd_r[0] = rest[0]
-    sd_r[1] = rest[1]
-    lines = jnp.concatenate([sd_r[0, 1:5, tile], sd_r[1, 1:5, tile]], axis=0)
+    got(swap.at[1], i_swap[1])
+    tile = pl.ds(pl.multiple_of((1 - x) * 128, 128), 128)
+    ours, theirs = swap[0, 0:4, tile], swap[1, 0:4, tile]
+    lines = jnp.concatenate([jnp.where(x == 0, ours, theirs), jnp.where(x == 0, theirs, ours)], axis=0)
     grpe_o[...] = exact(lines, pick((128, 64), lambda k, l: k == (1 - c) * 64 + 63 - l))
     outs.append(bring(grpe_o, grpe_h))
-    lines = [
-        rest[half][0:1, p * 256 + t * 128 : p * 256 + (t + 1) * 128]
-        for p in range(3) for half in range(2) for t in range(2)
-    ] + [ups[half][6:7, t * 128 : (t + 1) * 128] for half in range(2) for t in range(8)]
+    ours, theirs = swap[0, 8:16], swap[1, 8:16]
+    rest = [jnp.where(x == half, ours, theirs) for half in range(2)]
+    lines = [rest[half][4 + p : 5 + p, t * 128 : (t + 1) * 128] for p in range(3) for half in range(2) for t in range(2)]
+    lines += [
+        rest[half][t // 2 : t // 2 + 1, (t % 2) * 128 : (t % 2 + 1) * 128] for half in range(2) for t in range(8)
+    ]
     lines = jnp.concatenate(lines + [jnp.zeros((4, 128), F32)], axis=0)
     found = jnp.zeros((4, 56), F32)
     for par in range(2):
@@ -1462,13 +1497,14 @@
     scratch += [vm((4, 128, 1024)), vm((512, 1024)), vm((512, 1024), F32)]
     scratch += [vm((4, 128, 1024)), vm((512, 1024)), vm((4, 128, 1024)), vm((512, 1024), F32)]
     scratch += [vm((128, 1024), F32)] * 2 + [vm((128, 128), F32), vm((128, 1024), F32)]
-    scratch += [vm((4, 128, 256))] * 2 + [vm((16, 128)), vm((512, 512)), vm((256, 256)), vm((24, 1024), F32)]
+    scratch += [vm((4, 128, 256))] * 2 + [vm((16, 128)), vm((128, 128)), vm((256, 256)), vm((24, 1024), F32)]
     scratch += [vm((512, 256))] * 2 + [vm((512, 512)), vm((4, 512, 512)), vm((2, 512, 256), F32), vm((512, 256), F32)]
-    scratch += [vm((3, 512, 256))]
+    scratch += [vm((3, 512, 256)), vm((1024, 512))]
     scratch += [vm((4, 2, 2, 64, n)) for n in widths]
     scratch += [vm((4, 2, 64, n)) for n in widths] * 2 + [vm((2, 2, 64, n)) for n in widths]
     scratch += [vm((2, 64, 1024), F32)] + [vm((64, n)) for n in widths] * 2
-    scratch += [vm((8, 1024), F32), vm((3, 8, 1024), F32)] + [vm((8, 1024), F32)] * 2 + [vm((8, 8, 1024), F32)] * 2
+    scratch += [vm((8, 1024), F32), vm((3, 8, 1024), F32)] + [vm((4, 8, 256), F32), vm((4, 16, 256), F32)] * 3
+    scratch += [vm((2, 16, 256), F32)]
     scratch += [vm((128, 1024)), vm((256, 1024))]
     scratch += [pltpu.SemaphoreType.DMA((SENDS,)), pltpu.SemaphoreType.DMA((RECEIVES,)), pltpu.SemaphoreType.DMA((24,))]
 

time: 158 us -> 151 us (0.956)
  Pallas kernels: 157 us -> 149 us
    pallas_call x1, Pallas kernels: 154 us -> 146 us  [fast_local(): pl.pallas_call(layer_kernel, out_shape=shapes, in_specs=[anywhere] * 13,...]
where the time goes in v5:
time: 151 us; the launch traced here: 150 us
  Pallas kernels  149 us (99%)
    pallas_call x1, Pallas kernels, fast_local(): pl.pallas_call(layer_kernel, out_shape=shapes, in_specs=[anywhere] * 13,...  146 us
    pallas_call x1, Pallas kernels, fast_local(): pl.pallas_call(copy_kernel, out_shape=shapes, in_specs=[anywhere] * len(s...  3.09 us

profile of v5, /device:TPU:0, one launch (start us, length us, event | category | flops | bytes accessed | tf_op | source)
XLA Modules:
  0.0 150.4 jit_solution(9130425718663417427)
XLA Ops:
  1.3 145.8 %layer.1 = (bf16[256,1024]{1,0:T(8,128)(2,1)}, f32[256,1024]{1,0:T(8,128)}, f32[3,64,512]{2,1,0:T(8,128)}, f32[3,4,8]{2,1,0:T(4,128)}, f32[64,512]{1,0:T(8,128)}...) custom-call(bf16[256,1024]{1,0:T(8,128)(2,1)} %tok.1, ...), custom_call_target="tpu_custom_call" | custom-call | tf_op jit(solution)/shard_map/layer/pallas_call | solution.py:1513
  147.1 3.1 %results.1 = (bf16[256,1024]{1,0:T(8,128)(2,1)}, f32[256,1024]{1,0:T(8,128)}, f32[3,64,512]{2,1,0:T(8,128)}, f32[3,4,8]{2,1,0:T(4,128)}, f32[64,512]{1,0:T(8,128...) custom-call(bf16[256,1024]{1,0:T(8,128)(2,1)} %get-tuple-element.33., ...), custom_call_target="tpu_custom_call" | custom-call | tf_op jit(solution)/shard_map/results/pallas_call | solution.py:1527

commit v6 on v5

--- a/solution.py
+++ b/solution.py
@@ -403,7 +403,7 @@
 
 MESH = pl.DeviceIdType.MESH
 PLANES = 4
-SENDS, RECEIVES = 86, 214
+SENDS, RECEIVES = 86, 215
 F32 = jnp.float32
 BF16 = jnp.bfloat16
 SCALE = HEAD ** (-0.25)
@@ -445,7 +445,7 @@
     qkv, phi, ex, unit, inv, r0, pp, num, den, quo, att, attf,
     pb, rb_f, rb_d, rb_i, fb, hid, dgel, efb, dub, dzb, acc,
     fst, n1, i1, dr, dat_s, dat, out_s, anti, ones64, rows_v,
-    dn, dd, ds_, gg, dph, dvv, dqkv, xt,
+    dn, dd, ds_, gg, dph, dvv, dqkv, xt, ppt,
     g_k, g_v, g_o, g_u, g_d, r_k, r_v, r_o, r_u, r_d, rz_k, rz_v, rz_o, rz_u, rz_d, cb_k, cb_v, cb_o, cb_u, cb_d,
     fs, xs_k, xs_v, xs_o, xs_u, xs_d, xr_k, xr_v, xr_o, xr_u, xr_d,
     sd, sd_r, st_a, st_b, work_a, work_b, recv_a, recv_b, swap, mix_s, gt_r,
@@ -892,19 +892,63 @@
         def sent(self):
             rc(self.ref, self.ref, self.out, 0, sib).wait_send()
 
+    class RelayScatter:
+        def __init__(self, ref):
+            self.ref, self.out = ref, s_sems.take()
+            self.near, self.far, self.last = r_sems.take(4), r_sems.take(4), r_sems.take(4)
+
+        def part(self, n, value):
+            cols = cols256(n)
+            pb[:, :, cols] = value.astype(BF16).reshape(4, 128, 256)
+            even = n % 2 == 0
+            beside = dev(z, jnp.where(even, 1 - x, x), jnp.where(even, y, 1 - y), c)
+            block = jnp.where(even, plane_block[1], plane_block[2])
+            rc(pb.at[plane_block[0], :, cols], self.ref.at[1, :, cols], self.out, self.far + n, beside).start()
+            rc(pb.at[block, :, cols], self.ref.at[0, :, cols], self.out, self.near + n, beside).start()
+
+        def pass_on(self, n):
+            cols, slot = slice(n * 256, (n + 1) * 256), 2 - n % 2
+            part = self.ref.at[1, :, cols]
+            got(part, self.far + n)
+            part[...] = (part[...].astype(F32) + pb[plane_block[slot], :, cols].astype(F32)).astype(BF16)
+            rc(part, self.ref.at[2, :, cols], self.out, self.last + n, plane[slot]).start()
+
+        def total(self):
+            pieces = []
+            for n in range(4):
+                cols = slice(n * 256, (n + 1) * 256)
+                got(self.ref.at[0, :, cols], self.near + n)
+                got(self.ref.at[2, :, cols], self.last + n)
+                value = pb[own_block, :, cols].astype(F32) + self.ref[0, :, cols].astype(F32)
+                pieces.append(value + self.ref[2, :, cols].astype(F32))
+            return jnp.concatenate(pieces, axis=1)
+
+        def sent(self):
+            rc(self.ref, self.ref, self.out, 0, sib).wait_send()
+
     class Gather:
         def __init__(self, ref, order):
-            self.ref, self.out, self.base, self.order = ref, s_sems.take(), r_sems.take(4), order
+            self.ref, self.out, self.base, self.order = ref, s_sems.take(), r_sems.take(5), order
             pending.append(lambda: rc(ref.at[pl.ds(0, 3)], ref.at[pl.ds(0, 3)], self.out, 0, sib).wait_send())
 
         def start(self):
-            for n in self.order:
+            for half in range(2):
                 for slot in range(3):
-                    mine = self.ref.at[own_block, :, cols256(n)]
-                    rc(mine, mine, self.out, self.base + n, plane[slot]).start()
-
-        def need(self, n):
-            got(self.ref.at[pl.ds(0, 3), :, cols256(n)], self.base + n)
+                    mine = self.ref.at[own_block, :, self.half_cols(half)]
+                    rc(mine, mine, self.out, self.base + 3 + half, plane[slot]).start()
+            for k in range(1, 4):
+                for slot in range(3):
+                    mine = self.ref.at[own_block, :, cols256(self.order[k])]
+                    rc(mine, mine, self.out, self.base + k - 1, plane[slot]).start()
+
+        def half_cols(self, half):
+            return pl.ds(pl.multiple_of(self.order[0] * 256 + half * 128, 128), 128)
+
+        def need_half(self, half):
+            got(self.ref.at[pl.ds(0, 3), :, self.half_cols(half)], self.base + 3 + half)
+
+        def need(self, k):
+            got(self.ref.at[pl.ds(0, 3), :, cols256(at_step(self.order, k))], self.base + k - 1)
 
     class RelayGather:
         def __init__(self, ref, order):
@@ -1046,7 +1090,8 @@
         def __init__(self, g, r, rz, cb, xs, xr, first):
             self.first = first
             self.g, self.r, self.rz, self.cb, self.xs, self.xr = g, r, rz, cb, xs, xr
-            self.d, self.z, self.k, self.x = r_sems.take(4), r_sems.take(PLANES), r_sems.take(2), take()
+            self.d, self.z, self.k, self.x = r_sems.take(4), r_sems.take(2), r_sems.take(2), take()
+            self.mine = z // 2
             self.d_out, self.z_out = s_sems.take(), s_sems.take()
             self.width = r.shape[-1]
 
@@ -1062,27 +1107,42 @@
 
             @pl.when(jnp.logical_or(outer if self.first else False, m == jnp.where(z == 1, 0, 3)) & (far == 1))
             def _():
-                rc(part, self.rz.at[z], self.z_out, self.z + z, beside).start()
+                rc(part, self.rz.at[self.mine], self.z_out, self.z + self.mine, beside).start()
 
             for slot in range(2):
                 @pl.when(outer & (far == 3 - slot))
                 def _(slot=slot):
                     rc(part, self.cb.at[slot], self.z_out, self.k + slot, beside).start()
 
+        def pair_half(self, m, half, i):
+            part = self.r.at[m, half]
+            got(part, i)
+            part[...] = (self.g[m, half, c].astype(F32) + part[...].astype(F32)).astype(BF16)
+            beside = dev(jnp.where(z == 0, 1, jnp.where(z == 1, 0, jnp.where(z == 2, 3, 2))), x, y, c)
+
+            @pl.when(outer)
+            def _():
+                rc(part, self.cb.at[0, half], self.z_out, self.k, beside).start()
+
+            @pl.when(inner)
+            def _():
+                rc(part, self.rz.at[self.mine, half], self.z_out, self.z + self.mine, beside).start()
+
         def near(self):
             for at, m in ((0, 1), (3, 2)):
                 @pl.when(z == at)
                 def _(at=at, m=m):
-                    rc(self.r.at[m], self.rz.at[at], self.z_out, self.z + at, dev(m, x, y, c)).start()
-
-        def relay(self):
+                    rc(self.r.at[m], self.rz.at[at // 2], self.z_out, self.z + at // 2, dev(m, x, y, c)).start()
+
+        def relay(self, *slots):
             for at, blocks in ((1, (3, 2)), (2, (0, 1))):
                 @pl.when(z == at)
                 def _(at=at, blocks=blocks):
-                    for slot, m in enumerate(blocks):
+                    for slot in slots:
+                        m = blocks[slot]
                         got(self.cb.at[slot], self.k + slot)
                         self.r[m] = (self.r[m].astype(F32) + self.cb[slot].astype(F32)).astype(BF16)
-                        rc(self.r.at[m], self.rz.at[at], self.z_out, self.z + at, dev(m, x, y, c)).start()
+                        rc(self.r.at[m], self.rz.at[at // 2], self.z_out, self.z + at // 2, dev(m, x, y, c)).start()
 
         def run(self, make):
             def body(k, carry):
@@ -1101,8 +1161,9 @@
             for dz in (1, -1, 2, -2):
                 @pl.when(valid(dz) if abs(dz) == 1 else z == (0 if dz > 0 else 3))
                 def _(dz=dz):
-                    got(self.rz.at[z + dz], self.z + z + dz)
-                    total[...] += self.rz[z + dz].astype(F32)
+                    slot = (z + dz) // 2
+                    got(self.rz.at[slot], self.z + slot)
+                    total[...] += self.rz[slot].astype(F32)
             self.xs[...] = fs[1 - x, :, 0 : self.width].astype(BF16)
             give(self.xs, self.xr, self.x, xn)
 
@@ -1131,21 +1192,33 @@
     gr_v = Grad(g_v, r_v, rz_v, cb_v, xs_v, xr_v, False)
     gr_k = Grad(g_k, r_k, rz_k, cb_k, xs_k, xr_k, False)
 
-    def make_down(m):
-        g_ef.need(m)
+    def act_part(m):
         left = d_cols(efb, m)
-        g_d[m] = dot(left, hid[...], TN).astype(BF16).reshape(2, 2, 64, 1024)
-        gr_d.give(m)
         for j in range(4):
             cols = slice(j * 256, (j + 1) * 256)
             acc[:, cols] += dot(left, wd[pl.ds(2 * m, 2), :, :, cols].reshape(256, 256))
+
+    i_half = r_sems.take(2)
+    for half in range(2):
+        g_ef.need_half(half)
+        left = efb[:, :, g_ef.half_cols(half)].reshape(512, 128)
+        g_d[leave[0], half] = dot(left, hid[...], TN).astype(BF16).reshape(2, 64, 1024)
+        rc(g_d.at[leave[0], half, 1 - c], r_d.at[leave[0], half], gr_d.d_out, i_half + half, sib).start()
+    for half in range(2):
+        gr_d.pair_half(leave[0], half, i_half + half)
+        if half == 0:
+            act_part(leave[0])
+
+    def down_grads(k, carry):
+        m = at_step(leave, k)
+        g_ef.need(k)
+        g_d[m] = dot(d_cols(efb, m), hid[...], TN).astype(BF16).reshape(2, 2, 64, 1024)
+        gr_d.give(m)
+        act_part(m)
         gr_d.pair_step(m)
-
-    def down_grads(k, carry):
-        make_down(at_step(leave, k))
         return carry
 
-    lax.fori_loop(0, PLANES, down_grads, 0)
+    lax.fori_loop(1, PLANES, down_grads, 0)
     def du_body(n, carry):
         cols = cols256(n)
         du = (acc[:, cols] * dgel[:, cols]).astype(BF16)
@@ -1155,7 +1228,7 @@
         return carry
 
     lax.fori_loop(0, 4, du_body, 0)
-    sc_d = Scatter(rb_d)
+    sc_d = RelayScatter(rb_d)
 
     def back_part(n, carry):
         sc_d.part(n, dot(dub[...], wu[pl.ds(2 * n, 2)].reshape(256, 1024), NT))
@@ -1166,11 +1239,21 @@
     for m in range(4):
         xt[m * 256 : (m + 1) * 256] = xg[:, m * 256 : (m + 1) * 256].T
 
+    def transpose_body(h, carry):
+        ppt[h] = pp[h].T
+        return carry
+    gr_d.relay(0)
+    sc_d.pass_on(0)
+    sc_d.pass_on(1)
+
     def make_up(m):
         g_u[m] = dot(d_cols(fb, m), dub[...], TN).astype(BF16).reshape(2, 2, 64, 1024)
 
-    gr_d.relay()
     gr_u.run(make_up)
+    sc_d.pass_on(2)
+    sc_d.pass_on(3)
+    lax.fori_loop(0, 4, transpose_body, 0)
+    gr_d.relay(1)
     dfirst = dr[...] + sc_d.total()
     back = norm_back(dfirst, n1[...], i1[:, 0:1], rows_v[0:1, :])
     dz = back.astype(BF16)
@@ -1226,6 +1309,7 @@
     sc_d.sent()
     dph[...] = jnp.zeros_like(dph)
     dvv[...] = jnp.zeros_like(dvv)
+    gr_u.relay(0)
     for slot in range(3):
         got(dat.at[plane_block[slot]], i_da[1] + slot)
 
@@ -1238,7 +1322,7 @@
     def value_back(h, carry):
         cols, mine = head_cols(h)
         keep = jnp.where(mine, 1.0, 0.0).astype(BF16)
-        dvv[:, cols] += dot(pp[h], dn[:, cols] * keep, TN)
+        dvv[:, cols] += dot(ppt[h], dn[:, cols] * keep)
         return carry
 
     lax.fori_loop(0, 4, value_back, 0)
@@ -1266,13 +1350,13 @@
         dph[1, :, cols] += dot(ds_[...], phi[0, :, cols] * keep, TN)
         return carry
 
+    lax.fori_loop(0, 4, head_back, 0)
+    gr_u.relay(1)
     g_dz.pass_on(0)
-    lax.fori_loop(0, 4, head_back, 0)
     g_dz.pass_on(1)
+    gr_v.run(make_v)
     g_dz.pass_on(2)
-    gr_v.run(make_v)
     g_dz.pass_on(3)
-    gr_u.relay()
 
     def feature_back_body(t, carry):
         dlog = (dph[t] * ex[t]).astype(BF16)
@@ -1333,6 +1417,24 @@
         return carry
 
     lax.fori_loop(0, 4, input_part, 0)
+
+    def make_k(m):
+        for p in range(2):
+            g_k[m, :, :, :, p * 256 : (p + 1) * 256] = (
+                dot(x_rows(m), dqkv[p]).astype(BF16).reshape(2, 2, 64, 256)
+            )
+
+    gr_k.run(make_k)
+
+    def make_out(m):
+        g_o[m] = dot(d_cols(dzb, m), att[...].reshape(512, 256), TN).astype(BF16).reshape(2, 2, 64, 256)
+
+    for k in range(4):
+        g_dz.need(k)
+    gr_o.run(make_out)
+    gr_v.near()
+    gr_k.near()
+    gr_v.relay(0, 1)
     for k in range(3):
         got(sd_r.at[k], i_sd[1] + k)
     sums = sd[...] + sd_r[0] + sd_r[1] + sd_r[2]
@@ -1341,15 +1443,6 @@
     early.pair()
     gr_d.finish()
     gr_d.write_own(gd_o)
-
-    def make_k(m):
-        for p in range(2):
-            g_k[m, :, :, :, p * 256 : (p + 1) * 256] = (
-                dot(x_rows(m), dqkv[p]).astype(BF16).reshape(2, 2, 64, 256)
-            )
-
-    early.over_planes()
-    gr_k.run(make_k)
 
     def diagonal_body(h, carry):
         sums = jnp.zeros((1, 1024), F32)
@@ -1376,31 +1469,23 @@
         st_b[zz, 4:8, :] = jnp.zeros((4, 256), F32)
         st_b[zz, 15:16, :] = jnp.zeros((1, 256), F32)
     late.pair()
-
-
-    def make_out(m):
-        g_o[m] = dot(d_cols(dzb, m), att[...].reshape(512, 256), TN).astype(BF16).reshape(2, 2, 64, 256)
-
-    for k in range(4):
-        g_dz.need(k)
+    gr_k.relay(0)
+    early.over_planes()
     late.over_planes()
-    gr_o.run(make_out)
-    for gr in (gr_v, gr_k, gr_o):
-        gr.near()
+    gr_o.near()
+    gr_k.relay(1)
     outs = []
     own_mix.need(0)
     outs.append(bring(mixed_o, mixed_h))
-    gr_v.relay()
+    gr_o.relay(0, 1)
     gr_u.finish()
     gr_u.write_own(gu_o)
     sc_i.column(0)
     sc_i.column(1)
-    gr_k.relay()
     sc_i.column(2)
     sc_i.column(3)
     gr_d.write_other(gd_o)
     outs.append(bring(gd_o, gd_h))
-    gr_o.relay()
     gr_v.finish()
     gr_v.write_own(gq_o, 2)
     gr_u.write_other(gu_o)
@@ -1499,9 +1584,9 @@
     scratch += [vm((128, 1024), F32)] * 2 + [vm((128, 128), F32), vm((128, 1024), F32)]
     scratch += [vm((4, 128, 256))] * 2 + [vm((16, 128)), vm((128, 128)), vm((256, 256)), vm((24, 1024), F32)]
     scratch += [vm((512, 256))] * 2 + [vm((512, 512)), vm((4, 512, 512)), vm((2, 512, 256), F32), vm((512, 256), F32)]
-    scratch += [vm((3, 512, 256)), vm((1024, 512))]
+    scratch += [vm((3, 512, 256)), vm((1024, 512)), vm((4, 512, 512))]
     scratch += [vm((4, 2, 2, 64, n)) for n in widths]
-    scratch += [vm((4, 2, 64, n)) for n in widths] * 2 + [vm((2, 2, 64, n)) for n in widths]
+    scratch += [vm((4, 2, 64, n)) for n in widths] + [vm((2, 2, 64, n)) for n in widths] * 2
     scratch += [vm((2, 64, 1024), F32)] + [vm((64, n)) for n in widths] * 2
     scratch += [vm((8, 1024), F32), vm((3, 8, 1024), F32)] + [vm((4, 8, 256), F32), vm((4, 16, 256), F32)] * 3
     scratch += [vm((2, 16, 256), F32)]

time: 151 us -> 149 us (0.987)
  Pallas kernels: 149 us -> 147 us
    pallas_call x1, Pallas kernels: 146 us -> 144 us  [fast_local(): pl.pallas_call(layer_kernel, out_shape=shapes, in_specs=[anywhere] * 13,...]
where the time goes in v6:
time: 149 us
  Pallas kernels  147 us (99%)
    pallas_call x1, Pallas kernels, fast_local(): pl.pallas_call(layer_kernel, out_shape=shapes, in_specs=[anywhere] * 13,...  144 us
    pallas_call x1, Pallas kernels, fast_local(): pl.pallas_call(copy_kernel, out_shape=shapes, in_specs=[anywhere] * len(s...  3.09 us

profile of v6, /device:TPU:0, one launch (start us, length us, event | category | flops | bytes accessed | tf_op | source)
XLA Modules:
  0.0 148.6 jit_solution(8310113500737835470)
XLA Ops:
  1.3 144.0 %layer.1 = (bf16[256,1024]{1,0:T(8,128)(2,1)}, f32[256,1024]{1,0:T(8,128)}, f32[3,64,512]{2,1,0:T(8,128)}, f32[3,4,8]{2,1,0:T(4,128)}, f32[64,512]{1,0:T(8,128)}...) custom-call(bf16[256,1024]{1,0:T(8,128)(2,1)} %tok.1, ...), custom_call_target="tpu_custom_call" | custom-call | tf_op jit(solution)/shard_map/layer/pallas_call | solution.py:1598
  145.3 3.1 %results.1 = (bf16[256,1024]{1,0:T(8,128)(2,1)}, f32[256,1024]{1,0:T(8,128)}, f32[3,64,512]{2,1,0:T(8,128)}, f32[3,4,8]{2,1,0:T(4,128)}, f32[64,512]{1,0:T(8,128...) custom-call(bf16[256,1024]{1,0:T(8,128)(2,1)} %get-tuple-element.33., ...), custom_call_target="tpu_custom_call" | custom-call | tf_op jit(solution)/shard_map/results/pallas_call | solution.py:1612

commit v7 on v6

--- a/solution.py
+++ b/solution.py
@@ -403,7 +403,7 @@
 
 MESH = pl.DeviceIdType.MESH
 PLANES = 4
-SENDS, RECEIVES = 86, 215
+SENDS, RECEIVES = 86, 202
 F32 = jnp.float32
 BF16 = jnp.bfloat16
 SCALE = HEAD ** (-0.25)
@@ -440,11 +440,11 @@
     tok, wq_h, qb_h, wo_h, gain_h, bias_h, wu_h, ub_h, wd_h, rpe_h, om_h, bk_h, cot,
     mixed_h, gtok_h, gq_h, gqb_h, go_h, ggain_h, gbias_h, gu_h, gub_h, gd_h, grpe_h,
     qb_v, gain_v, bias_v, ub_v, rpe_v, om_v, bk_v, small_s, om_s,
-    mixed_o, gtok_o, gq_o, gqb_o, go_o, ggain_o, gbias_o, gu_o, gub_o, gd_o, grpe_o,
+    mixed_o, gq_o, gqb_o, go_o, ggain_o, gbias_o, gu_o, gub_o, gd_o, grpe_o,
     wq, wo, wu, wd, small, om2, xg, cotb,
     qkv, phi, ex, unit, inv, r0, pp, num, den, quo, att, attf,
     pb, rb_f, rb_d, rb_i, fb, hid, dgel, efb, dub, dzb, acc,
-    fst, n1, i1, dr, dat_s, dat, out_s, anti, ones64, rows_v,
+    fst, n1, i1, dr, summed, dat_s, dat, anti, ones64, rows_v,
     dn, dd, ds_, gg, dph, dvv, dqkv, xt, ppt,
     g_k, g_v, g_o, g_u, g_d, r_k, r_v, r_o, r_u, r_d, rz_k, rz_v, rz_o, rz_u, rz_d, cb_k, cb_v, cb_o, cb_u, cb_d,
     fs, xs_k, xs_v, xs_o, xs_u, xs_d, xr_k, xr_v, xr_o, xr_u, xr_d,
@@ -563,10 +563,10 @@
     inner, outer = (z == 1) | (z == 2), (z == 0) | (z == 3)
 
     class Item:
-        def __init__(self, ref, kind):
-            self.ref, self.kind = ref, kind
+        def __init__(self, ref, kind, whole=True):
+            self.ref, self.kind, self.whole = ref, kind, whole
             self.z_out, self.c_out = s_sems.take(), s_sems.take()
-            self.zs, self.sb = r_sems.take(PLANES), r_sems.take(PLANES)
+            self.zs, self.sb = r_sems.take(PLANES), r_sems.take(1 if whole else PLANES)
 
         def block(self, zz, cc):
             if self.kind == "both":
@@ -589,7 +589,7 @@
             pl.when(z > 0)(lambda: self.onward(z, -1))
             pl.when(z < PLANES - 1)(lambda: self.onward(z, 1))
             mine = self.block(z, c)
-            rc(mine, mine, self.c_out, self.sb + z, sib).start()
+            rc(mine, mine, self.c_out, self.sb if self.whole else self.sb + z, sib).start()
 
         def pump_step(self, n):
             here = self.block(n, c)
@@ -599,7 +599,7 @@
                 got(here, self.zs + n)
                 pl.when(jnp.logical_and(z == 1, n > z))(lambda: self.onward(n, -1))
                 pl.when(jnp.logical_and(z == 2, n < z))(lambda: self.onward(n, 1))
-                rc(here, here, self.c_out, self.sb + n, sib).start()
+                rc(here, here, self.c_out, self.sb if self.whole else self.sb + n, sib).start()
 
         def pump_done(self):
             def sent(sem, count):
@@ -622,8 +622,7 @@
             got(self.block(n, 1 - c), self.sb + n)
 
         def need(self):
-            for zz in range(PLANES):
-                self.need_step(zz)
+            got(self.some(PLANES), self.sb)
 
     half_of = {}
 
@@ -648,7 +647,7 @@
     give(tok.at[rows_of(y, 128)], xg.at[rows_of(2 * c + y, 128)], i_tx, dev(z, 1 - x, y, x), None, 0, c)
     it_oa, it_ob = Item(wo_own, "own"), Item(wo_own, "other")
     it_qa, it_s, it_qb = Item(wq, "own"), Item(small, "both"), Item(wq, "other")
-    it_ua, it_ub, it_da, it_db = Item(wu, "own"), Item(wu, "other"), Item(wd, "own"), Item(wd, "other")
+    it_ua, it_ub, it_da, it_db = Item(wu, "own"), Item(wu, "other"), Item(wd, "own", False), Item(wd, "other", False)
     in_o()
     it_oa.start()
     in_q()
@@ -866,62 +865,52 @@
     first = normed * rows_v[0:1, :] + rows_v[3:4, :]
     fb[own_block] = first.astype(BF16)
 
-    class Scatter:
-        def __init__(self, ref):
-            self.ref, self.out, self.base = ref, s_sems.take(), r_sems.take(4)
-
-        def part(self, n, value):
-            cols = cols256(n)
+    class RelayScatter:
+        def __init__(self, ref, order, last_direct=False):
+            self.ref, self.out, self.order, self.relayed = ref, s_sems.take(), order, 3 if last_direct else 4
+            self.near, self.far, self.last = r_sems.take(4), r_sems.take(4), r_sems.take(4)
+
+        def cols(self, k):
+            return cols256(self.order[k])
+
+        def part(self, k, value):
+            cols = cols256(at_step(self.order, k))
             pb[:, :, cols] = value.astype(BF16).reshape(4, 128, 256)
-            for slot in range(3):
-                rc(
-                    pb.at[plane_block[slot], :, cols], self.ref.at[slot, :, cols], self.out, self.base + n, plane[slot]
-                ).start()
-
-        def column(self, n):
-            cols = slice(n * 256, (n + 1) * 256)
-            got(self.ref.at[:, :, cols], self.base + n)
-            value = pb[own_block, :, cols].astype(F32)
-            for slot in range(3):
-                value = value + self.ref[slot, :, cols].astype(F32)
-            return value
+
+            def out(block, slot, sem, device):
+                rc(pb.at[block, :, cols], self.ref.at[slot, :, cols], self.out, sem + k, device).start()
+
+            @pl.when(k < self.relayed)
+            def _():
+                even = k % 2 == 0
+                beside = dev(z, jnp.where(even, 1 - x, x), jnp.where(even, y, 1 - y), c)
+                out(plane_block[0], 1, self.far, beside)
+                out(jnp.where(even, plane_block[1], plane_block[2]), 0, self.near, beside)
+
+            @pl.when(k >= self.relayed)
+            def _():
+                out(plane_block[0], 1, self.far, dg)
+                out(plane_block[1], 0, self.near, xn)
+                out(plane_block[2], 2, self.last, yn)
+
+        def pass_on(self, k):
+            cols, slot = self.cols(k), 2 - k % 2
+            part = self.ref.at[1, :, cols]
+            got(part, self.far + k)
+            part[...] = (part[...].astype(F32) + pb[plane_block[slot], :, cols].astype(F32)).astype(BF16)
+            rc(part, self.ref.at[2, :, cols], self.out, self.last + k, plane[slot]).start()
 
         def total(self):
-            return jnp.concatenate([self.column(n) for n in range(4)], axis=1)
-
-        def sent(self):
-            rc(self.ref, self.ref, self.out, 0, sib).wait_send()
-
-    class RelayScatter:
-        def __init__(self, ref):
-            self.ref, self.out = ref, s_sems.take()
-            self.near, self.far, self.last = r_sems.take(4), r_sems.take(4), r_sems.take(4)
-
-        def part(self, n, value):
-            cols = cols256(n)
-            pb[:, :, cols] = value.astype(BF16).reshape(4, 128, 256)
-            even = n % 2 == 0
-            beside = dev(z, jnp.where(even, 1 - x, x), jnp.where(even, y, 1 - y), c)
-            block = jnp.where(even, plane_block[1], plane_block[2])
-            rc(pb.at[plane_block[0], :, cols], self.ref.at[1, :, cols], self.out, self.far + n, beside).start()
-            rc(pb.at[block, :, cols], self.ref.at[0, :, cols], self.out, self.near + n, beside).start()
-
-        def pass_on(self, n):
-            cols, slot = slice(n * 256, (n + 1) * 256), 2 - n % 2
-            part = self.ref.at[1, :, cols]
-            got(part, self.far + n)
-            part[...] = (part[...].astype(F32) + pb[plane_block[slot], :, cols].astype(F32)).astype(BF16)
-            rc(part, self.ref.at[2, :, cols], self.out, self.last + n, plane[slot]).start()
-
-        def total(self):
-            pieces = []
-            for n in range(4):
-                cols = slice(n * 256, (n + 1) * 256)
-                got(self.ref.at[0, :, cols], self.near + n)
-                got(self.ref.at[2, :, cols], self.last + n)
+            for k in range(4):
+                cols = self.cols(k)
+                got(self.ref.at[0, :, cols], self.near + k)
+                if k >= self.relayed:
+                    got(self.ref.at[1, :, cols], self.far + k)
+                got(self.ref.at[2, :, cols], self.last + k)
                 value = pb[own_block, :, cols].astype(F32) + self.ref[0, :, cols].astype(F32)
-                pieces.append(value + self.ref[2, :, cols].astype(F32))
-            return jnp.concatenate(pieces, axis=1)
+                value = value + self.ref[2, :, cols].astype(F32)
+                summed[:, cols] = value + self.ref[1, :, cols].astype(F32) if k >= self.relayed else value
+            return summed[...]
 
         def sent(self):
             rc(self.ref, self.ref, self.out, 0, sib).wait_send()
@@ -1017,18 +1006,20 @@
         return carry
 
     lax.fori_loop(0, 4, hidden_body, 0)
-    sc_f = Scatter(rb_f)
+    sc_f = RelayScatter(rb_f, arrive, True)
 
     def down_part(k, carry):
         n = at_step(arrive, k)
         pl.when(outer)(lambda: it_db.pump_step(n))
         it_da.need_step(n)
         it_db.need_step(n)
-        sc_f.part(n, dot(hid[...], wd[pl.ds(2 * n, 2)].reshape(256, 1024), NT))
+        sc_f.part(k, dot(hid[...], wd[pl.ds(2 * n, 2)].reshape(256, 1024), NT))
         return carry
 
     lax.fori_loop(0, 4, down_part, 0)
     it_db.pump_done()
+    for k in range(3):
+        sc_f.pass_on(k)
     pl.when(away)(lambda: got(cotb, i_cot[1]))
     in_cot()
     upstream = cotb[...].astype(F32)
@@ -1175,16 +1166,16 @@
         def columns(self, out, half, value, at=0):
             if len(out.shape) == 3:
                 for p in range(self.width // 256):
-                    out[at + p, :, half_cols(half, 256)] = value[:, p * 256 : (p + 1) * 256]
+                    out[at + p, :, half_cols(half, 256)] = value[:, p * 256 : (p + 1) * 256].astype(BF16)
             else:
-                out[:, half_cols(half, self.width)] = value
+                out[:, half_cols(half, self.width)] = value.astype(BF16)
 
         def write_own(self, out, at=0):
             self.columns(out, x, fs[x, :, 0 : self.width], at)
 
         def write_other(self, out, at=0):
             got(self.xr, self.x[1])
-            self.columns(out, 1 - x, self.xr[...].astype(F32), at)
+            self.columns(out, 1 - x, self.xr[...], at)
 
     gr_d = Grad(g_d, r_d, rz_d, cb_d, xs_d, xr_d, True)
     gr_u = Grad(g_u, r_u, rz_u, cb_u, xs_u, xr_u, True)
@@ -1228,7 +1219,7 @@
         return carry
 
     lax.fori_loop(0, 4, du_body, 0)
-    sc_d = RelayScatter(rb_d)
+    sc_d = RelayScatter(rb_d, [jnp.int32(k) for k in range(4)])
 
     def back_part(n, carry):
         sc_d.part(n, dot(dub[...], wu[pl.ds(2 * n, 2)].reshape(256, 1024), NT))
@@ -1399,13 +1390,11 @@
             mine = gt_r.at[rows_of(y, 128), cols]
             mine[...] = value.astype(BF16)
             give(mine, mine, self.last, yn, None, n, n)
-            gtok_o[rows_of(y, 128), cols] = value
 
         def need(self, n):
             cols = slice(n * 256, (n + 1) * 256)
             rows = rows_of(1 - y, 128)
             got(gt_r.at[rows, cols], self.last[1] + n)
-            gtok_o[rows, cols] = gt_r[rows, cols].astype(F32)
 
     sc_i = Return(rb_i)
 
@@ -1509,7 +1498,7 @@
     gr_o.write_own(go_o)
     for n in range(4):
         sc_i.need(n)
-    outs.append(bring(gtok_o, gtok_h))
+    outs.append(bring(gt_r, gtok_h))
     got(swap.at[1], i_swap[1])
     tile = pl.ds(pl.multiple_of((1 - x) * 128, 128), 128)
     ours, theirs = swap[0, 0:4, tile], swap[1, 0:4, tile]
@@ -1546,15 +1535,21 @@
 
 
 def copy_kernel(*refs):
-    count = len(refs) // 3
+    count = (len(refs) - 1) // 4
     sem = refs[-1]
-    ins = [pltpu.make_async_copy(refs[i], refs[2 * count + i], sem.at[0, i]) for i in range(count)]
-    outs = [pltpu.make_async_copy(refs[2 * count + i], refs[count + i], sem.at[1, i]) for i in range(count)]
+    given, held, wide, kept = (refs[k * count : (k + 1) * count] for k in (0, 2, 3, 1))
+    ins = [pltpu.make_async_copy(given[i], held[i], sem.at[0, i]) for i in range(count)]
     for copy in ins:
         copy.start()
-    for one, two in zip(ins, outs):
-        one.wait()
-        two.start()
+    outs = []
+    for i in range(count):
+        ins[i].wait()
+        if held[i].dtype == kept[i].dtype:
+            outs.append(pltpu.make_async_copy(held[i], kept[i], sem.at[1, i]))
+        else:
+            wide[i][...] = held[i][...].astype(kept[i].dtype)
+            outs.append(pltpu.make_async_copy(wide[i], kept[i], sem.at[1, i]))
+        outs[-1].start()
     for copy in outs:
         copy.wait()
 
@@ -1573,7 +1568,9 @@
         ((256, 1024), BF16), ((256, 1024), F32), ((3, 64, 512), F32), ((3, 4, 8), F32), ((64, 512), F32), ((2, 64), F32),
         ((4, 64), F32), ((64, 2048), F32), ((4, 32), F32), ((64, 2048), F32), ((8, 64), F32),
     )
-    scratch += [vm(*result) for result in results]
+    large = ((256, 1024), (3, 64, 512), (64, 512), (64, 2048))
+    sent = tuple((shape, BF16 if shape in large else dtype) for shape, dtype in results)
+    scratch += [vm(*result) for i, result in enumerate(sent) if i != 1]
     scratch += [vm((3, 8, 2, 64, 256)), vm((4, 8, 2, 64, 256)), vm((8, 2, 64, 1024)), vm((8, 2, 64, 1024))]
     scratch += [vm((8, 2, 32, 128)), vm((256, 256)), vm((512, 1024)), vm((128, 1024))]
     scratch += [vm((3, 512, 256)), vm((2, 512, 256))] + [vm((2, 512, 256), F32)] * 3
@@ -1581,8 +1578,8 @@
     scratch += [vm((4, 128, 1024))] + [vm((3, 128, 1024))] * 2 + [vm((4, 128, 1024))]
     scratch += [vm((4, 128, 1024)), vm((512, 1024)), vm((512, 1024), F32)]
     scratch += [vm((4, 128, 1024)), vm((512, 1024)), vm((4, 128, 1024)), vm((512, 1024), F32)]
-    scratch += [vm((128, 1024), F32)] * 2 + [vm((128, 128), F32), vm((128, 1024), F32)]
-    scratch += [vm((4, 128, 256))] * 2 + [vm((16, 128)), vm((128, 128)), vm((256, 256)), vm((24, 1024), F32)]
+    scratch += [vm((128, 1024), F32)] * 2 + [vm((128, 128), F32)] + [vm((128, 1024), F32)] * 2
+    scratch += [vm((4, 128, 256))] * 2 + [vm((128, 128)), vm((256, 256)), vm((24, 1024), F32)]
     scratch += [vm((512, 256))] * 2 + [vm((512, 512)), vm((4, 512, 512)), vm((2, 512, 256), F32), vm((512, 256), F32)]
     scratch += [vm((3, 512, 256)), vm((1024, 512)), vm((4, 512, 512))]
     scratch += [vm((4, 2, 2, 64, n)) for n in widths]
@@ -1594,10 +1591,11 @@
     scratch += [pltpu.SemaphoreType.DMA((SENDS,)), pltpu.SemaphoreType.DMA((RECEIVES,)), pltpu.SemaphoreType.DMA((24,))]
 
     shapes = tuple(jax.ShapeDtypeStruct(*result) for result in results)
+    narrow = tuple(jax.ShapeDtypeStruct(*result) for result in sent)
     anywhere = pl.BlockSpec(memory_space=pl.ANY)
     made = pl.pallas_call(
         layer_kernel,
-        out_shape=shapes,
+        out_shape=narrow,
         in_specs=[anywhere] * 13,
         out_specs=(anywhere,) * len(shapes),
         scratch_shapes=scratch,
@@ -1614,7 +1612,7 @@
         out_shape=shapes,
         in_specs=[anywhere] * len(shapes),
         out_specs=(anywhere,) * len(shapes),
-        scratch_shapes=[vm(*result) for result in results] + [pltpu.SemaphoreType.DMA((2, len(shapes)))],
+        scratch_shapes=[vm(*result) for result in sent + results] + [pltpu.SemaphoreType.DMA((2, len(shapes)))],
         compiler_params=pltpu.CompilerParams(vmem_limit_bytes=63 * 2**20),
         name="results",
     )(*made)

time: 149 us -> 148 us (level)
  no operation moved by 1% of the time
where the time goes in v7:
time: 148 us
  Pallas kernels  146 us (99%)
    pallas_call x1, Pallas kernels, fast_local(): pl.pallas_call(layer_kernel, out_shape=narrow, in_specs=[anywhere] * 13,...  143 us
    pallas_call x1, Pallas kernels, fast_local(): pl.pallas_call(copy_kernel, out_shape=shapes, in_specs=[anywhere] * len(s...  2.97 us

profile of v7, /device:TPU:0, one launch (start us, length us, event | category | flops | bytes accessed | tf_op | source)
XLA Modules:
  0.0 147.9 jit_solution(11402816684215652498)
XLA Ops:
  1.3 143.5 %layer.1 = (bf16[256,1024]{1,0:T(8,128)(2,1)}, bf16[256,1024]{1,0:T(8,128)(2,1)}, bf16[3,64,512]{2,1,0:T(8,128)(2,1)}, f32[3,4,8]{2,1,0:T(4,128)}, bf16[64,512]{...) custom-call(bf16[256,1024]{1,0:T(8,128)(2,1)} %tok.1, ...), custom_call_target="tpu_custom_call" | custom-call | tf_op jit(solution)/shard_map/layer/pallas_call | solution.py:1596
  144.8 3.0 %results.1 = (bf16[256,1024]{1,0:T(8,128)(2,1)}, f32[256,1024]{1,0:T(8,128)}, f32[3,64,512]{2,1,0:T(8,128)}, f32[3,4,8]{2,1,0:T(4,128)}, f32[64,512]{1,0:T(8,128...) custom-call(bf16[256,1024]{1,0:T(8,128)(2,1)} %get-tuple-element.33., ...), custom_call_target="tpu_custom_call" | custom-call | tf_op jit(solution)/shard_map/results/pallas_call | solution.py:1610

commit v8 on v7

--- a/solution.py
+++ b/solution.py
@@ -788,7 +788,7 @@
         qkv[p] = (dot(xg[...], wq[p].reshape(1024, 256)) + rows_v[16:17, cols256(p)]).astype(BF16)
         return carry
 
-    lax.fori_loop(0, 3, qkv_body, 0)
+    lax.fori_loop(0, 3, qkv_body, 0, unroll=True)
     got(om2, i_om[1])
     om2[...] = om2[...] + om_s[...]
 
@@ -805,7 +805,7 @@
         phi[t] = value.astype(BF16)
         return carry
 
-    lax.fori_loop(0, 2, feature_body, 0)
+    lax.fori_loop(0, 2, feature_body, 0, unroll=True)
     lane_head = iota((1, 128), 1) // HEAD
 
     def head_cols(h):
@@ -830,7 +830,7 @@
         return ref.at[block, :, t * 128 : (t + 1) * 128]
 
     for t in range(2):
-        lax.fori_loop(2 * t, 2 * t + 2, head_body, 0)
+        lax.fori_loop(2 * t, 2 * t + 2, head_body, 0, unroll=True)
         cols = slice(t * 128, (t + 1) * 128)
         quo[:, cols] = num[:, cols] / den[:, cols]
         att[:, :, cols] = quo[:, cols].astype(BF16).reshape(4, 128, 128)
@@ -1005,7 +1005,7 @@
         dgel[:, cols] = cdf + pre * (0.3989422804014327 * jnp.exp(-0.5 * pre * pre))
         return carry
 
-    lax.fori_loop(0, 4, hidden_body, 0)
+    lax.fori_loop(0, 4, hidden_body, 0, unroll=2)
     sc_f = RelayScatter(rb_f, arrive, True)
 
     def down_part(k, carry):
@@ -1218,7 +1218,7 @@
             st_b[zz, pl.ds(8 + n, 1), :] = down(du.astype(F32))
         return carry
 
-    lax.fori_loop(0, 4, du_body, 0)
+    lax.fori_loop(0, 4, du_body, 0, unroll=2)
     sc_d = RelayScatter(rb_d, [jnp.int32(k) for k in range(4)])
 
     def back_part(n, carry):
@@ -1316,7 +1316,7 @@
         dvv[:, cols] += dot(ppt[h], dn[:, cols] * keep)
         return carry
 
-    lax.fori_loop(0, 4, value_back, 0)
+    lax.fori_loop(0, 4, value_back, 0, unroll=True)
     dqkv[2] = dvv[...].astype(BF16)
 
     def x_rows(m):
@@ -1341,7 +1341,7 @@
         dph[1, :, cols] += dot(ds_[...], phi[0, :, cols] * keep, TN)
         return carry
 
-    lax.fori_loop(0, 4, head_back, 0)
+    lax.fori_loop(0, 4, head_back, 0, unroll=True)
     gr_u.relay(1)
     g_dz.pass_on(0)
     g_dz.pass_on(1)
@@ -1357,7 +1357,7 @@
         dqkv[t] = (inv[t] * (dunit - units * mean)).astype(BF16)
         return carry
 
-    lax.fori_loop(0, 2, feature_back_body, 0)
+    lax.fori_loop(0, 2, feature_back_body, 0, unroll=True)
     class Return:
         def __init__(self, ref):
             self.ref, self.out, self.base, self.last = ref, s_sems.take(), r_sems.take(4), take(4)
@@ -1405,7 +1405,7 @@
         sc_i.part(n, value)
         return carry
 
-    lax.fori_loop(0, 4, input_part, 0)
+    lax.fori_loop(0, 4, input_part, 0, unroll=2)
 
     def make_k(m):
         for p in range(2):

time: 148 us -> 147 us (level)
  no operation moved by 1% of the time
where the time goes in v8:
time: 147 us
  Pallas kernels  145 us (99%)
    pallas_call x1, Pallas kernels, fast_local(): pl.pallas_call(layer_kernel, out_shape=narrow, in_specs=[anywhere] * 13,...  142 us
    pallas_call x1, Pallas kernels, fast_local(): pl.pallas_call(copy_kernel, out_shape=shapes, in_specs=[anywhere] * len(s...  2.97 us

profile of v8, /device:TPU:0, one launch (start us, length us, event | category | flops | bytes accessed | tf_op | source)
XLA Modules:
  0.0 146.7 jit_solution(10740059577638376155)
XLA Ops:
  1.3 142.3 %layer.1 = (bf16[256,1024]{1,0:T(8,128)(2,1)}, bf16[256,1024]{1,0:T(8,128)(2,1)}, bf16[3,64,512]{2,1,0:T(8,128)(2,1)}, f32[3,4,8]{2,1,0:T(4,128)}, bf16[64,512]{...) custom-call(bf16[256,1024]{1,0:T(8,128)(2,1)} %tok.1, ...), custom_call_target="tpu_custom_call" | custom-call | tf_op jit(solution)/shard_map/layer/pallas_call | solution.py:1596
  143.6 3.0 %results.1 = (bf16[256,1024]{1,0:T(8,128)(2,1)}, f32[256,1024]{1,0:T(8,128)}, f32[3,64,512]{2,1,0:T(8,128)}, f32[3,4,8]{2,1,0:T(4,128)}, f32[64,512]{1,0:T(8,128...) custom-call(bf16[256,1024]{1,0:T(8,128)(2,1)} %get-tuple-element.33., ...), custom_call_target="tpu_custom_call" | custom-call | tf_op jit(solution)/shard_map/results/pallas_call | solution.py:1610
